TPU v7x, 128 devices: a whole 4x4x4 slice. The times are simulated.
128 devices in a mesh: dp: 32 (over y, x, z_hi), mp: 4 (over z_lo, core).
Axes of the slice: x: 4, y: 4, z: 4 (z_hi: 2, z_lo: 2; z = z_hi * 2 + z_lo), core: 2. Of those that a mesh axis runs over, the one named last changes fastest.
Arguments:
- layer_in: bfloat16 [32, 512, 1024], P('dp', 'mp'), may hold values from -6 to 6
- memory: bfloat16 [32, 512, 1024], P('dp', 'mp'), may hold values from -6 to 6
- squeezed_mem: bfloat16 [32, 512, 1024], P('dp', 'mp'), may hold values from -6 to 6
- memory_fill: int32 [32], P('dp'), may hold values from 16 to 512, as said below
- squeezed_fill: int32 [32], P('dp'), may hold values from 0 to 512, as said below
- grad_out: bfloat16 [32, 512, 1024], P('dp', 'mp'), may hold values from -6 to 6
- attn_gain: float32 [1024], replicated, may hold values from 0.5 to 1.5
- w_query: bfloat16 [1024, 1024], replicated, may hold values from -0.1875 to 0.1875
- w_keyval: bfloat16 [1024, 2048], replicated, may hold values from -0.1875 to 0.1875
- w_output: bfloat16 [1024, 1024], replicated, may hold values from -0.75 to 0.75
- slopes: float32 [8], replicated, may hold values from 0.0005 to 0.05
- ffn_gain: float32 [1024], replicated, may hold values from 0.5 to 1.5
- w_up: bfloat16 [1024, 4096], P(None, 'mp'), may hold values from -0.1875 to 0.1875
- up_bias: float32 [4096], P('mp'), may hold values from -3 to 3
- w_down: bfloat16 [4096, 1024], P('mp'), may hold values from -0.09375 to 0.09375
- w_squeeze: bfloat16 [3072, 1024], replicated, may hold values from -0.109375 to 0.109375
Outputs:
- layer_out: bfloat16 [32, 512, 1024], P('dp', 'mp')
- new_squeezed: bfloat16 [32, 172, 1024], P('dp', 'mp')
- grad_in: float32 [32, 512, 1024], P('dp', 'mp')
- grad_attn_gain: float32 [1024], replicated
- grad_query: float32 [1024, 1024], P('mp')
- grad_keyval: float32 [1024, 2048], P('mp')
- grad_output: float32 [1024, 1024], P('mp')
- grad_slopes: float32 [8], replicated
- grad_ffn_gain: float32 [1024], replicated
- grad_up: float32 [1024, 4096], P(None, 'mp')
- grad_up_bias: float32 [4096], P('mp')
- grad_down: float32 [4096, 1024], P('mp')
- grad_squeeze: float32 [3072, 1024], P('mp')
Inputs may be any that keep to these rules, and one draw needn't show every extreme that they name: A stream's valid memory slots are its last memory_fill ones. In every draw some stream has all 512 valid. A stream's valid compressed slots are its last squeezed_fill ones; it has any only where its memory_fill is 512. In every draw some stream has all 512 valid.
All inputs are finite; a program needn't handle non-finite values.
Results may differ from a plain program's by a relative error of at most 0.028.
Values may be sent and summed in bfloat16 or wider, within the bound.
A program may use at most 192 MiB of HBM per device.

v0:
```python
import jax
import jax.numpy as jnp
from jax import lax
from jax.sharding import PartitionSpec as P

D = 1024
H = 8
DH = 128
S = 512
M = 512
C = 512


EPS = 1e-05
NEG = -1e30


def shifted(value, axis, steps):
    count = lax.axis_size(axis)
    leading, last = (max(0, -steps), min(count, count - steps))
    return lax.ppermute(value, axis, [(source, source + steps) for source in range(leading, last)])


def layer_norm(rows, gain):
    centre = rows - jnp.mean(rows, axis=-1, keepdims=True)
    spread = jnp.mean(centre * centre, axis=-1, keepdims=True)
    return centre * lax.rsqrt(spread + EPS) * gain


def split_heads(block):
    return block.reshape(block.shape[0], block.shape[1], H, DH)


def scores_of(query, keyval, bias, valid):
    width = query.shape[2]
    keys = split_heads(keyval[:, :, :width])
    raw = (
        jnp.einsum("bihd,bjhd->bhij", split_heads(query), keys, preferred_element_type=jnp.float32)
        * DH ** (-0.5)
        + bias
    )
    return jnp.where(valid[:, None], raw, NEG)


def soft_forward(scores, keyval):
    width = keyval.shape[2] // 2
    top = jnp.max(scores, axis=-1, keepdims=True)
    weights = jnp.exp(scores - top)
    total = jnp.sum(weights, axis=-1, keepdims=True)
    probs = (weights / total).astype(jnp.bfloat16)
    mixed = jnp.einsum(
        "bhij,bjhd->bihd",
        probs,
        split_heads(keyval[:, :, width:]),
        preferred_element_type=jnp.float32,
    )
    return (mixed.reshape(mixed.shape[0], mixed.shape[1], width), top + jnp.log(total))


def soft_backward(scores, log_total, query, keyval, grad_mixed):
    width = query.shape[2]
    count = keyval.shape[1]
    probs = jnp.exp(scores - log_total)
    grad_heads = split_heads(grad_mixed)
    grad_probs = jnp.einsum(
        "bihd,bjhd->bhij",
        grad_heads,
        split_heads(keyval[:, :, width:]),
        preferred_element_type=jnp.float32,
    )
    grad_values = jnp.einsum(
        "bhij,bihd->bjhd",
        probs.astype(jnp.bfloat16),
        grad_heads,
        preferred_element_type=jnp.float32,
    )
    grad_scores = (
        probs * (grad_probs - jnp.sum(probs * grad_probs, axis=-1, keepdims=True))
    ).astype(jnp.bfloat16)
    grad_keys = jnp.einsum(
        "bhij,bihd->bjhd", grad_scores, split_heads(query), preferred_element_type=jnp.float32
    ) * DH ** (-0.5)
    grad_keyval = jnp.concatenate(
        [grad_keys.reshape(-1, count, width), grad_values.reshape(-1, count, width)], axis=2
    )
    return (grad_scores, grad_keyval)


def per_device(
    layer_in,
    memory,
    squeezed_mem,
    memory_fill,
    squeezed_fill,
    grad_out,
    attn_gain,
    w_query,
    w_keyval,
    w_output,
    slopes,
    ffn_gain,
    w_up,
    up_bias,
    w_down,
    w_squeeze,
):
    parts = lax.axis_size("mp")
    rank = lax.axis_index("mp")
    batch, own_rows, width = layer_in.shape
    old_rows = squeezed_mem.shape[1]
    mem_rows = memory.shape[1]
    seg_start = old_rows + mem_rows
    sq_rows = (M + 3 * parts - 1) // (3 * parts)
    extra = 3 * sq_rows - mem_rows
    span = C + M + S
    own_ctx = jnp.concatenate([squeezed_mem, memory, layer_in], axis=1).astype(jnp.float32)
    normed_full, ctx_back = jax.vjp(layer_norm, own_ctx, attn_gain)
    normed = normed_full.astype(jnp.bfloat16)
    seg_normed = normed[:, seg_start:]
    query = jnp.einsum(
        "brd,de->bre", seg_normed, w_query, preferred_element_type=jnp.float32
    ).astype(jnp.bfloat16)
    own_kv = jnp.einsum("brd,de->bre", normed, w_keyval, preferred_element_type=jnp.float32).astype(
        jnp.bfloat16
    )
    rim_rows = shifted(memory[:, : parts * extra], "mp", -1)
    longer = jnp.concatenate([memory, rim_rows], axis=1)
    windows = lax.dynamic_slice_in_dim(longer, rank * extra, 3 * sq_rows, 1).reshape(
        batch, sq_rows, 3 * width
    )
    squeezed = jnp.einsum("brk,kd->brd", windows, w_squeeze, preferred_element_type=jnp.float32)
    sq_norm, sq_norm_back = jax.vjp(lambda rows: layer_norm(rows, attn_gain), squeezed)
    sq_own = jnp.einsum(
        "brd,de->bre", sq_norm.astype(jnp.bfloat16), w_keyval, preferred_element_type=jnp.float32
    ).astype(jnp.bfloat16)
    old_kv, mem_kv, new_kv, sq_kv = (
        lax.all_gather(own_kv[:, :old_rows], "mp", axis=1, tiled=True),
        lax.all_gather(own_kv[:, old_rows:seg_start], "mp", axis=1, tiled=True),
        lax.all_gather(own_kv[:, seg_start:], "mp", axis=1, tiled=True),
        lax.all_gather(sq_own, "mp", axis=1, tiled=True),
    )
    keyval = jnp.concatenate([old_kv, mem_kv, new_kv], axis=1)
    row_ids = rank * own_rows + jnp.arange(own_rows)
    cols = jnp.arange(span)
    distance = (C + M + row_ids[:, None] - cols[None, :]).astype(jnp.float32)
    mem_limit = (M - memory_fill)[:, None, None]
    old_limit = (C - squeezed_fill)[:, None, None]
    valid = (
        (cols < C) & (cols >= old_limit)
        | (cols >= C) & (cols < C + M) & (cols >= C + mem_limit)
        | (cols >= C + M) & (cols <= C + M + row_ids[:, None])
    )
    bias = -slopes[:, None, None] * distance[None]
    mixed, log_total = soft_forward(scores_of(query, keyval, bias, valid), keyval)
    mixed = mixed.astype(jnp.bfloat16)
    branch = jnp.einsum("brd,de->bre", mixed, w_output, preferred_element_type=jnp.float32)
    mid = layer_in.astype(jnp.float32) + branch
    normed_mid, mid_back = jax.vjp(layer_norm, mid, ffn_gain)
    all_normed = lax.all_gather(normed_mid.astype(jnp.bfloat16), "mp", axis=1, tiled=True)
    pre = jnp.einsum("bsd,df->bsf", all_normed, w_up, preferred_element_type=jnp.float32) + up_bias
    activated, gelu_back = jax.vjp(jax.nn.gelu, pre)
    hidden = activated.astype(jnp.bfloat16)
    down_terms = jnp.einsum("bsf,fd->bsd", hidden, w_down, preferred_element_type=jnp.float32)
    layer_out = (
        mid
        + lax.psum_scatter(
            down_terms.astype(jnp.bfloat16), "mp", scatter_dimension=1, tiled=True
        ).astype(jnp.float32)
    ).astype(jnp.bfloat16)
    mem_valid = jnp.arange(M) >= mem_limit
    slots = jnp.arange(sq_rows * parts)
    sq_valid = (3 * slots < M) & (3 * slots + 2 >= mem_limit)
    first, unused = soft_forward(scores_of(query, mem_kv, 0.0, mem_valid), mem_kv)
    second, sq_total = soft_forward(scores_of(query, sq_kv, 0.0, sq_valid), sq_kv)
    diff = first - second
    all_grad = lax.all_gather(grad_out, "mp", axis=1, tiled=True)
    grad_down = jnp.einsum("bsf,bsd->fd", hidden, all_grad, preferred_element_type=jnp.float32)
    grad_hidden = jnp.einsum("bsd,fd->bsf", all_grad, w_down, preferred_element_type=jnp.float32)
    grad_pre = gelu_back(grad_hidden)[0].astype(jnp.bfloat16)
    grad_up_bias = jnp.sum(grad_pre.astype(jnp.float32), axis=(0, 1))
    grad_up = jnp.einsum("bsd,bsf->df", all_normed, grad_pre, preferred_element_type=jnp.float32)
    norm_terms = jnp.einsum("bsf,df->bsd", grad_pre, w_up, preferred_element_type=jnp.float32)
    grad_norm_mid = lax.psum_scatter(norm_terms, "mp", scatter_dimension=1, tiled=True)
    grad_mid_norm, grad_ffn_gain = mid_back(grad_norm_mid)
    grad_mid = grad_out.astype(jnp.float32) + grad_mid_norm
    grad_branch = grad_mid.astype(jnp.bfloat16)
    grad_output = jnp.einsum("brd,bre->de", mixed, grad_branch, preferred_element_type=jnp.float32)
    grad_mixed = jnp.einsum(
        "bre,de->brd", grad_branch, w_output, preferred_element_type=jnp.float32
    ).astype(jnp.bfloat16)
    grad_scores, grad_kv_all = soft_backward(
        scores_of(query, keyval, bias, valid), log_total, query, keyval, grad_mixed
    )
    grad_slopes = -jnp.sum(grad_scores.astype(jnp.float32) * distance, axis=(0, 2, 3))
    grad_q = jnp.einsum(
        "bhij,bjhd->bihd",
        grad_scores,
        split_heads(keyval[:, :, :width]),
        preferred_element_type=jnp.float32,
    ) * DH ** (-0.5)
    grad_q = grad_q.reshape(batch, own_rows, width).astype(jnp.bfloat16)
    grad_second = (diff * (-2.0 / (S * D))).astype(jnp.bfloat16)
    unused_scores, grad_sq_all = soft_backward(
        scores_of(query, sq_kv, 0.0, sq_valid), sq_total, query, sq_kv, grad_second
    )
    grad_old, grad_mem, grad_new, grad_sq = (
        lax.psum_scatter(
            grad_kv_all[:, :C].astype(jnp.bfloat16), "mp", scatter_dimension=1, tiled=True
        ).astype(jnp.float32),
        lax.psum_scatter(
            grad_kv_all[:, C : C + M].astype(jnp.bfloat16), "mp", scatter_dimension=1, tiled=True
        ).astype(jnp.float32),
        lax.psum_scatter(
            grad_kv_all[:, C + M :].astype(jnp.bfloat16), "mp", scatter_dimension=1, tiled=True
        ).astype(jnp.float32),
        lax.psum_scatter(
            grad_sq_all.astype(jnp.bfloat16), "mp", scatter_dimension=1, tiled=True
        ).astype(jnp.float32),
    )
    grad_own_kv = jnp.concatenate([grad_old, grad_mem, grad_new], axis=1).astype(jnp.bfloat16)
    grad_keyval = jnp.einsum("brd,bre->de", normed, grad_own_kv, preferred_element_type=jnp.float32)
    grad_query = jnp.einsum("brd,bre->de", seg_normed, grad_q, preferred_element_type=jnp.float32)
    grad_normed = jnp.einsum(
        "bre,de->brd", grad_own_kv, w_keyval, preferred_element_type=jnp.float32
    )
    seg_grad = grad_normed[:, seg_start:] + jnp.einsum(
        "bre,de->brd", grad_q, w_query, preferred_element_type=jnp.float32
    )
    grad_normed = jnp.concatenate([grad_normed[:, :seg_start], seg_grad], axis=1)
    grad_ctx, grad_attn_gain = ctx_back(grad_normed)
    grad_in = grad_mid + grad_ctx[:, seg_start:]
    grad_sq_normed = jnp.einsum(
        "bre,de->brd", grad_sq.astype(jnp.bfloat16), w_keyval, preferred_element_type=jnp.float32
    )
    grad_squeezed = sq_norm_back(grad_sq_normed)[0].astype(jnp.bfloat16)
    grad_squeeze = jnp.einsum(
        "brk,brd->kd", windows, grad_squeezed, preferred_element_type=jnp.float32
    )
    summed = (
        lax.psum(grad_query.astype(jnp.bfloat16), "dp").astype(jnp.float32),
        lax.psum(grad_keyval.astype(jnp.bfloat16), "dp").astype(jnp.float32),
        lax.psum(grad_output.astype(jnp.bfloat16), "dp").astype(jnp.float32),
        lax.psum(grad_squeeze.astype(jnp.bfloat16), "dp").astype(jnp.float32),
        lax.psum(grad_attn_gain.astype(jnp.bfloat16), "dp").astype(jnp.float32),
        lax.psum(grad_slopes.astype(jnp.bfloat16), "dp").astype(jnp.float32),
        lax.psum(grad_ffn_gain.astype(jnp.bfloat16), "dp").astype(jnp.float32),
        lax.psum(grad_up.astype(jnp.bfloat16), "dp").astype(jnp.float32),
        lax.psum(grad_up_bias.astype(jnp.bfloat16), "dp").astype(jnp.float32),
        lax.psum(grad_down.astype(jnp.bfloat16), "dp").astype(jnp.float32),
    )
    shares = (
        lax.psum_scatter(
            summed[0].astype(jnp.bfloat16), "mp", scatter_dimension=0, tiled=True
        ).astype(jnp.float32),
        lax.psum_scatter(
            summed[1].astype(jnp.bfloat16), "mp", scatter_dimension=0, tiled=True
        ).astype(jnp.float32),
        lax.psum_scatter(
            summed[2].astype(jnp.bfloat16), "mp", scatter_dimension=0, tiled=True
        ).astype(jnp.float32),
        lax.psum_scatter(
            summed[3].astype(jnp.bfloat16), "mp", scatter_dimension=0, tiled=True
        ).astype(jnp.float32),
    )
    smalls = lax.psum((summed[4], summed[5], summed[6]), "mp")
    split_part = (summed[7], summed[8], summed[9])
    return (
        layer_out,
        squeezed.astype(jnp.bfloat16),
        grad_in,
        smalls[0],
        shares[0],
        shares[1],
        shares[2],
        smalls[1],
        smalls[2],
        split_part[0],
        split_part[1],
        split_part[2],
        shares[3],
    )


def solution(mesh):
    in_specs = (
        P("dp", "mp", None),
        P("dp", "mp", None),
        P("dp", "mp", None),
        P("dp"),
        P("dp"),
        P("dp", "mp", None),
        P(),
        P(),
        P(),
        P(),
        P(),
        P(),
        P(None, "mp"),
        P("mp"),
        P("mp", None),
        P(),
    )
    out_specs = (
        P("dp", "mp", None),
        P("dp", "mp", None),
        P("dp", "mp", None),
        P(),
        P("mp", None),
        P("mp", None),
        P("mp", None),
        P(),
        P(),
        P(None, "mp"),
        P("mp"),
        P("mp", None),
        P("mp", None),
    )
    return jax.shard_map(
        per_device, mesh=mesh, in_specs=in_specs, out_specs=out_specs, check_vma=False
    )
```

profile of v0, /device:TPU:0, one launch (start us, length us, event | category | flops | bytes accessed | tf_op | source)
XLA Modules:
  0.0 997.2 jit_solution(2572844918554861047)
XLA Ops:
  10.1 4.4 fusion.11
  22.6 24.8 %all-gather.8.cloned.1.call-done = bf16[1,512,2048]{2,1,0:T(8,128)(2,1)} async-done(((bf16[1,128,2048]{2,1,0:T(8,128)(2,1)}), bf16[1,512,2048]{2,1,0:T(8,128)(2,1)}) %all-gather.8.cloned.1.call-update) | async-done | bytes 2097168 | tf_op jit(solution)/shard_map/all_gather | solution.py:137
  47.4 3.2 constant_dynamic-update-slice_fusion.2
  50.5 29.1 %all-gather.10.cloned.1.call-done = bf16[1,512,2048]{2,1,0:T(8,128)(2,1)} async-done(((bf16[1,128,2048]{2,1,0:T(8,128)(2,1)}), bf16[1,512,2048]{2,1,0:T(8,128)(2,1)}) %all-gather.10.cloned.1.call-update) | async-done | bytes 2097168 | tf_op jit(solution)/shard_map/all_gather | solution.py:138
  79.7 3.2 constant_dynamic-update-slice_fusion.1
  82.8 29.2 %all-gather.12.cloned.1.call-done = bf16[1,512,2048]{2,1,0:T(8,128)(2,1)} async-done(((bf16[1,128,2048]{2,1,0:T(8,128)(2,1)}), bf16[1,512,2048]{2,1,0:T(8,128)(2,1)}) %all-gather.12.cloned.1.call-update) | async-done | bytes 2097168 | tf_op jit(solution)/shard_map/all_gather | solution.py:139
  112.0 3.2 constant_dynamic-update-slice_fusion
  115.2 7.0 slice_bitcast_fusion
  122.1 4.6 copy.98
  126.8 2.9 copy.101
  129.9 1.8 fusion.120
  134.4 2.2 fusion.33
  139.4 21.0 %all-gather.14.cloned.1.call-done = bf16[1,512,1024]{2,1,0:T(8,128)(2,1)} async-done(((bf16[1,128,1024]{2,1,0:T(8,128)(2,1)}), bf16[1,512,1024]{2,1,0:T(8,128)(2,1)}) %all-gather.14.cloned.1.call-update) | async-done | bytes 1048592 | tf_op jit(solution)/shard_map/all_gather | solution.py:159
  160.3 4.5 fusion.48
  164.8 18.8 %all-gather.16.cloned.1.call-done = bf16[1,512,1024]{2,1,0:T(8,128)(2,1)} async-done(((bf16[1,128,1024]{2,1,0:T(8,128)(2,1)}), bf16[1,512,1024]{2,1,0:T(8,128)(2,1)}) %all-gather.16.cloned.1.call-update) | async-done | bytes 1048592 | tf_op jit(solution)/shard_map/all_gather | solution.py:176
  183.6 4.5 fusion.129
  189.1 2.6 convolution_bitcast_fusion
  191.8 4.1 fusion.27
  196.0 25.2 %reduce-scatter.21.cloned.1.call-done = f32[1,128,1024]{2,1,0:T(8,128)} async-done(((f32[1,512,1024]{2,1,0:T(8,128)}), f32[1,128,1024]{2,1,0:T(8,128)}) %reduce-scatter.21.cloned.1.call-update) | async-done | bytes 524304 | tf_op jit(solution)/shard_map/reduce_scatter | solution.py:183
  222.5 22.9 %reduce-scatter.19.cloned.1.call-done = bf16[1,128,1024]{2,1,0:T(8,128)(2,1)} async-done(((bf16[1,512,1024]{2,1,0:T(8,128)(2,1)}), bf16[1,128,1024]{2,1,0:T(8,128)(2,1)}) %reduce-scatter.19.cloned.1.call-update) | async-done | bytes 262160 | tf_op jit(solution)/shard_map/reduce_scatter | solution.py:166
  245.3 2.1 fusion.116
  251.0 5.8 multiply_reduce_fusion.1
  256.8 5.6 fusion.4
  262.5 4.4 multiply_reduce_fusion
  268.5 2.3 maximum_convert_fusion
  270.8 2.6 fusion.117
  273.5 10.7 %copy.91 = bf16[1,512,2048]{2,0,1:T(2,128)(2,1)} copy(bf16[1,512,2048]{1,2,0:T(8,128)(2,1)} %get-tuple-element.39) | data formatting | bytes 4194304
  284.2 4.8 copy.168
  289.1 10.7 %copy.89 = bf16[1,512,2048]{2,0,1:T(2,128)(2,1)} copy(bf16[1,512,2048]{1,2,0:T(8,128)(2,1)} %get-tuple-element.40) | data formatting | bytes 4194304
  299.8 4.8 copy.169
  304.7 7.4 copy.87
  312.2 4.8 copy.170
  317.2 3.9 fusion.36
  321.1 3.2 convolution_convert_fusion.7
  325.7 1.7 collective-permute-done
  327.8 4.2 fusion.122
  333.1 14.9 %all-gather.1 = bf16[4,43,2048]{2,1,0:T(8,128)(2,1)S(1)} all-gather(bf16[1,43,2048]{2,1,0:T(8,128)(2,1)S(1)} %fusion.12), channel_id=2, replica_groups=mesh['dp'=32,'mp'=4] {'mp'}, dimensions={0}, use_global_device_ids=true | all-gather | bytes 880640 | tf_op jit(solution)/shard_map/all_gather | solution.py:140
  350.9 2.0 convolution_convert_fusion.6
  352.9 2.8 slice_bitcast_fusion.1
  355.7 2.3 copy.86
  359.3 3.5 fusion.124
  362.8 2.2 fusion.41
  370.0 20.9 %fusion = bf16[48,2048]{1,0:T(8,128)(2,1)S(1)} fusion(bf16[1,172,2048]{2,1,0:T(8,128)(2,1)S(1)} %pad_maximum_fusion.3), kind=kCustom, calls=%all-reduce-scatter | all-reduce-scatter fusion | flops 393217 | bytes 901632
  394.2 3.7 multiply_reduce_fusion.7
  398.7 4.5 convolution_convert_fusion
  403.3 1.7 reshape_bitcast_fusion
  405.8 1.7 reshape_bitcast_fusion.1
  408.4 1.7 reshape_bitcast_fusion.2
  411.0 4.7 convolution_convert_fusion.1
  416.9 4.0 convolution_convert_fusion.5
  420.9 3.0 convolution_convert_fusion.4
  425.3 31.5 %reduce-scatter.27.cloned.1.call-done = bf16[256,1024]{1,0:T(8,128)(2,1)} async-done(((bf16[1024,1024]{1,0:T(8,128)(2,1)}), bf16[256,1024]{1,0:T(8,128)(2,1)}) %reduce-scatter.27.cloned.1.call-update) | async-done | bytes 524304 | tf_op jit(solution)/shard_map/reduce_scatter | solution.py:258
  456.8 66.1 %reduce-scatter.29.cloned.1.call-done = bf16[768,1024]{1,0:T(8,128)(2,1)} async-done(((bf16[3072,1024]{1,0:T(8,128)(2,1)}), bf16[768,1024]{1,0:T(8,128)(2,1)}) %reduce-scatter.29.cloned.1.call-update) | async-done | bytes 1572880 | tf_op jit(solution)/shard_map/reduce_scatter | solution.py:261
  522.9 49.4 %reduce-scatter.25.cloned.1.call-done = bf16[256,2048]{1,0:T(8,128)(2,1)} async-done(((bf16[1024,2048]{1,0:T(8,128)(2,1)}), bf16[256,2048]{1,0:T(8,128)(2,1)}) %reduce-scatter.25.cloned.1.call-update) | async-done | bytes 1048592 | tf_op jit(solution)/shard_map/reduce_scatter | solution.py:255
  573.3 4.1 convolution_bitcast_fusion.1
  580.4 1.6 fusion.115
  582.1 98.1 %all-reduce.3 = (bf16[1024]{0:T(1024)(128)(2,1)S(1)}, bf16[8]{0:T(256)(128)(2,1)S(1)}, bf16[1024]{0:T(1024)(128)(2,1)S(1)}, bf16[1024]{0:T(1024)(128)(2,1)S(1)}) all-reduce(bf16[1024]{0:T(1024)(128)(2,1)S(1)} %get-tuple-element.13, bf16[8]{0:T(256)(128)(2,1)S(1)} %negate_convert_fusion, ...), channel_id=1, replica_groups=mesh['dp'=32,'mp'=4] {'dp'}, use_global_device_ids=true, to_apply=%region_17.18 | all-reduce | flops 3080 | bytes 12320 | tf_op jit(solution)/shard_map/psum | solution.py:244
  680.7 13.2 %all-reduce.2 = (f32[1024]{0:T(1024)}, f32[8]{0:T(128)}, f32[1024]{0:T(1024)}) all-reduce(bf16[1024]{0:T(1024)(128)(2,1)S(1)} %get-tuple-element.20, bf16[8]{0:T(256)(128)(2,1)S(1)} %get-tuple-element.21, bf16[1024]{0:T(1024)(128)(2,1)S(1)} %get-tuple-element.22), channel_id=1, replica_groups=mesh['dp'=32,'mp'=4] {'mp'}, use_global_device_ids=true, to_apply=%region_18.19 | all-reduce | flops 2056 | bytes 12336 | tf_op jit(solution)/shard_map/psum | solution.py:265
  693.9 2.0 fusion.59
  695.9 282.3 %all-reduce.7.cloned.1.call-done = (bf16[256,1024]{1,0:T(8,128)(2,1)}, bf16[256,2048]{1,0:T(8,128)(2,1)}, bf16[256,1024]{1,0:T(8,128)(2,1)}, bf16[1024,1024]{1,0...) async-done(((bf16[256,1024]{1,0:T(8,128)(2,1)}, bf16[256,2048]{1,0:T(8,128)(2,1)}, bf16[256,1024]{1,0:T(8,128)(2,1)}, bf16[1024,1024]{1,0:T(8,128)(2,1)}, ...) | async-done | bytes 7864336 | tf_op jit(solution)/shard_map/psum | solution.py:240
  978.2 2.2 convert_element_type.337
  983.1 2.5 convert_element_type.348
  985.6 2.5 convert_element_type.351
  988.1 2.1 convert_element_type.363
  (208 shorter events, 51.0 us)
Async XLA Ops:
  7.2 176.4 %copy-start = (bf16[1024,1024]{1,0:T(8,128)(2,1)S(1)}, bf16[1024,1024]{1,0:T(8,128)(2,1)}, u32[]{:S(2)}) copy-start(bf16[1024,1024]{1,0:T(8,128)(2,1)} %param.30) | copy-start | bytes 6291460
  7.2 40.2 %all-gather.8.cloned.1.call-start = ((), (), s32[]{:S(2)}) async-start(), calls=%async_computation.9 | async-start | bytes 2621440 | tf_op jit(solution)/shard_map/all_gather | solution.py:137
  14.5 2.8 copy-start.46
  14.5 4.1 copy-start.6
  14.5 4.1 copy-start.7
  14.5 4.1 copy-start.12
  15.7 3.2 copy-start.39
  15.8 63.9 %all-gather.10.cloned.1.call-start = ((), (), s32[]{:S(2)}) async-start(), calls=%async_computation.10 | async-start | bytes 2621440 | tf_op jit(solution)/shard_map/all_gather | solution.py:138
  16.5 95.5 %all-gather.12.cloned.1.call-start = ((), (), s32[]{:S(2)}) async-start(), calls=%async_computation.11 | async-start | bytes 2621440 | tf_op jit(solution)/shard_map/all_gather | solution.py:139
  17.2 143.1 %all-gather.14.cloned.1.call-start = ((), (), s32[]{:S(2)}) async-start(), calls=%async_computation.12 | async-start | bytes 1310720 | tf_op jit(solution)/shard_map/all_gather | solution.py:159
  18.6 1.6 copy-start.10
  20.2 1.2 copy-start.15
  21.4 108.3 %copy-start.21 = (bf16[16,8,8,128]{3,2,1,0:T(8,128)(2,1)}, bf16[16,8,8,128]{3,2,1,0:T(8,128)(2,1)S(1)}, u32[]{:S(2)}) copy-start(bf16[16,8,8,128]{3,2,1,0:T(8,128)(2,1)S(1)} %fusion.40) | copy-start | bytes 786436
  126.8 2.9 copy-start.16
  126.8 3.1 copy-start.18
  129.7 3.1 copy-start.4
  131.7 2.7 copy-start.2
  134.4 2.2 copy-start.8
  136.6 0.9 copy-start.40
  138.4 45.2 %all-gather.16.cloned.1.call-start = ((), (), s32[]{:S(2)}) async-start(), calls=%async_computation.14 | async-start | bytes 1310720 | tf_op jit(solution)/shard_map/all_gather | solution.py:176
  139.0 44.6 %copy-start.45 = (f32[1024]{0:T(1024)S(1)}, f32[1024]{0:T(1024)}, u32[]{:S(2)}) copy-start(f32[1024]{0:T(1024)} %param.29) | copy-start | bytes 12292
  139.0 82.2 %reduce-scatter.21.cloned.1.call-start = ((), (), s32[]{:S(2)}) async-start(), calls=%async_computation.15 | async-start | bytes 2621440 | tf_op jit(solution)/shard_map/reduce_scatter | solution.py:183
  183.6 5.5 copy-start.42
  188.1 1.0 copy-start.48
  191.8 53.6 %reduce-scatter.19.cloned.1.call-start = ((), (), s32[]{:S(2)}) async-start(), calls=%async_computation.13 | async-start | bytes 1310720 | tf_op jit(solution)/shard_map/reduce_scatter | solution.py:166
  195.9 207.3 %reduce-scatter.35.cloned.1.call-start = ((), (), s32[]{:S(2)}) async-start(), calls=%async_computation.22 | async-start | bytes 2621440
  196.0 52.3 %copy-start.9 = (bf16[1024,1024]{1,0:T(8,128)(2,1)S(1)}, bf16[1024,1024]{1,0:T(8,128)(2,1)}, u32[]{:S(2)}) copy-start(bf16[1024,1024]{1,0:T(8,128)(2,1)} %param.25) | copy-start | bytes 6291460
  245.3 2.9 copy-start.19
  247.4 0.8 copy-start.13
  256.8 5.6 copy-start.17
  262.5 4.4 copy-start.22
  266.9 1.7 copy-start.5
  289.0 116.8 %reduce-scatter.33.cloned.1.call-start = ((), (), s32[]{:S(2)}) async-start(), calls=%async_computation.21 | async-start | bytes 2621440
  304.7 103.7 %reduce-scatter.31.cloned.1.call-start = ((), (), s32[]{:S(2)}) async-start(), calls=%async_computation.20 | async-start | bytes 2621440
  317.0 108.3 %reduce-scatter.23.cloned.1.call-start = ((), (), s32[]{:S(2)}) async-start(), calls=%async_computation.16 | async-start | bytes 2621440 | tf_op jit(solution)/shard_map/reduce_scatter | solution.py:252
  321.1 3.2 copy-start.34
  324.3 132.5 %reduce-scatter.27.cloned.1.call-start = ((), (), s32[]{:S(2)}) async-start(), calls=%async_computation.18 | async-start | bytes 2621440 | tf_op jit(solution)/shard_map/reduce_scatter | solution.py:258
  324.4 3.1 collective-permute-start
  327.8 4.5 copy-start.3
  348.2 1.0 copy-start.23
  349.2 1.7 copy-start.28
  349.5 1.3 copy-start.32
  352.9 170.0 %reduce-scatter.29.cloned.1.call-start = ((), (), s32[]{:S(2)}) async-start(), calls=%async_computation.19 | async-start | bytes 7864320 | tf_op jit(solution)/shard_map/reduce_scatter | solution.py:261
  355.7 3.6 copy-start.24
  359.3 3.5 copy-start.30
  368.7 23.8 %copy-start.41 = (u32[128]{0:T(128)S(1)}, u32[128]{0:T(128)}, u32[]{:S(2)}) copy-start(u32[128]{0:T(128)} %constant.87) | copy-start | bytes 1540
  391.0 2.8 collective-permute-start.1
  403.2 169.1 %reduce-scatter.25.cloned.1.call-start = ((), (), s32[]{:S(2)}) async-start(), calls=%async_computation.17 | async-start | bytes 5242880 | tf_op jit(solution)/shard_map/reduce_scatter | solution.py:255
  411.0 4.7 copy-start.37
  415.6 1.2 copy-start.43
  415.7 562.5 %all-reduce.7.cloned.1.call-start = ((), (), s32[]{:S(2)}) async-start(), calls=%async_computation.23 | async-start | bytes 15728640 | tf_op jit(solution)/shard_map/psum | solution.py:240
  416.9 4.0 copy-start.44
  416.9 4.0 copy-start.47
  572.3 1.0 copy-start.38
  573.3 4.2 copy-start.35
  577.4 1.6 copy-start.11
  580.4 113.5 %copy-start.14 = (f32[1,128,1024]{2,1,0:T(8,128)S(1)}, f32[1,128,1024]{2,1,0:T(8,128)}, u32[]{:S(2)}) copy-start(f32[1,128,1024]{2,1,0:T(8,128)} %copy-done.13) | copy-start | bytes 1572868
  580.4 113.5 %copy-start.20 = (bf16[1,128,1024]{2,1,0:T(8,128)(2,1)S(1)}, bf16[1,128,1024]{2,1,0:T(8,128)(2,1)}, u32[]{:S(2)}) copy-start(bf16[1,128,1024]{2,1,0:T(8,128)(2,1)} %param.21) | copy-start | bytes 786436
  978.2 2.3 copy-start.29
  978.2 3.8 copy-start.36
  980.5 2.7 copy-start.26
  983.1 2.5 copy-start.25
  985.6 2.5 copy-start.27
  988.1 2.1 copy-start.1
  (2 other events, 1.4 us)
Sparse Core Ops, SparseCore 0:
  15.9 31.4 all-gather.7
  49.6 30.0 all-gather.9
  81.9 30.0 all-gather.11
  138.5 21.7 all-gather.13
  161.8 21.7 all-gather.15
  191.9 29.2 reduce-scatter.20
  224.2 21.0 reduce-scatter.18
  289.2 29.7 reduce-scatter.34
  321.5 33.4 reduce-scatter.32
  357.3 35.5 reduce-scatter.30
  395.9 29.2 reduce-scatter.22
  427.5 29.2 reduce-scatter.26
  459.3 63.4 reduce-scatter.28
  525.8 46.3 reduce-scatter.24
  576.3 401.8 all-reduce.6
where the time goes:
time: 1010 us; the launch traced here: 997 us
  waiting for transfers between devices  605 us (60%)
  blocking collectives  147 us (15%)
  local copies, waits for them, and re-layouts  100 us (10%)
  matrix products  87.2 us (9%)
  other arithmetic  35.8 us (4%)
  between operations  17.2 us (2%)
    psum x1, waiting for transfers between devices, per_device(): lax.psum(grad_query.astype(jnp.bfloat16), 'dp').astype(jnp.float32)  282 us
    psum x1, blocking collectives, per_device(): lax.psum(grad_attn_gain.astype(jnp.bfloat16), 'dp').astype(jnp.float32)  98.1 us
    unnamed x121, local copies, waits for them, and re-layouts  83.5 us
    reduce_scatter x1, waiting for transfers between devices, per_device(): lax.psum_scatter(summed[3].astype(jnp.bfloat16), 'mp', scatter_dimension=...  66.1 us
    reduce_scatter x1, waiting for transfers between devices, per_device(): lax.psum_scatter(summed[1].astype(jnp.bfloat16), 'mp', scatter_dimension=...  49.4 us
    reduce_scatter x1, waiting for transfers between devices, per_device(): lax.psum_scatter(summed[2].astype(jnp.bfloat16), 'mp', scatter_dimension=...  31.5 us
    all_gather x1, waiting for transfers between devices, per_device(): lax.all_gather(own_kv[:, seg_start:], 'mp', axis=1, tiled=True)  29.2 us
    all_gather x1, waiting for transfers between devices, per_device(): lax.all_gather(own_kv[:, old_rows:seg_start], 'mp', axis=1, tiled=True)  29.1 us
  transfers between devices with their start and end apart: 17, of which 13 were waited for; matrix products, arithmetic and copies ran while one was open for 14% of the time, Pallas kernels for 0%

commit v1 on v0

v1 whole, which is shorter than its diff:
```python
import functools

import jax
import jax.numpy as jnp
from jax import lax
from jax.experimental import pallas as pl
from jax.experimental.pallas import tpu as pltpu
from jax.sharding import PartitionSpec as P

D = 1024
H = 8
DH = 128
S = 512
M = 512
C = 512
CN = 172
CP = 192
EPS = 1e-05
NEG = -1e30
MESH = pl.DeviceIdType.MESH
BF = jnp.bfloat16
F32 = jnp.float32
VMEM = pl.BlockSpec(memory_space=pltpu.VMEM)


def dp_places():
    dp = lax.axis_index("dp")
    y, x, z = dp // 8, (dp // 2) % 4, dp % 2
    xa, xb = x + 1 - 2 * (x % 2), 3 - x
    ya, yb = y + 1 - 2 * (y % 2), 3 - y
    cube = [
        ((x + x // 2) % 2, y * 8 + xa * 2 + z),
        ((y + y // 2) % 2, ya * 8 + x * 2 + z),
        (x // 2, y * 8 + xb * 2 + z),
        (y // 2, yb * 8 + x * 2 + z),
    ]
    return cube, y * 8 + x * 2 + (1 - z)


def mp_places():
    mp = lax.axis_index("mp")
    zl, core = mp // 2, mp % 2
    return mp, zl, core, zl * 2 + (1 - core), (1 - zl) * 2 + core


def to_mp(src, dst, ssem, rsem, k, peer):
    return pltpu.make_async_remote_copy(
        src_ref=src, dst_ref=dst, send_sem=ssem.at[k], recv_sem=rsem.at[k],
        device_id=(lax.axis_index("dp"), peer), device_id_type=MESH,
    )


def to_dp(src, dst, ssem, rsem, k, peer):
    return pltpu.make_async_remote_copy(
        src_ref=src, dst_ref=dst, send_sem=ssem.at[k], recv_sem=rsem.at[k],
        device_id=(peer, lax.axis_index("mp")), device_id_type=MESH,
    )


def barrier(dps, mps):
    sem = pltpu.get_barrier_semaphore()
    for peer in dps:
        pl.semaphore_signal(sem, inc=1, device_id=(peer, lax.axis_index("mp")), device_id_type=MESH)
    for peer in mps:
        pl.semaphore_signal(sem, inc=1, device_id=(lax.axis_index("dp"), peer), device_id_type=MESH)
    pl.semaphore_wait(sem, len(dps) + len(mps))


def call(body, outs, args, sems, scratch, cid, aliases={}):
    return pl.pallas_call(
        body,
        out_shape=outs,
        in_specs=[VMEM] * len(args),
        out_specs=jax.tree.map(lambda _: VMEM, outs),
        scratch_shapes=list(scratch) + [pltpu.SemaphoreType.DMA((sems,)), pltpu.SemaphoreType.DMA((sems,))],
        input_output_aliases=aliases,
        compiler_params=pltpu.CompilerParams(
            collective_id=cid, has_side_effects=True, vmem_limit_bytes=52 << 20
        ),
    )(*args)


def rows_loop(total, step, body):
    def run(i, carry):
        body(pl.multiple_of(i * step, step))
        return carry

    lax.fori_loop(0, total // step, run, 0)


def gather_body(x_ref, o_ref, ssem, rsem):
    mp, zl, core, part, far = mp_places()
    barrier([], [part, far])
    a = to_mp(x_ref, o_ref.at[mp], ssem, rsem, 0, far)
    a.start()
    b = to_mp(x_ref, o_ref.at[mp], ssem, rsem, 1, part)
    b.start()
    o_ref[mp] = x_ref[...]
    a.wait_recv()
    c = to_mp(o_ref.at[far], o_ref.at[far], ssem, rsem, 2, part)
    c.start()
    b.wait()
    a.wait_send()
    c.wait()


def gather_mp(x, cid):
    return call(gather_body, jax.ShapeDtypeStruct((4,) + x.shape, x.dtype), (x,), 3, [], cid)


def sums_body(gnm, down, gnm_sum, down_sum, out, got, out2, got2, ssem, rsem):
    mp, zl, core, part, far = mp_places()
    barrier([], [part, far])
    for z in range(2):
        out[0, z] = gnm[2 * z + 1 - core].astype(BF)
    a = to_mp(out.at[0], got.at[0], ssem, rsem, 0, part)
    a.start()
    for z in range(2):
        out[1, z] = down[2 * z + 1 - core].astype(BF)
    b = to_mp(out.at[1], got.at[1], ssem, rsem, 1, part)
    b.start()
    a.wait()
    for z in range(2):
        out2[z] = (gnm[2 * z + core] + got[0, z].astype(F32)).astype(BF)
    a = to_mp(out2.at[pl.ds(0, 2)], got2.at[pl.ds(0, 2)], ssem, rsem, 2, far)
    a.start()
    b.wait()
    out2[2] = (down[(1 - zl) * 2 + core] + got[1, 1 - zl].astype(F32)).astype(BF)
    b = to_mp(out2.at[2], got2.at[2], ssem, rsem, 3, far)
    b.start()
    mine = down[zl * 2 + core] + got[1, zl].astype(F32)
    a.wait()
    for z in range(2):
        gnm_sum[z] = out2[z].astype(F32) + got2[z].astype(F32)
    b.wait()
    down_sum[...] = mine + got2[2].astype(F32)


def sums_mp(gnm, down, cid):
    buf = pltpu.VMEM((2, 2, 128, D), BF)
    buf2 = pltpu.VMEM((3, 128, D), BF)
    return call(
        sums_body,
        (jax.ShapeDtypeStruct((2, 128, D), F32), jax.ShapeDtypeStruct((128, D), F32)),
        (gnm.reshape(4, 128, D), down.reshape(4, 128, D)), 4, [buf, buf, buf2, buf2], cid,
    )


def pair_body(x_ref, o_ref, ssem, rsem):
    mp, zl, core, part, far = mp_places()
    barrier([], [part])
    copies = []
    for z in range(2):
        copies.append(to_mp(x_ref.at[z], o_ref.at[z, core], ssem, rsem, z, part))
        copies[-1].start()
    for z in range(2):
        o_ref[z, core] = x_ref[z]
    for c in copies:
        c.wait()


def pair_gather(x, cid):
    return call(pair_body, jax.ShapeDtypeStruct((2, 2) + x.shape[1:], x.dtype), (x,), 2, [], cid)


def tail_body(seg, sq, seg_sum, sq_sum, out, got, out2, got2, sout, sgot, sout2, sgot2, ssem, rsem):
    mp, zl, core, part, far = mp_places()
    barrier([], [part, far])
    sout[...] = sq[1 - core].astype(BF)
    a = to_mp(sout, sgot, ssem, rsem, 0, part)
    a.start()
    for z in range(2):
        out[z] = seg[2 * z + 1 - core].astype(BF)
    b = to_mp(out, got, ssem, rsem, 1, part)
    b.start()
    a.wait()
    sout2[...] = (sq[core] + sgot[...].astype(F32)).astype(BF)
    a = to_mp(sout2, sgot2, ssem, rsem, 2, far)
    a.start()
    b.wait()
    out2[...] = (seg[(1 - zl) * 2 + core] + got[1 - zl].astype(F32)).astype(BF)
    b = to_mp(out2, got2, ssem, rsem, 3, far)
    b.start()
    mine = seg[zl * 2 + core] + got[zl].astype(F32)
    a.wait()
    sq_sum[core] = (sout2[...].astype(F32) + sgot2[...].astype(F32)).astype(BF)
    a = to_mp(sq_sum.at[core], sq_sum.at[core], ssem, rsem, 4, part)
    a.start()
    b.wait()
    seg_sum[...] = mine + got2[...].astype(F32)
    a.wait()


def tail_mp(seg, sq, cid):
    buf, one = pltpu.VMEM((2, 128, D), BF), pltpu.VMEM((128, D), BF)
    half = pltpu.VMEM((96, D), BF)
    return call(
        tail_body,
        (jax.ShapeDtypeStruct((128, D), F32), jax.ShapeDtypeStruct((2, 96, D), BF)),
        (seg.reshape(4, 128, D), sq.reshape(2, 96, D)), 5, [buf, buf, one, one, half, half, half, half], cid,
    )


ROWS = 3072
CHUNKS = ((0, 1024), (1024, 1024), (2048, 768), (2816, 256))
STRIPS = 6


def add_into(dst, dst_at, src, src_at, rows):
    step = 64 if rows % 64 == 0 else 16

    def body(i, carry):
        to = dst_at(pl.multiple_of(i * step, 16), step)
        at = src_at(pl.multiple_of(i * step, 16), step)
        dst[to] = (dst[to].astype(F32) + src[at].astype(F32)).astype(BF)
        return carry

    lax.fori_loop(0, rows // step, body, 0)


def reduce_body(x_ref, t_ref, s_ref, o_ref, ot_ref, os_ref, recv, trecv, tpack, tgot, srecv, free, ssem, rsem):
    cube, zp = dp_places()
    mp, zl, core, part, far = mp_places()
    diag = 3 - mp
    others = (part, far, diag)
    barrier([peer for _, peer in cube] + [zp], others)
    o_ref[...] = x_ref[...]
    ot_ref[...] = t_ref[...]
    os_ref[...] = s_ref[...]
    count = [0]

    def sem():
        count[0] += 1
        return count[0] - 1

    pending = []

    def go(cp):
        cp.start()
        pending.append(cp)
        return cp

    places = [(r0, n, [r0] * 4, [[] for _ in range(4)]) for r0, n in CHUNKS]
    tcur, told = [0] * 4, [[] for _ in range(4)]
    small_steps = [peer for _, peer in cube] + [zp]

    for s in range(10):
        waits = []
        if s == 4:
            for cp in pending:
                cp.wait_send()
            pending.clear()
            for _, peer in cube:
                pl.semaphore_signal(free, inc=1, device_id=(peer, mp), device_id_type=MESH)
        if s == 5:
            pl.semaphore_wait(free, 4)
        if s < 7:
            k = sem()
            rows = pl.ds(0, 16) if s < 5 else pl.ds(0, 8)
            if s < 5:
                cp = go(to_dp(os_ref.at[rows], srecv.at[s, rows], ssem, rsem, k, small_steps[s]))
            else:
                cp = go(to_mp(os_ref.at[rows], srecv.at[s, rows], ssem, rsem, k, (part, far)[s - 5]))
            waits.append(("small", cp, s, rows))
        if s < 4:
            half = 256 >> (s + 1)
            for j in range(STRIPS):
                q = j % 4
                bit, peer = cube[(q + s) % 4]
                cols = pl.ds(128 * j, 128)
                keep = pl.multiple_of(tcur[q] + bit * half, 16)
                give = pl.multiple_of(tcur[q] + (1 - bit) * half, 16)
                at = 256 - (256 >> s)
                cp = go(to_dp(ot_ref.at[:, pl.ds(give, half), cols], trecv.at[:, pl.ds(at, half), cols], ssem, rsem, sem(), peer))
                waits.append(("strip", cp, j, keep, at, half))
            for q in range(4):
                bit, peer = cube[(q + s) % 4]
                told[q].append(tcur[q])
                tcur[q] = pl.multiple_of(tcur[q] + bit * half, 16)
        elif s == 4:
            for j in range(STRIPS):
                cols = pl.ds(128 * j, 128)
                cp = go(to_dp(ot_ref.at[:, pl.ds(tcur[j % 4], 16), cols], trecv.at[:, pl.ds(240, 16), cols], ssem, rsem, sem(), zp))
                waits.append(("strip", cp, j, tcur[j % 4], 240, 16))
        elif s == 5:
            for j in range(STRIPS):
                cols = pl.ds(128 * j, 128)
                tpack[:, j] = ot_ref[:, pl.ds(tcur[j % 4], 16), cols]
            for peer in others:
                cp = go(to_mp(tpack.at[peer], tgot.at[mp], ssem, rsem, sem(), peer))
                waits.append(("swap", cp))
        else:
            k = 9 - s
            half = 256 >> (k + 1)
            for j in range(STRIPS):
                q = j % 4
                bit, peer = cube[(q + k) % 4]
                cols = pl.ds(128 * j, 128)
                here = ot_ref.at[:, pl.ds(tcur[q], half), cols]
                waits.append(("got", go(to_dp(here, here, ssem, rsem, sem(), peer))))
            for q in range(4):
                tcur[q] = told[q][k]
        for r0, n, cur, old in places:
            if s == 9:
                continue
            for q in range(4):
                cols = pl.ds(256 * q, 256)
                if s < 4:
                    bit, peer = cube[(q + s) % 4]
                    half = n >> (s + 1)
                    keep = pl.multiple_of(cur[q] + bit * half, 16)
                    give = pl.multiple_of(cur[q] + (1 - bit) * half, 16)
                    at = r0 + n - (n >> s)
                    cp = go(to_dp(o_ref.at[pl.ds(give, half), cols], recv.at[pl.ds(at, half), cols], ssem, rsem, sem(), peer))
                    waits.append(("quarter", cp, keep, at, half, cols))
                    old[q].append(cur[q])
                    cur[q] = keep
                elif s == 4:
                    size = n >> 4
                    at = r0 + n - size
                    cp = go(to_dp(o_ref.at[pl.ds(cur[q], size), cols], recv.at[pl.ds(at, size), cols], ssem, rsem, sem(), zp))
                    waits.append(("quarter", cp, cur[q], at, size, cols))
                else:
                    k = 8 - s
                    bit, peer = cube[(q + k) % 4]
                    here = o_ref.at[pl.ds(cur[q], n >> (k + 1)), cols]
                    waits.append(("got", go(to_dp(here, here, ssem, rsem, sem(), peer))))
                    cur[q] = old[q][k]
        for kind, cp, *rest in waits:
            if s == 4 or kind in ("small", "swap"):
                cp.wait_send()
                pending[:] = [other for other in pending if other is not cp]
            cp.wait_recv()
            if kind == "small":
                step, rows = rest
                os_ref[rows, :] = os_ref[rows, :] + srecv[step, rows, :]
            elif kind == "strip":
                j, keep, at, half = rest
                cols = pl.ds(128 * j, 128)
                add_into(
                    ot_ref, lambda r, m: (slice(None), pl.ds(keep + r, m), cols),
                    trecv, lambda r, m: (slice(None), pl.ds(at + r, m), cols), half,
                )
            elif kind == "quarter":
                keep, at, half, cols = rest
                add_into(
                    o_ref, lambda r, m: (pl.ds(keep + r, m), cols),
                    recv, lambda r, m: (pl.ds(at + r, m), cols), half,
                )
        if s == 5:
            tgot[mp] = tpack[mp]
            for j in range(STRIPS):
                cols = pl.ds(128 * j, 128)
                ot_ref[:, pl.ds(tcur[j % 4], 16), cols] = tgot[:, j]
    for cp in pending:
        cp.wait_send()


def reduce_dp(x, t, s, cid):
    return call(
        reduce_body,
        tuple(jax.ShapeDtypeStruct(a.shape, a.dtype) for a in (x, t, s)),
        (x, t, s), 7 + 5 * STRIPS + 3 + 4 * STRIPS + 9 * 4 * len(CHUNKS),
        [
            pltpu.VMEM(x.shape, BF), pltpu.VMEM(t.shape, BF), pltpu.VMEM((4, STRIPS, 16, 128), BF),
            pltpu.VMEM((4, STRIPS, 16, 128), BF), pltpu.VMEM((7, 16, D), F32), pltpu.SemaphoreType.REGULAR,
        ],
        cid,
    )


def normalize(rows):
    centre = rows - jnp.mean(rows, axis=-1, keepdims=True)
    inv = lax.rsqrt(jnp.mean(centre * centre, axis=-1, keepdims=True) + EPS)
    return centre * inv, inv


def norm_back(grad, gain, unit, inv):
    g = grad * gain
    return inv * (g - jnp.mean(g, axis=-1, keepdims=True) - unit * jnp.mean(g * unit, axis=-1, keepdims=True))


def mm(a, b, dims="nn"):
    left = 1 if dims[0] == "n" else 0
    right = 0 if dims[1] == "n" else 1
    return lax.dot_general(a, b, (((left,), (right,)), ((), ())), preferred_element_type=F32)


def softmax(scores):
    weights = jnp.exp(scores - jnp.max(scores, axis=-1, keepdims=True))
    return weights / jnp.sum(weights, axis=-1, keepdims=True)


def per_device(
    layer_in, memory, squeezed_mem, memory_fill, squeezed_fill, grad_out, attn_gain, w_query, w_keyval,
    w_output, slopes, ffn_gain, w_up, up_bias, w_down, w_squeeze,
):
    mp, zl, core, part, far = mp_places()
    raw = jnp.concatenate([layer_in[0], memory[0], squeezed_mem[0], grad_out[0]], axis=0)
    whole = gather_mp(raw, 0).reshape(4, 4, 128, D)
    seg, mem, old, gout = (whole[:, a].reshape(512, D) for a in range(4))
    wq = lax.dynamic_slice_in_dim(w_query, mp * 256, 256, 1)
    wkv = jnp.concatenate(
        [lax.dynamic_slice_in_dim(w_keyval, mp * 256, 256, 1), lax.dynamic_slice_in_dim(w_keyval, D + mp * 256, 256, 1)], axis=1
    )
    wo = lax.dynamic_slice_in_dim(w_output, mp * 256, 256, 0)
    slope = lax.dynamic_slice_in_dim(slopes, mp * 2, 2, 0)
    unit, _ = normalize(jnp.concatenate([old, mem, seg], axis=0).astype(F32))
    normed = (unit * attn_gain).astype(BF)
    seg_normed = normed[C + M:]
    query = mm(seg_normed, wq).astype(BF)
    keyval = mm(normed, wkv).astype(BF)
    windows = jnp.concatenate([mem, jnp.zeros((3 * CP - M, D), BF)], axis=0).reshape(CP, 3 * D)
    squeezed = mm(windows, w_squeeze)
    sq_unit, sq_inv = normalize(squeezed)
    sq_kv = mm((sq_unit * attn_gain).astype(BF), wkv).astype(BF)

    rows = jnp.arange(S)[:, None]
    cols = jnp.arange(C + M + S)[None, :]
    distance = (C + M + rows - cols).astype(F32)
    mem_limit = M - memory_fill[0]
    old_limit = C - squeezed_fill[0]
    valid = (
        (cols < C) & (cols >= old_limit)
        | (cols >= C) & (cols < C + M) & (cols >= C + mem_limit)
        | (cols >= C + M) & (cols <= C + M + rows)
    )
    mem_valid = (jnp.arange(M) >= mem_limit)[None, :]
    slots = jnp.arange(CP)[None, :]
    sq_valid = (3 * slots < M) & (3 * slots + 2 >= mem_limit)
    scale = DH ** (-0.5)
    kept, mixed_own = [], []
    gsq_k, gsq_v = [], []
    for h in range(2):
        at = slice(h * DH, (h + 1) * DH)
        vat = slice(256 + h * DH, 256 + (h + 1) * DH)
        q, k, v = query[:, at], keyval[:, at], keyval[:, vat]
        probs = softmax(jnp.where(valid, mm(q, k, "nt") * scale - slope[h] * distance, NEG))
        mixed_own.append(mm(probs.astype(BF), v).astype(BF))
        kept.append(probs)
        km, vm = keyval[C : C + M, at], keyval[C : C + M, vat]
        first = mm(softmax(jnp.where(mem_valid, mm(q, km, "nt") * scale, NEG)).astype(BF), vm)
        ks, vs = sq_kv[:, at], sq_kv[:, vat]
        sprobs = softmax(jnp.where(sq_valid, mm(q, ks, "nt") * scale, NEG))
        second = mm(sprobs.astype(BF), vs)
        gsecond = ((first - second) * (-2.0 / (S * D))).astype(BF)
        gp = mm(gsecond, vs, "nt")
        gsq_v.append(mm(sprobs.astype(BF), gsecond, "tn"))
        gs = (sprobs * (gp - jnp.sum(sprobs * gp, axis=-1, keepdims=True))).astype(BF)
        gsq_k.append(mm(gs, q, "tn") * scale)
    mixed_own = jnp.concatenate(mixed_own, axis=1)
    mixed = gather_mp(mixed_own, 1).transpose(1, 0, 2).reshape(S, D)
    gsq = jnp.concatenate(gsq_k + gsq_v, axis=1).astype(BF)
    dsq = mm(gsq, wkv, "nt")
    dsq = norm_back(dsq, attn_gain, sq_unit, sq_inv)

    mid = seg.astype(F32) + mm(mixed, w_output)
    mid_unit, mid_inv = normalize(mid)
    normed_mid = (mid_unit * ffn_gain).astype(BF)
    pre = mm(normed_mid, w_up) + up_bias
    hidden, gelu_back = jax.vjp(jax.nn.gelu, pre)
    hidden = hidden.astype(BF)
    down = mm(hidden, w_down)
    grad_down = mm(hidden, gout, "tn")
    ghid = mm(gout, w_down, "nt")
    gpre = gelu_back(ghid)[0].astype(BF)
    grad_up_bias = jnp.sum(gpre.astype(F32), axis=0)
    grad_up = mm(normed_mid, gpre, "tn")
    gnm, down_sum = sums_mp(mm(gpre, w_up, "nt"), down, 2)

    own_mid = lax.dynamic_slice_in_dim(mid, mp * 128, 128, 0)
    layer_out = (own_mid + down_sum).astype(BF)

    def parity(a):
        return lax.dynamic_index_in_dim(a.reshape(2, 2, 128, a.shape[-1]), core, 1, keepdims=False)

    unit2, inv2 = parity(mid_unit), parity(mid_inv)
    gmid = parity(gout).astype(F32) + norm_back(gnm, ffn_gain, unit2, inv2)
    own_gnm = lax.dynamic_index_in_dim(gnm, zl, 0, keepdims=False)
    own_unit = lax.dynamic_index_in_dim(unit2, zl, 0, keepdims=False)
    grad_ffn_gain = jnp.sum(own_gnm * own_unit, axis=0)
    own_gmid = lax.dynamic_index_in_dim(gmid, zl, 0, keepdims=False)
    gbranch = pair_gather(gmid.astype(BF), 3).reshape(S, D)
    grad_output = mm(mixed_own, gbranch, "tn")
    gmix = mm(gbranch, wo, "nt").astype(BF)
    gk, gv, gq, gslope = [], [], [], []
    for h in range(2):
        at = slice(h * DH, (h + 1) * DH)
        vat = slice(256 + h * DH, 256 + (h + 1) * DH)
        probs, g = kept[h], gmix[:, at]
        gp = mm(g, keyval[:, vat], "nt")
        gv.append(mm(probs.astype(BF), g, "tn"))
        gs = (probs * (gp - jnp.sum(probs * gp, axis=-1, keepdims=True))).astype(BF)
        gslope.append(-jnp.sum(gs.astype(F32) * distance))
        gq.append((mm(gs, keyval[:, at]) * scale).astype(BF))
        gk.append(mm(gs, query[:, at], "tn") * scale)
    gkv = jnp.concatenate(gk + gv, axis=1).astype(BF)
    gq = jnp.concatenate(gq, axis=1)
    grad_kv = mm(normed, gkv, "tn")
    grad_q = mm(seg_normed, gq, "tn")
    grad_attn_gain = (jnp.sum(grad_kv * wkv.astype(F32), axis=1) + jnp.sum(grad_q * wq.astype(F32), axis=1)) / attn_gain
    seg_terms = mm(gkv[C + M:], wkv, "nt") + mm(gq, wq, "nt")
    seg_sum, dsq_sum = tail_mp(seg_terms, dsq, 4)
    own_seg = layer_in[0].astype(F32)
    seg_unit, seg_inv = normalize(own_seg)
    grad_in = own_gmid + norm_back(seg_sum, attn_gain, seg_unit, seg_inv)
    own_windows = lax.dynamic_slice_in_dim(windows, mp * 768, 768, 1)
    grad_squeeze = mm(own_windows, dsq_sum.reshape(CP, D), "tn")

    x = jnp.concatenate([g.astype(BF) for g in (grad_down, grad_up, grad_squeeze, grad_output)], axis=0)
    t = jnp.concatenate([grad_kv, grad_q], axis=1).astype(BF).reshape(4, 256, 768)
    slope_row = lax.dynamic_update_slice(jnp.zeros((D,), F32), jnp.stack(gslope), (mp * 2,))
    s = jnp.concatenate(
        [jnp.stack([grad_attn_gain, grad_ffn_gain, slope_row]), jnp.zeros((5, D), F32), grad_up_bias[None], jnp.zeros((7, D), F32)], axis=0
    )
    x, t, s = reduce_dp(x, t, s, 5)
    x = x.astype(F32)
    t = t.astype(F32).transpose(1, 0, 2)
    new_squeezed = lax.dynamic_slice_in_dim(squeezed, mp * 43, 43, 0).astype(BF)
    return (
        layer_out[None],
        new_squeezed[None],
        grad_in[None],
        s[0],
        t[:, :, 512:].reshape(256, D),
        jnp.concatenate([t[:, :, :256].reshape(256, D), t[:, :, 256:512].reshape(256, D)], axis=1),
        x[2816:],
        s[2, :8],
        s[1],
        x[1024:2048],
        s[8],
        x[:1024],
        x[2048:2816],
    )


def solution(mesh):
    rows = P("dp", "mp", None)
    in_specs = (
        rows, rows, rows, P("dp"), P("dp"), rows, P(), P(), P(), P(), P(), P(), P(None, "mp"), P("mp"), P("mp", None), P(),
    )
    out_specs = (
        rows, rows, rows, P(), P("mp", None), P("mp", None), P("mp", None), P(), P(), P(None, "mp"), P("mp"), P("mp", None), P("mp", None),
    )
    return jax.shard_map(per_device, mesh=mesh, in_specs=in_specs, out_specs=out_specs, check_vma=False)
```

time: 1010 us -> 367 us (0.36)
  waiting for transfers between devices: 605 us -> 0 us
  Pallas kernels: 0 us -> 211 us
  blocking collectives: 147 us -> 0 us
  local copies, waits for them, and re-layouts: 100 us -> 44 us
  matrix products: 87.2 us -> 55 us
  between operations: 17.2 us -> 4.43 us
  other arithmetic: 35.8 us -> 47.1 us
    psum x1 -> x0, waiting for transfers between devices: 282 us -> none  [per_device(): lax.psum(grad_query.astype(jnp.bfloat16), 'dp').astype(jnp.float32)]
    pallas_call x0 -> x6, Pallas kernels: none -> 211 us  [call(): pl.pallas_call(body, out_shape=outs, in_specs=[VMEM] * len(args), out_spe...]
    reduce_scatter x6 -> x0, waiting for transfers between devices: 196 us -> none  [the longest x1 66.1 us: per_device(): lax.psum_scatter(summed[3].astype(jnp.bfloat16), 'mp', scatter_dimension=...]
    all_gather x5 -> x0, waiting for transfers between devices: 123 us -> none  [the longest x1 29.2 us: per_device(): lax.all_gather(own_kv[:, seg_start:], 'mp', axis=1, tiled=True)]
    psum x2 -> x0, blocking collectives: 111 us -> none  [the longest x1 98.1 us: per_device(): lax.psum(grad_attn_gain.astype(jnp.bfloat16), 'dp').astype(jnp.float32)]
    unnamed x121 -> x112, local copies, waits for them, and re-layouts: 83.5 us -> 15.5 us
    dot_general x31 -> x45, matrix products: 83.8 us -> 55 us  [mm(): lax.dot_general(a, b, (((left,), (right,)), ((), ())), preferred_element_...]
    unnamed x1 -> x0, blocking collectives: 20.9 us -> none
  transfers between devices with their start and end apart: 17 -> 0, of which waited for: 13 -> 0; matrix products, arithmetic and copies ran while one was open for 14% -> 0% of each run, Pallas kernels for 0% -> 0%
where the time goes in v1:
time: 367 us; the launch traced here: 361 us
  Pallas kernels  211 us (57%)
  matrix products  55 us (15%)
  other arithmetic  47.1 us (13%)
  local copies, waits for them, and re-layouts  44 us (12%)
  between operations  4.43 us (1%)
    pallas_call x6, Pallas kernels, call(): pl.pallas_call(body, out_shape=outs, in_specs=[VMEM] * len(args), out_spe...  211 us
    dot_general x45, matrix products, mm(): lax.dot_general(a, b, (((left,), (right,)), ((), ())), preferred_element_...  55 us
    concatenate x1, other arithmetic, per_device(): jnp.concatenate([g.astype(BF) for g in (grad_down, grad_up, grad_squeeze,...  16.3 us
    unnamed x112, local copies, waits for them, and re-layouts  15.5 us

profile of v1, /device:TPU:0, one launch (start us, length us, event | category | flops | bytes accessed | tf_op | source)
XLA Modules:
  0.0 361.4 jit_solution(2377753894066693821)
XLA Ops:
  0.7 0.9 dynamic_slice.49
  2.1 1.3 pad_maximum_fusion.4.x_ref
  3.4 30.2 %shard_map.255 = bf16[4,512,1024]{2,1,0:T(8,128)(2,1)} custom-call(bf16[512,1024]{1,0:T(8,128)(2,1)S(1)} %pad_maximum_fusion.4.x_ref), custom_call_target="tpu_custom_call" | custom-call | tf_op jit(solution)/shard_map/pallas_call | solution.py:70
  33.6 3.8 %fusion.166 = (bf16[4,1,128,1024]{3,2,1,0:T(8,128)(2,1)S(1)}, bf16[4,1,128,1024]{3,2,1,0:T(8,128)(2,1)S(1)}, bf16[4,1,128,1024]{3,2,1,0:T(8,128)(2,1)S(1)}, bf16[4,1,128,1024]{3,2,1,0:T(8,128)(2,1)}) fusion(bf16[4,4,128,1024]{3,2,1,0:T(8,128)(2,1)} %bitcast.132), kind=kLoop, calls=%fused_computation.272 | loop fusion | bytes 8388608 | tf_op jit(solution)/shard_map/slice | solution.py:401
  37.9 3.0 fusion.2
  41.0 4.6 %fusion.4 = bf16[1536,1024]{1,0:T(8,128)(2,1)} fusion(f32[1024]{0:T(1024)S(1)} %copy-done.41, f32[1536]{0:T(1024)S(1)} %add_rsqrt_fusion, f32[1536]{0:T(1024)S(1)} %broadcast_multiply_fusion, bf16[512,1024]{1,0:T(8,128)(2,1)S(1)} %bitcast.128, bf16[512,1024]{1,0:T(8,128)(2,1)S(1)} %bitcast.124, bf16[512,1024]{1,0:T(8,128)(2,1)S(1)} %bitcast.135), kind=kLoop, calls=%fused_computation.6 | loop fusion | flops 15728640 | bytes 6307840 | tf_op jit(solution)/shard_map/convert_element_type | solution.py:409
  45.6 1.3 constant_dynamic-slice_fusion.2
  46.9 0.8 copy-done.29
  47.9 4.9 %convolution_convert_fusion = bf16[1536,512]{1,0:T(8,128)(2,1)} fusion(bf16[1536,1024]{1,0:T(8,128)(2,1)} %fusion.4, bf16[1024,256]{1,0:T(8,128)(2,1)S(1)} %get-tuple-element.57, bf16[1024,256]{1,0:T(8,128)(2,1)S(1)} %get-tuple-element.56), kind=kOutput, calls=%fused_computation.30 | convolution fusion | flops 1613496320 | bytes 5767168 | tf_op jit(solution)/shard_map/dot_general | solution.py:386
  52.8 1.9 convolution_convert_fusion.8
  56.1 2.3 fusion.170
  58.9 0.7 fusion.13
  60.6 2.3 fusion.171
  63.5 0.7 fusion.11
  65.3 1.1 copy-done.4
  67.0 9.9 %shard_map.256 = bf16[4,512,256]{2,1,0:T(8,128)(2,1)S(1)} custom-call(bf16[512,256]{1,0:T(8,128)(2,1)S(1)} %pad_maximum_fusion.6.x_ref), custom_call_target="tpu_custom_call" | custom-call | tf_op jit(solution)/shard_map/pallas_call | solution.py:70
  76.9 1.5 copy.40
  78.4 3.5 fusion.172
  83.2 1.1 copy-done.43
  84.3 1.3 fusion.81
  86.3 2.5 convert_reduce_fusion.1
  88.8 2.6 fusion.178
  91.4 2.9 fusion.160
  94.3 24.2 %shard_map.257 = (f32[2,128,1024]{2,1,0:T(8,128)S(1)}, f32[128,1024]{1,0:T(8,128)S(1)}) custom-call(f32[4,128,1024]{2,1,0:T(8,128)} %bitcast.148, f32[4,128,1024]{2,1,0:T(8,128)} %bitcast.149), custom_call_target="tpu_custom_call" | custom-call | tf_op jit(solution)/shard_map/pallas_call | solution.py:70
  118.5 1.8 fusion.100
  120.5 1.4 reshape.257
  121.9 4.6 %fusion.174 = (f32[192]{0:T(256)S(1)}, f32[192,1024]{1,0:T(8,128)S(1)}) fusion(bf16[192,3072]{1,0:T(8,128)(2,1)} %reshape.257, bf16[3072,1024]{1,0:T(8,128)(2,1)} %param.31), kind=kOutput, calls=%fused_computation.280 | convolution fusion | flops 1208155904 | bytes 8258304 | tf_op jit(solution)/shard_map/dot_general | solution.py:386
  126.5 0.7 fusion.118
  127.2 1.5 multiply_reduce_fusion.7
  128.7 2.5 fusion.163
  131.2 1.9 shard_map.258
  133.2 1.5 convolution_convert_fusion.7
  135.2 1.5 copy-done.5
  137.1 1.1 copy-done.17
  138.2 0.7 multiply_reduce_fusion.3
  138.9 0.7 multiply_reduce_fusion.2
  139.5 1.2 copy-done.7
  140.8 1.0 copy-done.9
  141.7 4.3 %multiply_reduce_fusion.1 = (f32[]{:T(128)}, f32[]{:T(128)}, bf16[512,1536]{1,0:T(8,128)(2,1)S(1)}, bf16[512,1536]{1,0:T(8,128)(2,1)S(1)}) fusion(s32[512]{0:T(512)S(1)} %iota_add_fusion, f32[512,1536]{1,0:T(8,128)S(1)} %get-tuple-element.81, f32[512]{0:T(512)S(1)} %get-tuple-element.80, f32[512,1536]{1,0:T(8,128)S(1)} %get-tuple-element.83, ...), kind=kLoop, calls=%fused_computation.17 | loop fusion | flops 14155774 | bytes 15742984 | tf_op jit(solution)/shard_map/reduce_sum | solution.py:494
  147.2 0.8 fusion.67
  148.7 0.7 fusion.40
  149.3 2.9 convolution_add_fusion
  157.3 0.7 fusion.161
  158.3 16.1 %shard_map.259 = (f32[128,1024]{1,0:T(8,128)S(1)}, bf16[2,96,1024]{2,1,0:T(8,128)(2,1)S(1)}) custom-call(f32[4,128,1024]{2,1,0:T(8,128)} %bitcast.139, f32[2,96,1024]{2,1,0:T(8,128)S(1)} %bitcast.118), custom_call_target="tpu_custom_call" | custom-call | tf_op jit(solution)/shard_map/pallas_call | solution.py:70
  175.0 1.0 fusion.65
  176.5 1.6 convolution_convert_fusion.5
  178.1 3.3 convolution_convert_fusion.3
  181.5 1.6 convolution_convert_fusion.4
  183.1 16.3 %pad_maximum_fusion.x_ref = bf16[3072,1024]{1,0:T(8,128)(2,1)} fusion(bf16[256,1024]{1,0:T(8,128)(2,1)S(1)} %convolution_convert_fusion.6, bf16[768,1024]{1,0:T(8,128)(2,1)S(1)} %convolution_convert_fusion.5, bf16[1024,1024]{1,0:T(8,128)(2,1)S(1)} %convolution_convert_fusion.3, bf16[1024,1024]{1,0:T(8,128)(2,1)S(1)} %convolution_convert_fusion.4), kind=kLoop, calls=%fused_computation.7 | loop fusion | flops 25165824 | bytes 12582912 | tf_op jit(solution)/shard_map/concatenate | solution.py:510
  199.5 1.8 multiply_reduce_fusion.6
  201.3 1.9 multiply_reduce_fusion.4
  203.2 1.2 pad_maximum_fusion.3.t_ref
  204.4 1.1 fusion.75
  207.1 128.6 %shard_map.260 = (bf16[3072,1024]{1,0:T(8,128)(2,1)}, bf16[4,256,768]{2,1,0:T(8,128)(2,1)S(1)}, f32[16,1024]{1,0:T(8,128)S(1)}) custom-call(bf16[3072,1024]{1,0:T(8,128)(2,1)} %pad_maximum_fusion.x_ref, bf16[4,256,768]{2,1,0:T(8,128)(2,1)} %pad_maximum_fusion.3.t_ref, f32[16,1024]{1,0:T(8,128)S(1)} %concatenate.56.s_ref), custom_call_target="tpu_custom_call" | custom-call | tf_op jit(solution)/shard_map/pallas_call | solution.py:70
  336.7 1.7 fusion.167
  338.3 1.6 copy.44
  339.9 1.3 copy.47
  341.2 1.6 copy.46
  342.8 1.3 copy.45
  344.1 2.7 pad_maximum_fusion.2
  346.7 2.9 copy.48
  349.6 2.1 slice.170
  352.3 6.8 %fusion.165 = (f32[1024,1024]{1,0:T(8,128)}, f32[1024,1024]{1,0:T(8,128)}) fusion(bf16[3072,1024]{1,0:T(8,128)(2,1)} %get-tuple-element.26), kind=kLoop, calls=%fused_computation.271 | loop fusion | bytes 16777216 | tf_op jit(solution)/shard_map/slice | solution.py:532
  359.1 2.1 slice.173
  (172 shorter events, 18.1 us)
Async XLA Ops:
  0.6 85.0 %copy-start = (bf16[1024,1024]{1,0:T(8,128)(2,1)S(1)}, bf16[1024,1024]{1,0:T(8,128)(2,1)}, u32[]{:S(2)}) copy-start(bf16[1024,1024]{1,0:T(8,128)(2,1)} %param.30) | copy-start | bytes 6291460
  37.3 3.6 %copy-start.10 = (bf16[4,1,128,1024]{3,2,1,0:T(8,128)(2,1)}, bf16[4,1,128,1024]{3,2,1,0:T(8,128)(2,1)S(1)}, u32[]{:S(2)}) copy-start(bf16[4,1,128,1024]{3,2,1,0:T(8,128)(2,1)S(1)} %get-tuple-element.59) | copy-start | bytes 3145732
  37.3 3.6 %copy-start.12 = (bf16[4,1,128,1024]{3,2,1,0:T(8,128)(2,1)}, bf16[4,1,128,1024]{3,2,1,0:T(8,128)(2,1)S(1)}, u32[]{:S(2)}) copy-start(bf16[4,1,128,1024]{3,2,1,0:T(8,128)(2,1)S(1)} %get-tuple-element.60) | copy-start | bytes 3145732
  37.9 3.1 copy-start.41
  46.9 0.8 copy-start.29
  46.9 1.0 copy-start.32
  52.8 3.3 copy-start.16
  54.7 5.9 %copy-start.39 = (bf16[512,256]{1,0:T(8,128)(2,1)}, bf16[512,256]{1,0:T(8,128)(2,1)S(1)}, u32[]{:S(2)}) copy-start(bf16[512,256]{1,0:T(8,128)(2,1)S(1)} %convolution_convert_fusion.8) | copy-start | bytes 786436
  58.4 1.7 copy-start.6
  60.0 2.9 copy-start.2
  60.6 4.6 %copy-start.25 = (bf16[512,128]{1,0:T(8,128)(2,1)}, bf16[512,128]{1,0:T(8,128)(2,1)S(1)}, u32[]{:S(2)}) copy-start(bf16[512,128]{1,0:T(8,128)(2,1)S(1)} %convolution_convert_fusion.10) | copy-start | bytes 393220
  63.0 1.7 copy-start.8
  64.7 1.7 copy-start.4
  66.3 0.7 copy-start.27
  81.9 1.3 copy-start.13
  82.3 0.9 copy-start.42
  82.3 2.0 copy-start.43
  84.3 1.3 copy-start.14
  84.3 2.0 copy-start.20
  84.3 2.0 copy-start.44
  85.6 5.8 %copy-start.50 = (f32[512,1024]{1,0:T(8,128)}, f32[512,1024]{1,0:T(8,128)S(1)}, u32[]{:S(2)}) copy-start(f32[512,1024]{1,0:T(8,128)S(1)} %fusion.81) | copy-start | bytes 6291460
  88.8 2.6 copy-start.52
  94.3 26.0 %copy-start.11 = (bf16[4,1,128,1024]{3,2,1,0:T(8,128)(2,1)S(1)}, bf16[4,1,128,1024]{3,2,1,0:T(8,128)(2,1)}, u32[]{:S(2)}) copy-start(bf16[4,1,128,1024]{3,2,1,0:T(8,128)(2,1)} %copy-done.10) | copy-start | bytes 3145732
  126.5 2.2 copy-start.21
  131.2 3.5 copy-start.3
  134.7 1.9 copy-start.5
  136.6 10.2 %copy-start.35 = (bf16[1536,128]{0,1:T(8,128)(2,1)}, bf16[1536,128]{0,1:T(8,128)(2,1)S(1)}, u32[]{:S(2)}) copy-start(bf16[1536,128]{0,1:T(8,128)(2,1)S(1)} %convolution_convert_fusion.1) | copy-start | bytes 1179652
  136.6 1.5 copy-start.17
  138.2 8.7 %copy-start.37 = (bf16[1536,128]{0,1:T(8,128)(2,1)}, bf16[1536,128]{0,1:T(8,128)(2,1)S(1)}, u32[]{:S(2)}) copy-start(bf16[1536,128]{0,1:T(8,128)(2,1)S(1)} %convolution_convert_fusion.2) | copy-start | bytes 1179652
  138.9 1.9 copy-start.7
  138.9 2.8 copy-start.9
  141.7 4.3 %copy-start.40 = (bf16[512,256]{1,0:T(8,128)(2,1)S(1)}, bf16[512,256]{1,0:T(8,128)(2,1)}, u32[]{:S(2)}) copy-start(bf16[512,256]{1,0:T(8,128)(2,1)} %copy-done.39) | copy-start | bytes 786436
  146.0 1.0 copy-start.30
  146.0 1.2 copy-start.33
  146.4 1.5 copy-start.46
  147.2 0.8 copy-start.48
  149.3 2.9 copy-start.23
  158.0 16.4 %copy-start.15 = (bf16[1,128,1024]{2,1,0:T(8,128)(2,1)S(1)}, bf16[1,128,1024]{2,1,0:T(8,128)(2,1)}, u32[]{:S(2)}) copy-start(bf16[1,128,1024]{2,1,0:T(8,128)(2,1)} %param.16) | copy-start | bytes 786436
  158.2 16.7 %copy-start.19 = (f32[2,128,1024]{2,1,0:T(8,128)S(1)}, f32[2,128,1024]{2,1,0:T(8,128)}, u32[]{:S(2)}) copy-start(f32[2,128,1024]{2,1,0:T(8,128)} %get-tuple-element.53) | copy-start | bytes 3145732
  174.3 1.7 copy-start.26
  174.3 1.7 copy-start.28
  178.1 3.3 copy-start.22
  178.1 3.3 copy-start.45
  178.1 3.3 copy-start.51
  183.1 16.3 %copy-start.18 = (bf16[1536,1024]{1,0:T(8,128)(2,1)S(1)}, bf16[1536,1024]{1,0:T(8,128)(2,1)}, u32[]{:S(2)}) copy-start(bf16[1536,1024]{1,0:T(8,128)(2,1)} %fusion.4) | copy-start | bytes 9437188
  183.1 16.3 %copy-start.24 = (bf16[512,128]{0,1:T(8,128)(2,1)S(1)}, bf16[512,128]{0,1:T(8,128)(2,1)}, u32[]{:S(2)}) copy-start(bf16[512,128]{0,1:T(8,128)(2,1)} %copy-done.23) | copy-start | bytes 393220
  199.4 1.8 copy-start.31
  199.4 1.8 copy-start.34
  199.4 1.8 copy-start.36
  199.4 1.8 copy-start.38
  199.4 1.8 copy-start.47
  199.4 1.8 copy-start.49
  352.3 6.8 %slice-start = ((s8[6291456]{0:T(1024)(128)(4,1)}), s8[4194304]{0:T(1024)(128)(4,1)S(1)}, s32[]{:S(2)}) async-start(s8[6291456]{0:T(1024)(128)(4,1)} %bitcast.130), calls=%async_computation | async-start | bytes 8388608
  352.3 6.8 %slice-start.1 = ((s8[6291456]{0:T(1024)(128)(4,1)}), s8[2097152]{0:T(1024)(128)(4,1)S(1)}, s32[]{:S(2)}) async-start(s8[6291456]{0:T(1024)(128)(4,1)} %bitcast.130), calls=%async_computation.1 | async-start | bytes 4194304
  359.1 2.1 copy-start.1

commit v2 on v0

v2 whole, which is shorter than its diff:
```python
import functools

import jax
import jax.numpy as jnp
from jax import lax
from jax.experimental import pallas as pl
from jax.experimental.pallas import tpu as pltpu
from jax.sharding import PartitionSpec as P

D = 1024
H = 8
DH = 128
S = 512
M = 512
C = 512
CN = 172
CP = 192
EPS = 1e-05
NEG = -1e30
SCALE = DH ** (-0.5)
RECON = -2.0 / (S * D)
MESH = pl.DeviceIdType.MESH
BF = jnp.bfloat16
F32 = jnp.float32
VMEM = pl.BlockSpec(memory_space=pltpu.VMEM)
SMEM = pl.BlockSpec(memory_space=pltpu.SMEM)
ANY = pl.BlockSpec(memory_space=pl.ANY)
STRIPS = 6
SEG, MEM, OLD, GOUT = 0, 1, 2, 3
BASE = {OLD: 0, MEM: 512, SEG: 1024}
COPIES = 420


def dp_places():
    dp = lax.axis_index("dp")
    y, x, z = dp // 8, (dp // 2) % 4, dp % 2
    xa, xb = x + 1 - 2 * (x % 2), 3 - x
    ya, yb = y + 1 - 2 * (y % 2), 3 - y
    cube = [
        ((x + x // 2) % 2, y * 8 + xa * 2 + z),
        ((y + y // 2) % 2, ya * 8 + x * 2 + z),
        (x // 2, y * 8 + xb * 2 + z),
        (y // 2, yb * 8 + x * 2 + z),
    ]
    return cube, y * 8 + x * 2 + (1 - z)


def mp_places():
    mp = lax.axis_index("mp")
    zl, core = mp // 2, mp % 2
    return mp, zl, core, zl * 2 + (1 - core), (1 - zl) * 2 + core


class Links:
    def __init__(self, ssem, rsem):
        self.ssem, self.rsem, self.count = ssem, rsem, 0

    def start(self, src, dst, place):
        k = self.count
        self.count += 1
        cp = pltpu.make_async_remote_copy(
            src_ref=src, dst_ref=dst, send_sem=self.ssem.at[k], recv_sem=self.rsem.at[k],
            device_id=place, device_id_type=MESH,
        )
        cp.start()
        return cp

    def mp(self, src, dst, peer):
        return self.start(src, dst, (lax.axis_index("dp"), peer))

    def dp(self, src, dst, peer):
        return self.start(src, dst, (peer, lax.axis_index("mp")))


def loop(total, step, body, init=None):
    def run(i, carry):
        return body(pl.multiple_of(i * step, step), carry)

    return lax.fori_loop(0, total // step, run, init)


def each(total, step, body):
    def run(r, carry):
        body(r)
        return carry

    loop(total, step, run, 0)


def add_into(dst, dst_at, src, src_at, rows):
    step = 64 if rows % 64 == 0 else 16

    def body(r):
        to, at = dst_at(r, step), src_at(r, step)
        dst[to] = (dst[to].astype(F32) + src[at].astype(F32)).astype(BF)

    each(rows, step, body)


class Quarters:
    def __init__(self, links, ref, n, recv, base, free):
        self.links, self.ref, self.n, self.recv, self.base, self.free = links, ref, n, recv, base, free
        self.cube, self.zp = dp_places()
        self.cur, self.old = [0] * 4, [[] for _ in range(4)]
        self.flying, self.sent, self.stage = [None] * 4, [], 0

    def launch(self, q, s):
        cols = pl.ds(256 * q, 256)
        n, cur = self.n, self.cur
        if s < 4:
            bit, peer = self.cube[(q + s) % 4]
            half = n >> (s + 1)
            give = pl.multiple_of(cur[q] + (1 - bit) * half, 16)
            self.old[q].append(cur[q])
            cur[q] = pl.multiple_of(cur[q] + bit * half, 16)
            cp = self.links.dp(
                self.ref.at[pl.ds(give, half), cols], self.recv.at[pl.ds(self.base + n - (n >> s), half), cols], peer
            )
        elif s == 4:
            size = n >> 4
            cp = self.links.dp(
                self.ref.at[pl.ds(cur[q], size), cols], self.recv.at[pl.ds(self.base + n - size, size), cols], self.zp
            )
        else:
            k = 8 - s
            bit, peer = self.cube[(q + k) % 4]
            here = self.ref.at[pl.ds(cur[q], n >> (k + 1)), cols]
            cp = self.links.dp(here, here, peer)
            cur[q] = self.old[q][k]
        self.flying[q] = cp

    def begin(self):
        for q in range(4):
            self.launch(q, 0)

    def advance(self):
        s, n = self.stage, self.n
        if s > 8:
            return
        if s == 4:
            pl.semaphore_wait(self.free, 4)
        for q in range(4):
            cp, cols = self.flying[q], pl.ds(256 * q, 256)
            if s == 4:
                cp.wait_send()
            else:
                self.sent.append(cp)
            cp.wait_recv()
            if s <= 4:
                rows = n >> min(s + 1, 4)
                at = self.base + n - (n >> s)
                here = self.cur[q]
                add_into(
                    self.ref, lambda r, m: (pl.ds(here + r, m), cols),
                    self.recv, lambda r, m: (pl.ds(at + r, m), cols), rows,
                )
            if s < 8:
                self.launch(q, s + 1)
        if s == 3:
            for cp in self.sent:
                cp.wait_send()
            self.sent = []
            for _, peer in self.cube:
                pl.semaphore_signal(self.free, inc=1, device_id=(peer, lax.axis_index("mp")), device_id_type=MESH)
        self.stage += 1

    def finish(self):
        for cp in self.sent:
            cp.wait_send()


class Strips:
    def __init__(self, links, ref, recv, pack, got, free):
        self.links, self.ref, self.recv, self.pack, self.got, self.free = links, ref, recv, pack, got, free
        self.cube, self.zp = dp_places()
        self.cur, self.old = [0] * 4, [[] for _ in range(4)]
        self.flying, self.sent, self.stage = [], [], 0

    def launch(self, s):
        ref, cur = self.ref, self.cur
        self.flying = []
        for j in range(STRIPS):
            q, cols = j % 4, pl.ds(128 * j, 128)
            if s < 4:
                bit, peer = self.cube[(q + s) % 4]
                half = 256 >> (s + 1)
                give = pl.multiple_of(cur[q] + (1 - bit) * half, 16)
                cp = self.links.dp(
                    ref.at[:, pl.ds(give, half), cols], self.recv.at[:, pl.ds(256 - (256 >> s), half), cols], peer
                )
            elif s == 4:
                cp = self.links.dp(ref.at[:, pl.ds(cur[q], 16), cols], self.recv.at[:, pl.ds(240, 16), cols], self.zp)
            else:
                k = 9 - s
                bit, peer = self.cube[(q + k) % 4]
                here = ref.at[:, pl.ds(cur[q], 256 >> (k + 1)), cols]
                cp = self.links.dp(here, here, peer)
            self.flying.append(cp)
        for q in range(4):
            if s < 4:
                bit, _ = self.cube[(q + s) % 4]
                self.old[q].append(cur[q])
                cur[q] = pl.multiple_of(cur[q] + bit * (256 >> (s + 1)), 16)
            elif s > 4:
                cur[q] = self.old[q][9 - s]

    def begin(self):
        self.launch(0)

    def advance(self):
        s = self.stage
        if s > 9:
            return
        mp, zl, core, part, far = mp_places()
        if s == 5:
            for cp in self.flying:
                cp.wait()
            self.got[mp] = self.pack[mp]
            for j in range(STRIPS):
                self.ref[:, pl.ds(self.cur[j % 4], 16), pl.ds(128 * j, 128)] = self.got[:, j]
            pl.semaphore_wait(self.free, 4)
            self.launch(6)
        else:
            for j, cp in enumerate(self.flying):
                cols = pl.ds(128 * j, 128)
                if s == 4:
                    cp.wait_send()
                else:
                    self.sent.append(cp)
                cp.wait_recv()
                if s <= 4:
                    rows, at, here = 256 >> min(s + 1, 4), 256 - (256 >> s), self.cur[j % 4]
                    add_into(
                        self.ref, lambda r, m: (slice(None), pl.ds(here + r, m), cols),
                        self.recv, lambda r, m: (slice(None), pl.ds(at + r, m), cols), rows,
                    )
            if s == 3:
                for cp in self.sent:
                    cp.wait_send()
                self.sent = []
                for _, peer in self.cube:
                    pl.semaphore_signal(self.free, inc=1, device_id=(peer, mp), device_id_type=MESH)
            if s == 4:
                for j in range(STRIPS):
                    self.pack[:, j] = self.ref[:, pl.ds(self.cur[j % 4], 16), pl.ds(128 * j, 128)]
                self.flying = [self.links.mp(self.pack.at[peer], self.got.at[mp], peer) for peer in (part, far, 3 - mp)]
            elif s < 9:
                self.launch(s + 1)
        self.stage += 1

    def finish(self):
        for cp in self.sent:
            cp.wait_send()


class Smalls:
    def __init__(self, links, ref, recv):
        self.links, self.ref, self.recv, self.stage = links, ref, recv, 0
        cube, zp = dp_places()
        self.peers = [peer for _, peer in cube] + [zp]

    def begin(self):
        s = self.stage
        mp, zl, core, part, far = mp_places()
        self.rows = pl.ds(0, 16 if s < 5 else 8)
        src, dst = self.ref.at[self.rows], self.recv.at[s, self.rows]
        if s < 5:
            self.cp = self.links.dp(src, dst, self.peers[s])
        else:
            self.cp = self.links.mp(src, dst, (part, far)[s - 5])

    def advance(self):
        if self.stage > 6:
            return
        self.cp.wait()
        self.ref[self.rows, :] = self.ref[self.rows, :] + self.recv[self.stage, self.rows, :]
        self.stage += 1
        if self.stage <= 6:
            self.begin()

    def finish(self):
        pass


def dg(a, b, left=1, right=0):
    return lax.dot_general(a, b, (((left,), (right,)), ((), ())), preferred_element_type=F32)


def normalize(rows):
    centre = rows - jnp.mean(rows, axis=-1, keepdims=True)
    inv = lax.rsqrt(jnp.mean(centre * centre, axis=-1, keepdims=True) + EPS)
    return centre * inv, inv


def norm_back(grad, gain, unit, inv):
    g = grad * gain
    return inv * (g - jnp.mean(g, axis=-1, keepdims=True) - unit * jnp.mean(g * unit, axis=-1, keepdims=True))


def iota(shape, dim):
    return lax.broadcasted_iota(jnp.int32, shape, dim)


def fold(x, op):
    out = x[:8]
    for i in range(1, x.shape[0] // 8):
        out = op(out, x[8 * i : 8 * i + 8])
    return out


def layer_body(
    seg_in, mem_in, old_in, gout_in, wq_in, wkv_in, wo_in, wup_in, wdn_in, wsq_in,
    mfill, sfill, slopes, again, fgain, ubias,
    lout, sqz_out, gin, x_down, x_up, x_sq, x_out, t_ref, s_ref,
    raw, normed, wkvq, wo, wup, wdn, wsq, kv, query, expo, tmp, tmp2, stat, acc, mixt, mixg, mid, nm, hid, gpre,
    out, got, keep, out2, got2, gb, gmix, gkv, gq, win, sqz, skv, esq, gsq, rec, sbuf, sgot, sqsum, trecv, tpack, tgot, srecv,
    lsem, free, ssem, rsem,
):
    links = Links(ssem, rsem)
    mp, zl, core, part, far = mp_places()
    diag = 3 - mp
    cube, zp = dp_places()
    dp = lax.axis_index("dp")
    mine = pl.ds(pl.multiple_of(mp * 256, 256), 256)

    ins = {SEG: seg_in, MEM: mem_in, OLD: old_in, GOUT: gout_in}
    own_loads = {}
    nlocal = [0]

    def load(src, dst):
        cp = pltpu.make_async_copy(src, dst, lsem.at[nlocal[0]])
        nlocal[0] += 1
        cp.start()
        return cp

    for a in (SEG, MEM, OLD, GOUT):
        own_loads[a] = load(ins[a], raw.at[a, mp])
    w_loads = [
        load(wkv_in.at[:, mine], wkvq.at[:, pl.ds(0, 256)]),
        load(wkv_in.at[:, pl.ds(pl.multiple_of(D + mp * 256, 256), 256)], wkvq.at[:, pl.ds(256, 256)]),
        load(wq_in.at[:, mine], wkvq.at[:, pl.ds(512, 256)]),
    ]
    sq_load = load(wsq_in, wsq)
    late_loads = [load(wo_in, wo), load(wup_in, wup), load(wdn_in, wdn)]

    sem = pltpu.get_barrier_semaphore()
    for peer in [peer for _, peer in cube] + [zp]:
        pl.semaphore_signal(sem, inc=1, device_id=(peer, mp), device_id_type=MESH)
    for peer in (part, far, diag):
        pl.semaphore_signal(sem, inc=1, device_id=(dp, peer), device_id_type=MESH)
    pl.semaphore_wait(sem, 8)

    done = []

    far_cp, part_cp, fwd_cp = {}, {}, {}

    def send_far(a):
        far_cp[a] = links.mp(ins[a], raw.at[a, mp], far)

    send_far(SEG)
    send_far(MEM)
    for a in (SEG, MEM, OLD, GOUT):
        part_cp[a] = links.mp(ins[a], raw.at[a, mp], part)

    def norm_rows(a, owner):
        unit, _ = normalize(raw[a, owner].astype(F32))
        normed[pl.ds(pl.multiple_of(BASE[a] + owner * 128, 128), 128), :] = (unit * again[...]).astype(BF)

    def arrive(a, following=None):
        far_cp[a].wait_recv()
        fwd_cp[a] = links.mp(raw.at[a, far], raw.at[a, far], part)
        done.extend([far_cp[a], fwd_cp[a]])
        if following is not None:
            send_far(following)

    def project(a):
        rows = pl.ds(BASE[a], 512)
        kv[rows, :] = dg(normed[rows, :], wkvq[:, 0:512]).astype(BF)
        if a == SEG:
            query[...] = dg(normed[rows, :], wkvq[:, 512:768]).astype(BF)

    mem_limit = M - mfill[0]
    old_limit = C - sfill[0]

    def slope_of(h):
        return slopes[mp * 2 + h]

    def heads(h):
        return pl.ds(h * DH, DH)

    def column(r, rows):
        return iota((rows, 1), 0) + r

    def exponentials(src, dst, dst0, rows, colmask, causal=False):
        step = 64

        def one(r, top):
            s = src[pl.ds(r, step), :] * SCALE + colmask(r, step)
            if causal:
                s = jnp.where(iota((step, 512), 0) + r <= iota((step, 512), 1), s, NEG)
            src[pl.ds(r, step), :] = s
            return jnp.maximum(top, fold(s, jnp.maximum))

        top = loop(rows, step, one, jnp.full((8, 512), NEG, F32))
        top = jnp.max(top, axis=0, keepdims=True)

        def two(r, total):
            e = jnp.exp(src[pl.ds(r, step), :] - top).astype(BF)
            dst[pl.ds(dst0 + r, step), :] = e
            return total + fold(e.astype(F32), jnp.add)

        total = loop(rows, step, two, jnp.zeros((8, 512), F32))
        return top, jnp.sum(total, axis=0, keepdims=True)

    def attend(h, a):
        base = BASE[a]
        rows = pl.ds(base, 512)
        g = base // 512
        tmp[...] = dg(kv[rows, heads(h)], query[:, heads(h)], 1, 1)
        slope = slope_of(h)

        def colmask(r, step):
            j = column(r, step)
            bias = slope * (j + (base - 1536)).astype(F32)
            if a == MEM:
                bias = jnp.where(j >= mem_limit, bias, NEG)
            if a == OLD:
                bias = jnp.where(j >= old_limit, bias, NEG)
            return bias

        top, total = exponentials(tmp, expo.at[h], base, 512, colmask, a == SEG)
        stat[h * 6 + g : h * 6 + g + 1, :] = top
        stat[h * 6 + 3 + g : h * 6 + 4 + g, :] = total
        acc[h * 3 + g] = dg(kv[rows, pl.ds(256 + h * DH, DH)], expo[h, rows, :], 0, 0)

    def first_of(h):
        rows = pl.ds(BASE[MEM], 512)
        tmp[...] = dg(kv[rows, heads(h)], query[:, heads(h)], 1, 1)
        _, total = exponentials(
            tmp, gkv, 0, 512, lambda r, step: jnp.where(column(r, step) >= mem_limit, 0.0, NEG)
        )
        rec[heads(h), :] = dg(kv[rows, pl.ds(256 + h * DH, DH)], gkv[0:512, :], 0, 0) / total

    for a in (SEG, MEM, OLD):
        own_loads[a].wait()
        norm_rows(a, mp)
    own_loads[GOUT].wait()
    for a in (SEG, MEM, OLD):
        part_cp[a].wait_recv()
        norm_rows(a, part)
    arrive(SEG, OLD)
    norm_rows(SEG, far)
    for cp in w_loads:
        cp.wait()
    fwd_cp[SEG].wait_recv()
    norm_rows(SEG, diag)
    project(SEG)
    attend(0, SEG)
    arrive(MEM, GOUT)
    norm_rows(MEM, far)
    attend(1, SEG)
    fwd_cp[MEM].wait_recv()
    norm_rows(MEM, diag)
    project(MEM)
    for h in range(2):
        attend(h, MEM)

    sq_load.wait()

    def squeeze():
        rows = raw[MEM].reshape(512, D)
        for tap in range(3):
            pick = (iota((CP, 512), 1) == 3 * iota((CP, 512), 0) + tap).astype(BF)
            win[:, tap * D : (tap + 1) * D] = dg(pick, rows).astype(BF)
        for half in range(2):
            cols = pl.ds(half * 512, 512)
            sqz[:, cols] = dg(win[...], wsq[:, cols])

    squeeze()
    for peer in [peer for _, peer in cube] + [zp]:
        pl.semaphore_signal(free.at[0], inc=1, device_id=(peer, mp), device_id_type=MESH)
    arrive(OLD)
    norm_rows(OLD, far)
    sqz_out[...] = sqz[...].astype(BF)
    unit, _ = normalize(sqz[...])
    skv[...] = dg((unit * again[...]).astype(BF), wkvq[:, 0:512]).astype(BF)
    fwd_cp[OLD].wait_recv()
    norm_rows(OLD, diag)
    project(OLD)
    for h in range(2):
        attend(h, OLD)

    for h in range(2):
        tops = [stat[h * 6 + g : h * 6 + g + 1, :] for g in range(3)]
        sums = [stat[h * 6 + 3 + g : h * 6 + 4 + g, :] for g in range(3)]
        top = jnp.maximum(jnp.maximum(tops[0], tops[1]), tops[2])
        scales = [jnp.exp(t - top) for t in tops]
        total = scales[0] * sums[0] + scales[1] * sums[1] + scales[2] * sums[2]
        mixed = jnp.zeros((DH, 512), F32)
        for g in range(3):
            inv = scales[g] / total
            stat[12 + h * 3 + g : 13 + h * 3 + g, :] = inv
            mixed = mixed + acc[h * 3 + g] * inv
        mixt[heads(h), :] = mixed
        mixg[mp, :, heads(h)] = mixed.T.astype(BF)
    mix_far = links.mp(mixg.at[mp], mixg.at[mp], far)
    mix_part = links.mp(mixg.at[mp], mixg.at[mp], part)
    done.extend([mix_far, mix_part])

    for h in range(2):
        first_of(h)
    arrive(GOUT)

    def second_of(h):
        keys, values = skv[:, heads(h)], skv[:, pl.ds(256 + h * DH, DH)]
        tmp[0:CP, :] = dg(keys, query[:, heads(h)], 1, 1)

        def colmask(r, step):
            slot = column(r, step)
            return jnp.where((3 * slot < M) & (3 * slot + 2 >= mem_limit), 0.0, NEG)

        _, total = exponentials(tmp, esq, 0, CP, colmask)
        inv = 1.0 / total
        second = dg(values, esq[...], 0, 0) * inv
        grad = (rec[heads(h), :] - second) * RECON
        inner = inv * jnp.sum(grad * second, axis=0, keepdims=True)
        scaled = (grad * inv).astype(BF)
        gsq[:, pl.ds(256 + h * DH, DH)] = dg(esq[...], scaled, 1, 1).astype(BF)
        gp = dg(values, scaled)
        gs = (esq[...].astype(F32) * (gp - inner)).astype(BF)
        gsq[:, heads(h)] = (dg(gs, query[:, heads(h)]) * SCALE).astype(BF)

    for h in range(2):
        second_of(h)

    def seg_rows():
        return raw[SEG].reshape(512, D).astype(F32)

    def mix_into(owners, first=False):
        for half in range(2):
            cols = pl.ds(half * 512, 512)
            base = raw[SEG, :, :, cols].reshape(512, 512).astype(F32) if first else mid[:, cols]
            for owner in owners:
                base = base + dg(mixg[owner], wo[pl.ds(pl.multiple_of(owner * 256, 256), 256), cols])
            mid[:, cols] = base

    for cp in late_loads:
        cp.wait()
    mix_part.wait_recv()
    mix_into((mp, part), True)
    mix_far.wait_recv()
    mix_fwd = links.mp(mixg.at[far], mixg.at[far], part)
    done.append(mix_fwd)
    unit, inv = normalize(sqz[...])
    sqz[...] = norm_back(dg(gsq[...], wkvq[:, 0:512], 1, 1), again[...], unit, inv)
    sbuf[0] = sqz[pl.ds(pl.multiple_of((1 - core) * 96, 16), 96), :].astype(BF)
    sq_part = links.mp(sbuf.at[0], sgot.at[0], part)
    done.append(sq_part)
    mix_into((far,))
    mix_fwd.wait_recv()
    mix_into((diag,))

    def norm_mid(r):
        unit, _ = normalize(mid[pl.ds(r, 128), :])
        nm[pl.ds(r, 128), :] = (unit * fgain[...]).astype(BF)

    each(512, 128, norm_mid)
    for a in (SEG, MEM, OLD, GOUT):
        done.append(part_cp[a])
    part_cp[GOUT].wait_recv()
    fwd_cp[GOUT].wait_recv()

    def gout_rows():
        return raw[GOUT].reshape(512, D)

    for half in range(2):
        cols = pl.ds(half * 512, 512)
        tmp[...] = dg(nm[...], wup[:, cols])
        tmp2[...] = dg(gout_rows(), wdn[cols, :], 1, 1)

        def gelu(r, total):
            rows = pl.ds(r, 32)
            v = tmp[rows, :] + ubias[:, cols]
            square = v * v
            th = jnp.tanh(0.7978845608028654 * v * (1.0 + 0.044715 * square))
            hid[rows, cols] = (0.5 * v * (1.0 + th)).astype(BF)
            slope = 0.5 * (1.0 + th) + (0.5 * 0.7978845608028654) * v * (1.0 - th * th) * (1.0 + 3 * 0.044715 * square)
            g = (slope * tmp2[rows, :]).astype(BF)
            gpre[rows, cols] = g
            return total + fold(g.astype(F32), jnp.add)

        total = loop(512, 32, gelu, jnp.zeros((8, 512), F32))
        s_ref[8:9, cols] = jnp.sum(total, axis=0, keepdims=True)

    def block(z, other):
        return pl.ds(pl.multiple_of((2 * z + ((1 - core) if other else core)) * 128, 128), 128)

    gnm_part, gnm_far, down_part = [], [], []
    for z in range(2):
        out[0, z] = dg(gpre[block(z, True), :], wup[...], 1, 1).astype(BF)
        gnm_part.append(links.mp(out.at[0, z], got.at[0, z], part))
    for z in range(2):
        keep[0, z] = dg(gpre[block(z, False), :], wup[...], 1, 1)
    for z in range(2):
        gnm_part[z].wait_recv()
        out2[z] = (keep[0, z] + got[0, z].astype(F32)).astype(BF)
        gnm_far.append(links.mp(out2.at[z], got2.at[z], far))
    sq_part.wait_recv()
    sbuf[1] = (sqz[pl.ds(pl.multiple_of(core * 96, 16), 96), :] + sgot[0].astype(F32)).astype(BF)
    sq_far = links.mp(sbuf.at[1], sgot.at[1], far)
    for z in range(2):
        out[1, z] = dg(hid[block(z, True), :], wdn[...]).astype(BF)
        down_part.append(links.mp(out.at[1, z], got.at[1, z], part))
    for half in range(2):
        rows = pl.ds(half * 512, 512)
        for quarter in range(2):
            cols = pl.ds(quarter * 512, 512)
            x_down[rows, cols] = dg(hid[:, rows], raw[GOUT, :, :, cols].reshape(512, 512), 0, 0).astype(BF)
    pl.semaphore_wait(free.at[0], 5)
    sums_down = Quarters(links, x_down, 1024, wsq, 0, free.at[1])
    sums_up = Quarters(links, x_up, 1024, wsq, 1024, free.at[2])
    sums_sq = Quarters(links, x_sq, 768, wsq, 2048, free.at[3])
    sums_down.begin()
    for z in range(2):
        keep[1, z] = dg(hid[block(z, False), :], wdn[...])
    for z in range(2):
        down_part[z].wait_recv()
    out2[2] = (keep[1, 1 - zl] + got[1, 1 - zl].astype(F32)).astype(BF)
    down_far = links.mp(out2.at[2], got2.at[2], far)
    for half in range(2):
        rows = pl.ds(half * 512, 512)
        for quarter in range(2):
            cols = pl.ds(quarter * 512, 512)
            x_up[rows, cols] = dg(nm[:, rows], gpre[:, cols], 0, 0).astype(BF)
    sums_up.begin()
    sq_far.wait()
    sqsum[core] = (sbuf[1].astype(F32) + sgot[1].astype(F32)).astype(BF)
    sq_back = links.mp(sqsum.at[core], sqsum.at[core], part)

    gb_cp = []
    gain_total = jnp.zeros((1, D), F32)
    for z in range(2):
        gnm_far[z].wait()
        rows = block(z, False)
        unit, inv = normalize(mid[rows, :])
        g = out2[z].astype(F32) + got2[z].astype(F32)
        gain_total = gain_total + jnp.sum(g * unit, axis=0, keepdims=True) * jnp.where(zl == z, 1.0, 0.0)
        gmid = raw[GOUT, 2 * z + core].astype(F32) + norm_back(g, fgain[...], unit, inv)
        keep[0, z] = gmid
        gb[z, core] = gmid.astype(BF)
        gb_cp.append(links.mp(gb.at[z, core], gb.at[z, core], part))
    s_ref[1:2, :] = gain_total
    sq_back.wait()
    for half in range(2):
        cols = pl.ds(half * 512, 512)
        x_sq[:, cols] = dg(win[:, pl.ds(pl.multiple_of(mp * 768, 256), 768)], sqsum[:, :, cols].reshape(CP, 512), 0, 0).astype(BF)
    sums_sq.begin()
    for cp in gb_cp:
        cp.wait()

    gmix[...] = dg(wo[mine, :], gb[...].reshape(512, D), 1, 1)
    for half in range(2):
        cols = pl.ds(half * 512, 512)
        x_out[:, cols] = dg(mixg[mp], gb[:, :, :, cols].reshape(512, 512), 0, 0).astype(BF)
    sums_out = Quarters(links, x_out, 256, wsq, 2816, free.at[4])
    sums_out.begin()
    slope_row = jnp.zeros((1, D), F32)
    for h in range(2):
        grad = gmix[heads(h), :]
        inner = jnp.sum(grad * mixt[heads(h), :], axis=0, keepdims=True)
        slope_acc = jnp.zeros((8, 512), F32)
        gqt = jnp.zeros((DH, 512), F32)
        for a in (OLD, MEM, SEG):
            base = BASE[a]
            rows = pl.ds(base, 512)
            inv = stat[12 + h * 3 + base // 512 : 13 + h * 3 + base // 512, :]
            scaled = (grad * inv).astype(BF)
            shift = inv * inner
            tmp[...] = dg(kv[rows, pl.ds(256 + h * DH, DH)], scaled)
            gkv[rows, pl.ds(256 + h * DH, DH)] = dg(expo[h, rows, :], scaled, 1, 1).astype(BF)

            def score_grads(r, total):
                at = pl.ds(base + r, 64)
                gs = (expo[h, at, :].astype(F32) * (tmp[pl.ds(r, 64), :] - shift)).astype(BF)
                expo[h, at, :] = gs
                dist = (iota((64, 512), 1) - iota((64, 512), 0) + (1024 - base - r)).astype(F32)
                return total + fold(gs.astype(F32) * dist, jnp.add)

            slope_acc = loop(512, 64, score_grads, slope_acc)
            gkv[rows, heads(h)] = (dg(expo[h, rows, :], query[:, heads(h)]) * SCALE).astype(BF)
            gqt = gqt + dg(kv[rows, heads(h)], expo[h, rows, :], 0, 0)
        gq[:, heads(h)] = (gqt * SCALE).T.astype(BF)
        value = -jnp.sum(jnp.sum(slope_acc, axis=0, keepdims=True), axis=1, keepdims=True)
        slope_row = slope_row + jnp.where(iota((1, D), 1) == mp * 2 + h, value, 0.0)
        sums_down.advance()
        sums_up.advance()
    s_ref[2:3, :] = slope_row
    s_ref[3:8, :] = jnp.zeros((5, D), F32)
    s_ref[9:16, :] = jnp.zeros((7, D), F32)

    for b in range(4):
        feats = pl.ds(b * 256, 256)
        big = dg(normed[:, feats], gkv[...], 0, 0)
        small = dg(normed[1024:1536, feats], gq[...], 0, 0)
        t_ref[b, :, 0:512] = big.astype(BF)
        t_ref[b, :, 512:768] = small.astype(BF)
        terms = small[:, 0:128] * wkvq[feats, 512:640].astype(F32) + small[:, 128:256] * wkvq[feats, 640:768].astype(F32)
        for j in range(4):
            terms = terms + big[:, j * 128 : (j + 1) * 128] * wkvq[feats, j * 128 : (j + 1) * 128].astype(F32)
        s_ref[0:1, feats] = jnp.sum(terms.T, axis=0, keepdims=True) / again[:, feats]
    sums_t = Strips(links, t_ref, trecv, tpack, tgot, free.at[5])
    sums_t.begin()
    sums_s = Smalls(links, s_ref, srecv)
    sums_s.begin()

    def seg_terms(z, other):
        rows = block(z, other)
        at = pl.ds(pl.multiple_of(BASE[SEG] + (2 * z + ((1 - core) if other else core)) * 128, 128), 128)
        return dg(gkv[at, :], wkvq[:, 0:512], 1, 1) + dg(gq[rows, :], wkvq[:, 512:768], 1, 1)

    for cp in gnm_part:
        cp.wait_send()
    for cp in down_part:
        cp.wait_send()
    seg_part = []
    for z in range(2):
        out[0, z] = seg_terms(z, True).astype(BF)
        seg_part.append(links.mp(out.at[0, z], got.at[0, z], part))
    down_far.wait()
    lout[...] = (
        mid[pl.ds(pl.multiple_of(mp * 128, 128), 128), :]
        + keep[1, zl] + got[1, zl].astype(F32) + got2[2].astype(F32)
    ).astype(BF)
    for z in range(2):
        keep[1, z] = seg_terms(z, False)
    for cp in seg_part:
        cp.wait_recv()
    out2[3] = (keep[1, 1 - zl] + got[0, 1 - zl].astype(F32)).astype(BF)
    seg_far = links.mp(out2.at[3], got2.at[3], far)
    done.extend(seg_part)

    for sums in (sums_sq, sums_down, sums_up, sums_out, sums_t, sums_s):
        sums.advance()
    seg_far.wait()
    unit, inv = normalize(raw[SEG, mp].astype(F32))
    total = keep[1, zl] + got[0, zl].astype(F32) + got2[3].astype(F32)
    gin[...] = keep[0, zl] + norm_back(total, again[...], unit, inv)
    everything = (sums_sq, sums_down, sums_up, sums_out, sums_t, sums_s)
    for _ in range(10):
        for sums in everything:
            sums.advance()
    for sums in everything:
        sums.finish()
    for cp in done:
        cp.wait_send()


def layer(args):
    def out_shape(shape, dtype):
        return jax.ShapeDtypeStruct(shape, dtype)

    outs = (
        out_shape((128, D), BF), out_shape((CP, D), BF), out_shape((128, D), F32), out_shape((1024, D), BF),
        out_shape((1024, D), BF), out_shape((768, D), BF), out_shape((256, D), BF), out_shape((4, 256, 768), BF),
        out_shape((16, D), F32),
    )
    v = pltpu.VMEM
    scratch = [
        v((4, 4, 128, D), BF), v((1536, D), BF), v((D, 768), BF), v((D, D), BF), v((D, D), BF), v((D, D), BF),
        v((3072, D), BF), v((1536, 512), BF), v((512, 256), BF), v((2, 1536, 512), BF), v((512, 512), F32),
        v((512, 512), F32), v((24, 512), F32), v((6, DH, 512), F32), v((256, 512), F32), v((4, 512, 256), BF),
        v((512, D), F32), v((512, D), BF), v((512, D), BF), v((512, D), BF),
        v((2, 2, 128, D), BF), v((2, 2, 128, D), BF), v((2, 2, 128, D), F32), v((4, 128, D), BF), v((4, 128, D), BF),
        v((2, 2, 128, D), BF), v((256, 512), F32), v((1536, 512), BF), v((512, 256), BF),
        v((CP, 3 * D), BF), v((CP, D), F32), v((CP, 512), BF), v((CP, 512), BF), v((CP, 512), BF), v((256, 512), F32),
        v((2, 96, D), BF), v((2, 96, D), BF), v((2, 96, D), BF),
        v((4, 256, 768), BF), v((4, STRIPS, 16, 128), BF), v((4, STRIPS, 16, 128), BF), v((7, 16, D), F32),
        pltpu.SemaphoreType.DMA((16,)), pltpu.SemaphoreType.REGULAR((8,)),
        pltpu.SemaphoreType.DMA((COPIES,)), pltpu.SemaphoreType.DMA((COPIES,)),
    ]
    return pl.pallas_call(
        layer_body,
        out_shape=outs,
        in_specs=[ANY] * 10 + [SMEM] * 3 + [VMEM] * 3,
        out_specs=tuple(VMEM for _ in outs),
        scratch_shapes=scratch,
        compiler_params=pltpu.CompilerParams(collective_id=0, has_side_effects=True, vmem_limit_bytes=62 << 20),
    )(*args)


def per_device(
    layer_in, memory, squeezed_mem, memory_fill, squeezed_fill, grad_out, attn_gain, w_query, w_keyval,
    w_output, slopes, ffn_gain, w_up, up_bias, w_down, w_squeeze,
):
    mp = lax.axis_index("mp")
    lout, sqz, gin, down, up, sq, gout, t, s = layer((
        layer_in[0], memory[0], squeezed_mem[0], grad_out[0], w_query, w_keyval, w_output, w_up, w_down, w_squeeze,
        memory_fill, squeezed_fill, slopes, attn_gain[None], ffn_gain[None], up_bias[None],
    ))
    t = t.astype(F32).transpose(1, 0, 2)
    return (
        lout[None],
        lax.dynamic_slice_in_dim(sqz, mp * 43, 43, 0)[None],
        gin[None],
        s[0],
        t[:, :, 512:].reshape(256, D),
        jnp.concatenate([t[:, :, :256].reshape(256, D), t[:, :, 256:512].reshape(256, D)], axis=1),
        gout.astype(F32),
        s[2, :8],
        s[1],
        up.astype(F32),
        s[8],
        down.astype(F32),
        sq.astype(F32),
    )


def solution(mesh):
    rows = P("dp", "mp", None)
    in_specs = (
        rows, rows, rows, P("dp"), P("dp"), rows, P(), P(), P(), P(), P(), P(), P(None, "mp"), P("mp"), P("mp", None), P(),
    )
    out_specs = (
        rows, rows, rows, P(), P("mp", None), P("mp", None), P("mp", None), P(), P(), P(None, "mp"), P("mp"), P("mp", None), P("mp", None),
    )
    return jax.shard_map(per_device, mesh=mesh, in_specs=in_specs, out_specs=out_specs, check_vma=False)
```

time: 1010 us -> 192 us (0.19)
  waiting for transfers between devices: 605 us -> 0 us
  Pallas kernels: 0 us -> 162 us
  blocking collectives: 147 us -> 0 us
  local copies, waits for them, and re-layouts: 100 us -> 12.1 us
  matrix products: 87.2 us -> 0 us
  other arithmetic: 35.8 us -> 13.2 us
  between operations: 17.2 us -> 2.43 us
    psum x1 -> x0, waiting for transfers between devices: 282 us -> none  [per_device(): lax.psum(grad_query.astype(jnp.bfloat16), 'dp').astype(jnp.float32)]
    reduce_scatter x6 -> x0, waiting for transfers between devices: 196 us -> none  [the longest x1 66.1 us: per_device(): lax.psum_scatter(summed[3].astype(jnp.bfloat16), 'mp', scatter_dimension=...]
    pallas_call x0 -> x1, Pallas kernels: none -> 162 us  [layer(): pl.pallas_call(layer_body, out_shape=outs, in_specs=[ANY] * 10 + [SMEM] *...]
    all_gather x5 -> x0, waiting for transfers between devices: 123 us -> none  [the longest x1 29.2 us: per_device(): lax.all_gather(own_kv[:, seg_start:], 'mp', axis=1, tiled=True)]
    psum x2 -> x0, blocking collectives: 111 us -> none  [the longest x1 98.1 us: per_device(): lax.psum(grad_attn_gain.astype(jnp.bfloat16), 'dp').astype(jnp.float32)]
    dot_general x31 -> x0, matrix products: 83.8 us -> none  [the longest x2 7.18 us: soft_backward(): jnp.einsum('bihd,bjhd->bhij', grad_heads, split_heads(keyval[:, :, width:...]
    unnamed x121 -> x14, local copies, waits for them, and re-layouts: 83.5 us -> 4.64 us
    unnamed x1 -> x0, blocking collectives: 20.9 us -> none
  transfers between devices with their start and end apart: 17 -> 0, of which waited for: 13 -> 0; matrix products, arithmetic and copies ran while one was open for 14% -> 0% of each run, Pallas kernels for 0% -> 0%
where the time goes in v2:
time: 192 us; the launch traced here: 189 us
  Pallas kernels  162 us (84%)
  other arithmetic  13.2 us (7%)
  local copies, waits for them, and re-layouts  12.1 us (6%)
  between operations  2.43 us (1%)
    pallas_call x1, Pallas kernels, layer(): pl.pallas_call(layer_body, out_shape=outs, in_specs=[ANY] * 10 + [SMEM] *...  162 us
    unnamed x14, local copies, waits for them, and re-layouts  4.64 us
    convert_element_type x1, other arithmetic, per_device(): up.astype(F32)  4.22 us

profile of v2, /device:TPU:0, one launch (start us, length us, event | category | flops | bytes accessed | tf_op | source)
XLA Modules:
  0.0 189.2 jit_solution(3539354436620307041)
XLA Ops:
  1.9 161.5 %shard_map.255 = (bf16[128,1024]{1,0:T(8,128)(2,1)}, bf16[192,1024]{1,0:T(8,128)(2,1)}, f32[128,1024]{1,0:T(8,128)}, bf16[1024,1024]{1,0:T(8,128)(2,1)}, bf16[10...) custom-call(bf16[128,1024]{1,0:T(8,128)(2,1)} %bitcast.25, ...), custom_call_target="tpu_custom_call" | custom-call | tf_op jit(solution)/shard_map/pallas_call | solution.py:781
  163.5 1.7 convert_bitcast_fusion
  165.2 0.3 fusion
  165.5 1.3 copy.30
  166.8 1.3 copy.31
  168.1 1.7 pad_maximum_fusion
  169.8 1.8 copy.33
  171.6 1.6 dynamic-slice_bitcast_fusion
  173.2 1.4 fusion.1
  174.6 0.3 copy.29
  174.9 1.3 copy.32
  176.3 1.2 slice_bitcast_fusion
  177.4 0.0 copy-start
  177.5 4.2 %convert_element_type.14 = f32[1024,1024]{1,0:T(8,128)} convert(bf16[1024,1024]{1,0:T(8,128)(2,1)} %get-tuple-element.28) | non-fusion elementwise | flops 1048576 | bytes 6291456 | tf_op jit(solution)/shard_map/convert_element_type | solution.py:811
  181.7 0.0 copy-done
  181.7 0.0 copy-start.1
  181.7 2.5 %convert_element_type.15 = f32[1024,1024]{1,0:T(8,128)} convert(bf16[1024,1024]{1,0:T(8,128)(2,1)S(1)} %copy-done) | non-fusion elementwise | flops 1048576 | bytes 6291456 | tf_op jit(solution)/shard_map/convert_element_type | solution.py:813
  184.2 0.0 copy-done.1
  184.2 0.0 copy-start.2
  184.2 0.0 copy-start.4
  184.2 2.1 %convert_element_type.16 = f32[768,1024]{1,0:T(8,128)} convert(bf16[768,1024]{1,0:T(8,128)(2,1)S(1)} %copy-done.1) | non-fusion elementwise | flops 786432 | bytes 4718592 | tf_op jit(solution)/shard_map/convert_element_type | solution.py:814
  186.2 0.0 copy-start.3
  186.2 0.0 copy-done.2
  186.2 1.1 convert_element_type.13
  187.3 0.0 copy-done.4
  187.3 0.7 copy.38
  188.0 0.0 copy-done.3
  188.0 0.8 copy.39
Async XLA Ops:
  177.4 4.2 %copy-start = (bf16[1024,1024]{1,0:T(8,128)(2,1)S(1)}, bf16[1024,1024]{1,0:T(8,128)(2,1)}, u32[]{:S(2)}) copy-start(bf16[1024,1024]{1,0:T(8,128)(2,1)} %get-tuple-element.29) | copy-start | bytes 6291460
  181.7 2.5 %copy-start.1 = (bf16[768,1024]{1,0:T(8,128)(2,1)S(1)}, bf16[768,1024]{1,0:T(8,128)(2,1)}, u32[]{:S(2)}) copy-start(bf16[768,1024]{1,0:T(8,128)(2,1)} %get-tuple-element.30) | copy-start | bytes 4718596
  184.2 2.1 %copy-start.2 = (bf16[256,1024]{1,0:T(8,128)(2,1)S(1)}, bf16[256,1024]{1,0:T(8,128)(2,1)}, u32[]{:S(2)}) copy-start(bf16[256,1024]{1,0:T(8,128)(2,1)} %get-tuple-element.27) | copy-start | bytes 1572868
  184.2 3.1 %copy-start.4 = (bf16[128,1024]{1,0:T(8,128)(2,1)S(1)}, bf16[128,1024]{1,0:T(8,128)(2,1)}, u32[]{:S(2)}) copy-start(bf16[128,1024]{1,0:T(8,128)(2,1)} %get-tuple-element.22) | copy-start | bytes 786436
  186.2 1.8 copy-start.3

commit v3 on v2

--- a/solution.py
+++ b/solution.py
@@ -28,7 +28,8 @@
 STRIPS = 6
 SEG, MEM, OLD, GOUT = 0, 1, 2, 3
 BASE = {OLD: 0, MEM: 512, SEG: 1024}
-COPIES = 420
+SENDS = 72
+RECVS = 160
 
 
 def dp_places():
@@ -51,25 +52,47 @@
     return mp, zl, core, zl * 2 + (1 - core), (1 - zl) * 2 + core
 
 
+class Flight:
+    def __init__(self, links, cp, send, recv):
+        self.links, self.cp, self.send, self.recv = links, cp, send, recv
+
+    def wait_send(self):
+        self.cp.wait_send()
+        self.links.spare.append(self.send)
+
+    def wait_recv(self):
+        self.cp.wait_recv()
+
+    def wait(self):
+        self.wait_send()
+        self.wait_recv()
+
+
 class Links:
     def __init__(self, ssem, rsem):
-        self.ssem, self.rsem, self.count = ssem, rsem, 0
-
-    def start(self, src, dst, place):
-        k = self.count
-        self.count += 1
+        self.ssem, self.rsem, self.spare, self.sends, self.recvs = ssem, rsem, [], 0, 0
+
+    def start(self, src, dst, place, like=None):
+        if self.spare:
+            k = self.spare.pop(0)
+        else:
+            k, self.sends = self.sends, self.sends + 1
+        if like is not None:
+            r = like.recv
+        else:
+            r, self.recvs = self.recvs, self.recvs + 1
         cp = pltpu.make_async_remote_copy(
-            src_ref=src, dst_ref=dst, send_sem=self.ssem.at[k], recv_sem=self.rsem.at[k],
+            src_ref=src, dst_ref=dst, send_sem=self.ssem.at[k], recv_sem=self.rsem.at[r],
             device_id=place, device_id_type=MESH,
         )
         cp.start()
-        return cp
+        return Flight(self, cp, k, r)
 
     def mp(self, src, dst, peer):
         return self.start(src, dst, (lax.axis_index("dp"), peer))
 
-    def dp(self, src, dst, peer):
-        return self.start(src, dst, (peer, lax.axis_index("mp")))
+    def dp(self, src, dst, peer, like=None):
+        return self.start(src, dst, (peer, lax.axis_index("mp")), like)
 
 
 def loop(total, step, body, init=None):
@@ -92,23 +115,26 @@
 
     def body(r):
         to, at = dst_at(r, step), src_at(r, step)
-        dst[to] = (dst[to].astype(F32) + src[at].astype(F32)).astype(BF)
+        dst[to] = dst[to] + src[at]
 
     each(rows, step, body)
 
 
 class Quarters:
-    def __init__(self, links, ref, n, recv, base, free):
+    last = 8
+
+    def __init__(self, links, ref, n, recv, base, free, order=(0, 1, 2, 3)):
         self.links, self.ref, self.n, self.recv, self.base, self.free = links, ref, n, recv, base, free
+        self.order = order
         self.cube, self.zp = dp_places()
         self.cur, self.old = [0] * 4, [[] for _ in range(4)]
-        self.flying, self.sent, self.stage = [None] * 4, [], 0
+        self.flying, self.sent, self.stage, self.out = [None] * 4, [], 0, [[] for _ in range(4)]
 
     def launch(self, q, s):
         cols = pl.ds(256 * q, 256)
         n, cur = self.n, self.cur
         if s < 4:
-            bit, peer = self.cube[(q + s) % 4]
+            bit, peer = self.cube[(self.order[q] + s) % 4]
             half = n >> (s + 1)
             give = pl.multiple_of(cur[q] + (1 - bit) * half, 16)
             self.old[q].append(cur[q])
@@ -123,10 +149,11 @@
             )
         else:
             k = 8 - s
-            bit, peer = self.cube[(q + k) % 4]
+            bit, peer = self.cube[(self.order[q] + k) % 4]
             here = self.ref.at[pl.ds(cur[q], n >> (k + 1)), cols]
-            cp = self.links.dp(here, here, peer)
+            cp = self.links.dp(here, here, peer, self.out[q][k])
             cur[q] = self.old[q][k]
+        self.out[q].append(cp)
         self.flying[q] = cp
 
     def begin(self):
@@ -139,6 +166,7 @@
             return
         if s == 4:
             pl.semaphore_wait(self.free, 4)
+        earlier, self.sent = self.sent, []
         for q in range(4):
             cp, cols = self.flying[q], pl.ds(256 * q, 256)
             if s == 4:
@@ -156,6 +184,8 @@
                 )
             if s < 8:
                 self.launch(q, s + 1)
+        for cp in earlier:
+            cp.wait_send()
         if s == 3:
             for cp in self.sent:
                 cp.wait_send()
@@ -170,11 +200,13 @@
 
 
 class Strips:
+    last = 9
+
     def __init__(self, links, ref, recv, pack, got, free):
         self.links, self.ref, self.recv, self.pack, self.got, self.free = links, ref, recv, pack, got, free
         self.cube, self.zp = dp_places()
         self.cur, self.old = [0] * 4, [[] for _ in range(4)]
-        self.flying, self.sent, self.stage = [], [], 0
+        self.flying, self.sent, self.stage, self.out = [], [], 0, []
 
     def launch(self, s):
         ref, cur = self.ref, self.cur
@@ -194,8 +226,9 @@
                 k = 9 - s
                 bit, peer = self.cube[(q + k) % 4]
                 here = ref.at[:, pl.ds(cur[q], 256 >> (k + 1)), cols]
-                cp = self.links.dp(here, here, peer)
+                cp = self.links.dp(here, here, peer, self.out[k][j])
             self.flying.append(cp)
+        self.out.append(self.flying)
         for q in range(4):
             if s < 4:
                 bit, _ = self.cube[(q + s) % 4]
@@ -212,6 +245,7 @@
         if s > 9:
             return
         mp, zl, core, part, far = mp_places()
+        earlier, self.sent = self.sent, []
         if s == 5:
             for cp in self.flying:
                 cp.wait()
@@ -246,6 +280,8 @@
                 self.flying = [self.links.mp(self.pack.at[peer], self.got.at[mp], peer) for peer in (part, far, 3 - mp)]
             elif s < 9:
                 self.launch(s + 1)
+        for cp in earlier:
+            cp.wait_send()
         self.stage += 1
 
     def finish(self):
@@ -254,6 +290,8 @@
 
 
 class Smalls:
+    last = 6
+
     def __init__(self, links, ref, recv):
         self.links, self.ref, self.recv, self.stage = links, ref, recv, 0
         cube, zp = dp_places()
@@ -311,10 +349,10 @@
 def layer_body(
     seg_in, mem_in, old_in, gout_in, wq_in, wkv_in, wo_in, wup_in, wdn_in, wsq_in,
     mfill, sfill, slopes, again, fgain, ubias,
-    lout, sqz_out, gin, x_down, x_up, x_sq, x_out, t_ref, s_ref,
+    lout, sqz_out, gin, down_out, up_out, sq_out, out_out, t_out, s_ref,
     raw, normed, wkvq, wo, wup, wdn, wsq, kv, query, expo, tmp, tmp2, stat, acc, mixt, mixg, mid, nm, hid, gpre,
     out, got, keep, out2, got2, gb, gmix, gkv, gq, win, sqz, skv, esq, gsq, rec, sbuf, sgot, sqsum, trecv, tpack, tgot, srecv,
-    lsem, free, ssem, rsem,
+    x_down, x_up, x_sq, x_out, t_ref, lsem, free, ssem, rsem,
 ):
     links = Links(ssem, rsem)
     mp, zl, core, part, far = mp_places()
@@ -340,8 +378,6 @@
         load(wkv_in.at[:, pl.ds(pl.multiple_of(D + mp * 256, 256), 256)], wkvq.at[:, pl.ds(256, 256)]),
         load(wq_in.at[:, mine], wkvq.at[:, pl.ds(512, 256)]),
     ]
-    sq_load = load(wsq_in, wsq)
-    late_loads = [load(wo_in, wo), load(wup_in, wup), load(wdn_in, wdn)]
 
     sem = pltpu.get_barrier_semaphore()
     for peer in [peer for _, peer in cube] + [zp]:
@@ -354,24 +390,33 @@
 
     far_cp, part_cp, fwd_cp = {}, {}, {}
 
-    def send_far(a):
-        far_cp[a] = links.mp(ins[a], raw.at[a, mp], far)
-
-    send_far(SEG)
-    send_far(MEM)
+    queue = [(a, i) for a in (SEG, MEM, OLD, GOUT) for i in range(2)]
+
+    def send_far():
+        a, i = queue[len(far_cp)]
+        rows = pl.ds(64 * i, 64)
+        far_cp[a, i] = links.mp(ins[a].at[rows], raw.at[a, mp, rows], far)
+
+    def pump():
+        far_cp[queue[len(far_cp) - 2]].wait_send()
+        send_far()
+
+    send_far()
+    send_far()
     for a in (SEG, MEM, OLD, GOUT):
         part_cp[a] = links.mp(ins[a], raw.at[a, mp], part)
+    sq_load = load(wsq_in, wsq)
+    late_loads = [load(wo_in, wo), load(wup_in, wup), load(wdn_in, wdn)]
 
     def norm_rows(a, owner):
         unit, _ = normalize(raw[a, owner].astype(F32))
         normed[pl.ds(pl.multiple_of(BASE[a] + owner * 128, 128), 128), :] = (unit * again[...]).astype(BF)
 
-    def arrive(a, following=None):
-        far_cp[a].wait_recv()
+    def arrive(a):
+        far_cp[a, 0].wait_recv()
+        far_cp[a, 1].wait_recv()
         fwd_cp[a] = links.mp(raw.at[a, far], raw.at[a, far], part)
-        done.extend([far_cp[a], fwd_cp[a]])
-        if following is not None:
-            send_far(following)
+        done.append(fwd_cp[a])
 
     def project(a):
         rows = pl.ds(BASE[a], 512)
@@ -448,47 +493,37 @@
     for a in (SEG, MEM, OLD):
         part_cp[a].wait_recv()
         norm_rows(a, part)
-    arrive(SEG, OLD)
-    norm_rows(SEG, far)
+    pump()
     for cp in w_loads:
         cp.wait()
+    pump()
+    arrive(SEG)
+    norm_rows(SEG, far)
     fwd_cp[SEG].wait_recv()
     norm_rows(SEG, diag)
+    pump()
     project(SEG)
+    pump()
+    arrive(MEM)
+    norm_rows(MEM, far)
     attend(0, SEG)
-    arrive(MEM, GOUT)
-    norm_rows(MEM, far)
-    attend(1, SEG)
     fwd_cp[MEM].wait_recv()
     norm_rows(MEM, diag)
+    pump()
     project(MEM)
-    for h in range(2):
-        attend(h, MEM)
-
-    sq_load.wait()
-
-    def squeeze():
-        rows = raw[MEM].reshape(512, D)
-        for tap in range(3):
-            pick = (iota((CP, 512), 1) == 3 * iota((CP, 512), 0) + tap).astype(BF)
-            win[:, tap * D : (tap + 1) * D] = dg(pick, rows).astype(BF)
-        for half in range(2):
-            cols = pl.ds(half * 512, 512)
-            sqz[:, cols] = dg(win[...], wsq[:, cols])
-
-    squeeze()
-    for peer in [peer for _, peer in cube] + [zp]:
-        pl.semaphore_signal(free.at[0], inc=1, device_id=(peer, mp), device_id_type=MESH)
+    attend(1, SEG)
+    pump()
     arrive(OLD)
     norm_rows(OLD, far)
-    sqz_out[...] = sqz[...].astype(BF)
-    unit, _ = normalize(sqz[...])
-    skv[...] = dg((unit * again[...]).astype(BF), wkvq[:, 0:512]).astype(BF)
+    attend(0, MEM)
     fwd_cp[OLD].wait_recv()
     norm_rows(OLD, diag)
     project(OLD)
+    attend(1, MEM)
     for h in range(2):
         attend(h, OLD)
+    far_cp[GOUT, 0].wait_send()
+    done.append(far_cp[GOUT, 1])
 
     for h in range(2):
         tops = [stat[h * 6 + g : h * 6 + g + 1, :] for g in range(3)]
@@ -503,13 +538,136 @@
             mixed = mixed + acc[h * 3 + g] * inv
         mixt[heads(h), :] = mixed
         mixg[mp, :, heads(h)] = mixed.T.astype(BF)
-    mix_far = links.mp(mixg.at[mp], mixg.at[mp], far)
-    mix_part = links.mp(mixg.at[mp], mixg.at[mp], part)
-    done.extend([mix_far, mix_part])
-
-    for h in range(2):
-        first_of(h)
+    mix_far, mix_part, mix_fwd = [], [], []
+
+    def half_rows(z):
+        return pl.ds(z * 256, 256)
+
+    for z in range(2):
+        here = mixg.at[mp, half_rows(z)]
+        mix_far.append(links.mp(here, here, far))
+        mix_part.append(links.mp(here, here, part))
+    done.extend(mix_far + mix_part)
+
+    sq_load.wait()
+
+    def squeeze():
+        rows = raw[MEM].reshape(512, D)
+        for tap in range(3):
+            pick = (iota((CP, 512), 1) == 3 * iota((CP, 512), 0) + tap).astype(BF)
+            win[:, tap * D : (tap + 1) * D] = dg(pick, rows).astype(BF)
+        for half in range(2):
+            cols = pl.ds(half * 512, 512)
+            sqz[:, cols] = dg(win[...], wsq[:, cols])
+
+    squeeze()
+    for peer in [peer for _, peer in cube] + [zp]:
+        pl.semaphore_signal(free.at[0], inc=1, device_id=(peer, mp), device_id_type=MESH)
     arrive(GOUT)
+
+    def seg_rows():
+        return raw[SEG].reshape(512, D).astype(F32)
+
+    def mix_into(z, owners, first=False):
+        rows = half_rows(z)
+        for half in range(2):
+            cols = pl.ds(half * 512, 512)
+            base = raw[SEG, 2 * z : 2 * z + 2, :, cols].reshape(256, 512).astype(F32) if first else mid[rows, cols]
+            for owner in owners:
+                base = base + dg(mixg[owner, rows, :], wo[pl.ds(pl.multiple_of(owner * 256, 256), 256), cols])
+            mid[rows, cols] = base
+
+    for cp in late_loads:
+        cp.wait()
+    for a in (SEG, MEM, OLD, GOUT):
+        done.append(part_cp[a])
+    part_cp[GOUT].wait_recv()
+    fwd_cp[GOUT].wait_recv()
+
+    def norm_mid(r):
+        unit, _ = normalize(mid[pl.ds(r, 128), :])
+        nm[pl.ds(r, 128), :] = (unit * fgain[...]).astype(BF)
+
+    def forward_mix(z):
+        mix_far[z].wait_recv()
+        here = mixg.at[far, half_rows(z)]
+        mix_fwd.append(links.mp(here, here, part))
+        done.append(mix_fwd[z])
+
+    for z in range(2):
+        mix_part[z].wait_recv()
+        mix_into(z, (mp, part), True)
+    forward_mix(0)
+    mix_into(0, (far,))
+    bias_total = [jnp.zeros((8, 512), F32), jnp.zeros((8, 512), F32)]
+    for z in range(2):
+        if z == 1:
+            forward_mix(1)
+            mix_into(1, (far,))
+        mix_fwd[z].wait_recv()
+        mix_into(z, (diag,))
+        rows = half_rows(z)
+        norm_mid(z * 256)
+        norm_mid(z * 256 + 128)
+        for half in range(2):
+            cols = pl.ds(half * 512, 512)
+            tmp[half_rows(half), :] = dg(nm[rows, :], wup[:, cols])
+            tmp2[half_rows(half), :] = dg(raw[GOUT, 2 * z : 2 * z + 2].reshape(256, D), wdn[cols, :], 1, 1)
+        for half in range(2):
+            cols = pl.ds(half * 512, 512)
+
+            def gelu(r, total):
+                at = pl.ds(r + half * 256, 32)
+                to = pl.ds(r + z * 256, 32)
+                v = tmp[at, :] + ubias[:, cols]
+                square = v * v
+                th = jnp.tanh(0.7978845608028654 * v * (1.0 + 0.044715 * square))
+                hid[to, cols] = (0.5 * v * (1.0 + th)).astype(BF)
+                slope = 0.5 * (1.0 + th) + (0.5 * 0.7978845608028654) * v * (1.0 - th * th) * (1.0 + 3 * 0.044715 * square)
+                g = (slope * tmp2[at, :]).astype(BF)
+                gpre[to, cols] = g
+                return total + fold(g.astype(F32), jnp.add)
+
+            bias_total[half] = loop(256, 32, gelu, bias_total[half])
+    for half in range(2):
+        s_ref[8:9, pl.ds(half * 512, 512)] = jnp.sum(bias_total[half], axis=0, keepdims=True)
+
+    def block(z, other):
+        return pl.ds(pl.multiple_of((2 * z + ((1 - core) if other else core)) * 128, 128), 128)
+
+    pl.semaphore_wait(free.at[0], 5)
+    sums_down = Quarters(links, x_down, 1024, wsq, 0, free.at[1])
+    sums_up = Quarters(links, x_up, 1024, wsq, 1024, free.at[2])
+    sums_sq = Quarters(links, x_sq, 768, wsq, 2048, free.at[3])
+    for half in range(2):
+        rows = pl.ds(half * 512, 512)
+        for quarter in range(2):
+            cols = pl.ds(quarter * 512, 512)
+            x_down[rows, cols] = dg(hid[:, rows], raw[GOUT, :, :, cols].reshape(512, 512), 0, 0).astype(BF)
+    sums_down.begin()
+    gnm_part, gnm_far, down_part = [], [], []
+    for z in range(2):
+        out[0, z] = dg(gpre[block(z, True), :], wup[...], 1, 1).astype(BF)
+        gnm_part.append(links.mp(out.at[0, z], got.at[0, z], part))
+    for half in range(2):
+        rows = pl.ds(half * 512, 512)
+        for quarter in range(2):
+            cols = pl.ds(quarter * 512, 512)
+            x_up[rows, cols] = dg(nm[:, rows], gpre[:, cols], 0, 0).astype(BF)
+    sums_up.begin()
+    for z in range(2):
+        keep[0, z] = dg(gpre[block(z, False), :], wup[...], 1, 1)
+        gnm_part[z].wait_recv()
+        out2[z] = (keep[0, z] + got[0, z].astype(F32)).astype(BF)
+        gnm_far.append(links.mp(out2.at[z], got2.at[z], far))
+
+    pick = (iota((48, CP), 1) == iota((48, CP), 0) + mp * 43).astype(BF)
+    sqz_out[...] = dg(pick, sqz[...].astype(BF))[0:43].astype(BF)
+    unit, _ = normalize(sqz[...])
+    skv[...] = dg((unit * again[...]).astype(BF), wkvq[:, 0:512]).astype(BF)
+    first_of(0)
+    sums_down.advance()
+    first_of(1)
 
     def second_of(h):
         keys, values = skv[:, heads(h)], skv[:, pl.ds(256 + h * DH, DH)]
@@ -532,110 +690,21 @@
 
     for h in range(2):
         second_of(h)
-
-    def seg_rows():
-        return raw[SEG].reshape(512, D).astype(F32)
-
-    def mix_into(owners, first=False):
-        for half in range(2):
-            cols = pl.ds(half * 512, 512)
-            base = raw[SEG, :, :, cols].reshape(512, 512).astype(F32) if first else mid[:, cols]
-            for owner in owners:
-                base = base + dg(mixg[owner], wo[pl.ds(pl.multiple_of(owner * 256, 256), 256), cols])
-            mid[:, cols] = base
-
-    for cp in late_loads:
-        cp.wait()
-    mix_part.wait_recv()
-    mix_into((mp, part), True)
-    mix_far.wait_recv()
-    mix_fwd = links.mp(mixg.at[far], mixg.at[far], part)
-    done.append(mix_fwd)
     unit, inv = normalize(sqz[...])
     sqz[...] = norm_back(dg(gsq[...], wkvq[:, 0:512], 1, 1), again[...], unit, inv)
     sbuf[0] = sqz[pl.ds(pl.multiple_of((1 - core) * 96, 16), 96), :].astype(BF)
     sq_part = links.mp(sbuf.at[0], sgot.at[0], part)
     done.append(sq_part)
-    mix_into((far,))
-    mix_fwd.wait_recv()
-    mix_into((diag,))
-
-    def norm_mid(r):
-        unit, _ = normalize(mid[pl.ds(r, 128), :])
-        nm[pl.ds(r, 128), :] = (unit * fgain[...]).astype(BF)
-
-    each(512, 128, norm_mid)
-    for a in (SEG, MEM, OLD, GOUT):
-        done.append(part_cp[a])
-    part_cp[GOUT].wait_recv()
-    fwd_cp[GOUT].wait_recv()
-
-    def gout_rows():
-        return raw[GOUT].reshape(512, D)
-
-    for half in range(2):
-        cols = pl.ds(half * 512, 512)
-        tmp[...] = dg(nm[...], wup[:, cols])
-        tmp2[...] = dg(gout_rows(), wdn[cols, :], 1, 1)
-
-        def gelu(r, total):
-            rows = pl.ds(r, 32)
-            v = tmp[rows, :] + ubias[:, cols]
-            square = v * v
-            th = jnp.tanh(0.7978845608028654 * v * (1.0 + 0.044715 * square))
-            hid[rows, cols] = (0.5 * v * (1.0 + th)).astype(BF)
-            slope = 0.5 * (1.0 + th) + (0.5 * 0.7978845608028654) * v * (1.0 - th * th) * (1.0 + 3 * 0.044715 * square)
-            g = (slope * tmp2[rows, :]).astype(BF)
-            gpre[rows, cols] = g
-            return total + fold(g.astype(F32), jnp.add)
-
-        total = loop(512, 32, gelu, jnp.zeros((8, 512), F32))
-        s_ref[8:9, cols] = jnp.sum(total, axis=0, keepdims=True)
-
-    def block(z, other):
-        return pl.ds(pl.multiple_of((2 * z + ((1 - core) if other else core)) * 128, 128), 128)
-
-    gnm_part, gnm_far, down_part = [], [], []
-    for z in range(2):
-        out[0, z] = dg(gpre[block(z, True), :], wup[...], 1, 1).astype(BF)
-        gnm_part.append(links.mp(out.at[0, z], got.at[0, z], part))
-    for z in range(2):
-        keep[0, z] = dg(gpre[block(z, False), :], wup[...], 1, 1)
-    for z in range(2):
-        gnm_part[z].wait_recv()
-        out2[z] = (keep[0, z] + got[0, z].astype(F32)).astype(BF)
-        gnm_far.append(links.mp(out2.at[z], got2.at[z], far))
+    for z in range(2):
+        out[1, z] = dg(hid[block(z, True), :], wdn[...]).astype(BF)
+        down_part.append(links.mp(out.at[1, z], got.at[1, z], part))
+    sums_down.advance()
+    sums_up.advance()
     sq_part.wait_recv()
     sbuf[1] = (sqz[pl.ds(pl.multiple_of(core * 96, 16), 96), :] + sgot[0].astype(F32)).astype(BF)
-    sq_far = links.mp(sbuf.at[1], sgot.at[1], far)
-    for z in range(2):
-        out[1, z] = dg(hid[block(z, True), :], wdn[...]).astype(BF)
-        down_part.append(links.mp(out.at[1, z], got.at[1, z], part))
-    for half in range(2):
-        rows = pl.ds(half * 512, 512)
-        for quarter in range(2):
-            cols = pl.ds(quarter * 512, 512)
-            x_down[rows, cols] = dg(hid[:, rows], raw[GOUT, :, :, cols].reshape(512, 512), 0, 0).astype(BF)
-    pl.semaphore_wait(free.at[0], 5)
-    sums_down = Quarters(links, x_down, 1024, wsq, 0, free.at[1])
-    sums_up = Quarters(links, x_up, 1024, wsq, 1024, free.at[2])
-    sums_sq = Quarters(links, x_sq, 768, wsq, 2048, free.at[3])
-    sums_down.begin()
     for z in range(2):
         keep[1, z] = dg(hid[block(z, False), :], wdn[...])
-    for z in range(2):
-        down_part[z].wait_recv()
-    out2[2] = (keep[1, 1 - zl] + got[1, 1 - zl].astype(F32)).astype(BF)
-    down_far = links.mp(out2.at[2], got2.at[2], far)
-    for half in range(2):
-        rows = pl.ds(half * 512, 512)
-        for quarter in range(2):
-            cols = pl.ds(quarter * 512, 512)
-            x_up[rows, cols] = dg(nm[:, rows], gpre[:, cols], 0, 0).astype(BF)
-    sums_up.begin()
-    sq_far.wait()
-    sqsum[core] = (sbuf[1].astype(F32) + sgot[1].astype(F32)).astype(BF)
-    sq_back = links.mp(sqsum.at[core], sqsum.at[core], part)
+    sums_down.advance()
 
     gb_cp = []
     gain_total = jnp.zeros((1, D), F32)
@@ -650,11 +719,12 @@
         gb[z, core] = gmid.astype(BF)
         gb_cp.append(links.mp(gb.at[z, core], gb.at[z, core], part))
     s_ref[1:2, :] = gain_total
-    sq_back.wait()
-    for half in range(2):
-        cols = pl.ds(half * 512, 512)
-        x_sq[:, cols] = dg(win[:, pl.ds(pl.multiple_of(mp * 768, 256), 768)], sqsum[:, :, cols].reshape(CP, 512), 0, 0).astype(BF)
-    sums_sq.begin()
+    sq_far = links.mp(sbuf.at[1], sgot.at[1], far)
+    sums_down.advance()
+    sums_up.advance()
+    for z in range(2):
+        down_part[z].wait_recv()
+    out2[2] = (keep[1, 1 - zl] + got[1, 1 - zl].astype(F32)).astype(BF)
     for cp in gb_cp:
         cp.wait()
 
@@ -662,7 +732,7 @@
     for half in range(2):
         cols = pl.ds(half * 512, 512)
         x_out[:, cols] = dg(mixg[mp], gb[:, :, :, cols].reshape(512, 512), 0, 0).astype(BF)
-    sums_out = Quarters(links, x_out, 256, wsq, 2816, free.at[4])
+    sums_out = Quarters(links, x_out, 256, wsq, 2816, free.at[4], (2, 3, 2, 3))
     sums_out.begin()
     slope_row = jnp.zeros((1, D), F32)
     for h in range(2):
@@ -694,6 +764,17 @@
         slope_row = slope_row + jnp.where(iota((1, D), 1) == mp * 2 + h, value, 0.0)
         sums_down.advance()
         sums_up.advance()
+        if h == 0:
+            sq_far.wait()
+            sqsum[core] = (sbuf[1].astype(F32) + sgot[1].astype(F32)).astype(BF)
+            sq_back = links.mp(sqsum.at[core], sqsum.at[core], part)
+            down_far = links.mp(out2.at[2], got2.at[2], far)
+        else:
+            sq_back.wait()
+            for half in range(2):
+                cols = pl.ds(half * 512, 512)
+                x_sq[:, cols] = dg(win[:, pl.ds(pl.multiple_of(mp * 768, 256), 768)], sqsum[:, :, cols].reshape(CP, 512), 0, 0).astype(BF)
+            sums_sq.begin()
     s_ref[2:3, :] = slope_row
     s_ref[3:8, :] = jnp.zeros((5, D), F32)
     s_ref[9:16, :] = jnp.zeros((7, D), F32)
@@ -712,6 +793,8 @@
     sums_t.begin()
     sums_s = Smalls(links, s_ref, srecv)
     sums_s.begin()
+    sums_down.advance()
+    sums_up.advance()
 
     def seg_terms(z, other):
         rows = block(z, other)
@@ -739,18 +822,24 @@
     seg_far = links.mp(out2.at[3], got2.at[3], far)
     done.extend(seg_part)
 
-    for sums in (sums_sq, sums_down, sums_up, sums_out, sums_t, sums_s):
+    for sums in (sums_down, sums_up, sums_sq, sums_out, sums_t, sums_s):
         sums.advance()
     seg_far.wait()
     unit, inv = normalize(raw[SEG, mp].astype(F32))
     total = keep[1, zl] + got[0, zl].astype(F32) + got2[3].astype(F32)
     gin[...] = keep[0, zl] + norm_back(total, again[...], unit, inv)
-    everything = (sums_sq, sums_down, sums_up, sums_out, sums_t, sums_s)
-    for _ in range(10):
-        for sums in everything:
+    everything = {sums_down: (x_down, down_out), sums_up: (x_up, up_out), sums_t: (t_ref, t_out), sums_out: (x_out, out_out), sums_sq: (x_sq, sq_out), sums_s: None}
+    leaving = []
+    for _ in range(11):
+        for sums, where in everything.items():
+            last = sums.stage == sums.last
             sums.advance()
+            if last and where is not None:
+                leaving.append(load(*where))
     for sums in everything:
         sums.finish()
+    for cp in leaving:
+        cp.wait()
     for cp in done:
         cp.wait_send()
 
@@ -760,7 +849,7 @@
         return jax.ShapeDtypeStruct(shape, dtype)
 
     outs = (
-        out_shape((128, D), BF), out_shape((CP, D), BF), out_shape((128, D), F32), out_shape((1024, D), BF),
+        out_shape((128, D), BF), out_shape((43, D), BF), out_shape((128, D), F32), out_shape((1024, D), BF),
         out_shape((1024, D), BF), out_shape((768, D), BF), out_shape((256, D), BF), out_shape((4, 256, 768), BF),
         out_shape((16, D), F32),
     )
@@ -775,16 +864,74 @@
         v((CP, 3 * D), BF), v((CP, D), F32), v((CP, 512), BF), v((CP, 512), BF), v((CP, 512), BF), v((256, 512), F32),
         v((2, 96, D), BF), v((2, 96, D), BF), v((2, 96, D), BF),
         v((4, 256, 768), BF), v((4, STRIPS, 16, 128), BF), v((4, STRIPS, 16, 128), BF), v((7, 16, D), F32),
-        pltpu.SemaphoreType.DMA((16,)), pltpu.SemaphoreType.REGULAR((8,)),
-        pltpu.SemaphoreType.DMA((COPIES,)), pltpu.SemaphoreType.DMA((COPIES,)),
+        v((D, D), BF), v((D, D), BF), v((768, D), BF), v((256, D), BF), v((4, 256, 768), BF),
+        pltpu.SemaphoreType.DMA((17,)), pltpu.SemaphoreType.REGULAR((6,)),
+        pltpu.SemaphoreType.DMA((SENDS,)), pltpu.SemaphoreType.DMA((RECVS,)),
     ]
     return pl.pallas_call(
         layer_body,
         out_shape=outs,
         in_specs=[ANY] * 10 + [SMEM] * 3 + [VMEM] * 3,
-        out_specs=tuple(VMEM for _ in outs),
+        out_specs=(VMEM, VMEM, VMEM, ANY, ANY, ANY, ANY, ANY, VMEM),
         scratch_shapes=scratch,
         compiler_params=pltpu.CompilerParams(collective_id=0, has_side_effects=True, vmem_limit_bytes=62 << 20),
+    )(*args)
+
+
+def widen_body(lout, sqz, gin, down, up, sq, outp, t, s, *refs):
+    (o_lout, o_sqz, o_gin, o_again, o_q, o_kv, o_out, o_slopes, o_fgain, o_up, o_ubias, o_down, o_sq) = refs[:13]
+    lin, wide, sem_in, sem_out = refs[13:]
+    pieces = []
+    for src, dst, n in ((down, o_down, 4), (up, o_up, 4), (sq, o_sq, 3), (outp, o_out, 1)):
+        for i in range(n):
+            pieces.append((src.at[pl.ds(256 * i, 256)], dst.at[pl.ds(256 * i, 256)]))
+    loads = []
+    for i, (src, _) in enumerate(pieces):
+        loads.append(pltpu.make_async_copy(src, lin.at[i], sem_in.at[i]))
+    for cp in loads:
+        cp.start()
+    for b in range(4):
+        for part in range(2):
+            o_kv[:, pl.ds(part * D + b * 256, 256)] = t[b, :, part * 256 : part * 256 + 256].astype(F32)
+        o_q[:, pl.ds(b * 256, 256)] = t[b, :, 512:768].astype(F32)
+    o_lout[...] = lout[...]
+    o_gin[...] = gin[...]
+    o_sqz[...] = sqz[...]
+    o_again[...] = s[0:1, :]
+    o_fgain[...] = s[1:2, :]
+    o_slopes[...] = s[2:3, 0:8]
+    o_ubias[...] = s[8:9, :]
+    stores = []
+    for i, (_, dst) in enumerate(pieces):
+        loads[i].wait()
+        wide[i] = lin[i].astype(F32)
+        stores.append(pltpu.make_async_copy(wide.at[i], dst, sem_out.at[i]))
+        stores[-1].start()
+    for cp in stores:
+        cp.wait()
+
+
+def widen(args):
+    def out_shape(shape, dtype):
+        return jax.ShapeDtypeStruct(shape, dtype)
+
+    outs = (
+        out_shape((128, D), BF), out_shape((43, D), BF), out_shape((128, D), F32), out_shape((1, D), F32),
+        out_shape((256, D), F32), out_shape((256, 2 * D), F32), out_shape((256, D), F32), out_shape((1, 8), F32),
+        out_shape((1, D), F32), out_shape((D, D), F32), out_shape((1, D), F32), out_shape((D, D), F32),
+        out_shape((768, D), F32),
+    )
+    hbm = (6, 9, 11, 12)
+    return pl.pallas_call(
+        widen_body,
+        out_shape=outs,
+        in_specs=[VMEM, VMEM, VMEM, ANY, ANY, ANY, ANY, VMEM, VMEM],
+        out_specs=tuple(ANY if i in hbm else VMEM for i in range(13)),
+        scratch_shapes=[
+            pltpu.VMEM((12, 256, D), BF), pltpu.VMEM((12, 256, D), F32),
+            pltpu.SemaphoreType.DMA((12,)), pltpu.SemaphoreType.DMA((12,)),
+        ],
+        compiler_params=pltpu.CompilerParams(vmem_limit_bytes=62 << 20),
     )(*args)
 
 
@@ -792,26 +939,13 @@
     layer_in, memory, squeezed_mem, memory_fill, squeezed_fill, grad_out, attn_gain, w_query, w_keyval,
     w_output, slopes, ffn_gain, w_up, up_bias, w_down, w_squeeze,
 ):
-    mp = lax.axis_index("mp")
-    lout, sqz, gin, down, up, sq, gout, t, s = layer((
+    done = layer((
         layer_in[0], memory[0], squeezed_mem[0], grad_out[0], w_query, w_keyval, w_output, w_up, w_down, w_squeeze,
         memory_fill, squeezed_fill, slopes, attn_gain[None], ffn_gain[None], up_bias[None],
     ))
-    t = t.astype(F32).transpose(1, 0, 2)
+    lout, sqz, gin, again, q, kv, out, slope, fgain, up, ubias, down, sq = widen(done)
     return (
-        lout[None],
-        lax.dynamic_slice_in_dim(sqz, mp * 43, 43, 0)[None],
-        gin[None],
-        s[0],
-        t[:, :, 512:].reshape(256, D),
-        jnp.concatenate([t[:, :, :256].reshape(256, D), t[:, :, 256:512].reshape(256, D)], axis=1),
-        gout.astype(F32),
-        s[2, :8],
-        s[1],
-        up.astype(F32),
-        s[8],
-        down.astype(F32),
-        sq.astype(F32),
+        lout[None], sqz[None], gin[None], again[0], q, kv, out, slope[0], fgain[0], up, ubias[0], down, sq,
     )
 
 

time: 192 us -> 165 us (0.86); the launches traced: 189 us -> 165 us
  other arithmetic: 13.2 us -> 0 us
  local copies, waits for them, and re-layouts: 12.1 us -> 0 us
    convert_element_type x4 -> x0, other arithmetic: 9.84 us -> none  [the longest x1 4.22 us: per_device(): up.astype(F32)]
    pallas_call x0 -> x1, Pallas kernels: none -> 9.78 us  [widen(): pl.pallas_call(widen_body, out_shape=outs, in_specs=[VMEM, VMEM, VMEM, AN...]
    pallas_call x1, Pallas kernels: 162 us -> 153 us  [layer(): pl.pallas_call(layer_body, out_shape=outs, in_specs=[ANY] * 10 + [SMEM] *...]
    slice x5 -> x0, local copies, waits for them, and re-layouts: 4.7 us -> none  [the longest x2 1.63 us: per_device(): t[:, :, :256].reshape(256, D)]
    unnamed x14 -> x0, local copies, waits for them, and re-layouts: 4.64 us -> none
where the time goes in v3:
time: 165 us
  Pallas kernels  163 us (99%)
  between operations  2.13 us (1%)
    pallas_call x1, Pallas kernels, layer(): pl.pallas_call(layer_body, out_shape=outs, in_specs=[ANY] * 10 + [SMEM] *...  153 us
    pallas_call x1, Pallas kernels, widen(): pl.pallas_call(widen_body, out_shape=outs, in_specs=[VMEM, VMEM, VMEM, AN...  9.78 us

profile of v3, /device:TPU:0, one launch (start us, length us, event | category | flops | bytes accessed | tf_op | source)
XLA Modules:
  0.0 165.3 jit_solution(17501206323108020808)
XLA Ops:
  1.9 153.4 %shard_map.255 = (bf16[128,1024]{1,0:T(8,128)(2,1)}, bf16[43,1024]{1,0:T(8,128)(2,1)}, f32[128,1024]{1,0:T(8,128)}, bf16[1024,1024]{1,0:T(8,128)(2,1)}, bf16[102...) custom-call(bf16[128,1024]{1,0:T(8,128)(2,1)} %bitcast.14, ...), custom_call_target="tpu_custom_call" | custom-call | tf_op jit(solution)/shard_map/pallas_call | solution.py:871
  155.3 9.8 %shard_map.256 = (bf16[128,1024]{1,0:T(8,128)(2,1)}, bf16[43,1024]{1,0:T(8,128)(2,1)}, f32[128,1024]{1,0:T(8,128)}, f32[1,1024]{1,0:T(1,128)}, f32[256,1024]{1,0...) custom-call(bf16[128,1024]{1,0:T(8,128)(2,1)} %get-tuple-element.35., ...), custom_call_target="tpu_custom_call" | custom-call | tf_op jit(solution)/shard_map/pallas_call | solution.py:925

commit v4 on v3

v4 whole, which is shorter than its diff:
```python
import functools

import jax
import jax.numpy as jnp
from jax import lax
from jax.experimental import pallas as pl
from jax.experimental.pallas import tpu as pltpu
from jax.sharding import PartitionSpec as P

D = 1024
H = 8
DH = 128
S = 512
M = 512
C = 512
CN = 172
CP = 192
EPS = 1e-05
NEG = -1e30
SCALE = DH ** (-0.5)
RECON = -2.0 / (S * D)
MESH = pl.DeviceIdType.MESH
BF = jnp.bfloat16
F32 = jnp.float32
VMEM = pl.BlockSpec(memory_space=pltpu.VMEM)
SMEM = pl.BlockSpec(memory_space=pltpu.SMEM)
ANY = pl.BlockSpec(memory_space=pl.ANY)
STRIPS = 6
SEG, MEM, OLD, GOUT = 0, 1, 2, 3
BASE = {OLD: 0, MEM: 512, SEG: 1024}
ORDER = (
    "send.s", "psend.m", "psend.s", "own.o", "psend.o", "own.s", "par.o", "send.o", "par.m", "own.m", "par.s",
    "psend.g", "pjo.s", "arr.s", "pjo.o", "pjo.m", "dia.s", "send.m", "far.s", "pjf.s", "arr.o", "at.s.0", "at.s.1",
    "far.o", "dia.o", "pjf.o", "at.o.1", "arr.m", "send.g", "far.m", "at.o.0", "dia.m", "pjf.m", "at.m.1", "at.m.0",
    "combine", "f0", "arr.g", "mf1", "squeeze", "gh0", "mix0a", "fw0", "gh1", "mix0b", "mix1a", "fw1", "ffn0",
    "mix1b", "ffn1", "gnmo", "up", "gnmw", "gS0", "f1", "down", "gS1", "r1", "s1", "s0", "U0", "dsq", "dno", "lnb0",
    "sqS", "lnb1", "D0", "U1", "xout", "att0.0", "sqT", "att0.1", "att0", "att1.0", "xsq", "att1.1", "D1", "att1",
    "t.0", "t.1", "U2", "t.2", "D2", "t", "dnw", "sego", "S0", "D3", "Q0", "dnS", "segw", "T0", "O0", "Q1", "U3",
    "S1", "D4", "O1", "T1", "Q2", "D5", "S2", "Q3", "U4", "O2", "T2", "D6", "Q4", "T3", "O3", "U5", "Q5", "D7", "U6",
    "T4", "Q6", "T5", "segS", "O4", "T6", "S3", "lout", "O5", "Q7", "U7", "O6", "T7", "S4", "T8", "gin", "O7", "U8",
    "S5", "Q8", "D8", "O8", "S6", "T9",
)
SENDS = 86
RECVS = 173


def dp_places():
    dp = lax.axis_index("dp")
    y, x, z = dp // 8, (dp // 2) % 4, dp % 2
    xa, xb = x + 1 - 2 * (x % 2), 3 - x
    ya, yb = y + 1 - 2 * (y % 2), 3 - y
    cube = [
        ((x + x // 2) % 2, y * 8 + xa * 2 + z),
        ((y + y // 2) % 2, ya * 8 + x * 2 + z),
        (x // 2, y * 8 + xb * 2 + z),
        (y // 2, yb * 8 + x * 2 + z),
    ]
    return cube, y * 8 + x * 2 + (1 - z)


def mp_places():
    mp = lax.axis_index("mp")
    zl, core = mp // 2, mp % 2
    return mp, zl, core, zl * 2 + (1 - core), (1 - zl) * 2 + core


class Flight:
    def __init__(self, links, cp, send, recv):
        self.links, self.cp, self.send, self.recv = links, cp, send, recv

    def wait_send(self):
        self.cp.wait_send()
        self.links.spare.append(self.send)

    def wait_recv(self):
        self.cp.wait_recv()

    def wait(self):
        self.wait_send()
        self.wait_recv()


class Links:
    def __init__(self, ssem, rsem):
        self.ssem, self.rsem, self.spare, self.sends, self.recvs = ssem, rsem, [], 0, 0

    def start(self, src, dst, place, like=None):
        if self.spare:
            k = self.spare.pop(0)
        else:
            k, self.sends = self.sends, self.sends + 1
        if like is not None:
            r = like.recv
        else:
            r, self.recvs = self.recvs, self.recvs + 1
        cp = pltpu.make_async_remote_copy(
            src_ref=src, dst_ref=dst, send_sem=self.ssem.at[k], recv_sem=self.rsem.at[r],
            device_id=place, device_id_type=MESH,
        )
        cp.start()
        return Flight(self, cp, k, r)

    def mp(self, src, dst, peer):
        return self.start(src, dst, (lax.axis_index("dp"), peer))

    def dp(self, src, dst, peer, like=None):
        return self.start(src, dst, (peer, lax.axis_index("mp")), like)


def loop(total, step, body, init=None):
    def run(i, carry):
        return body(pl.multiple_of(i * step, step), carry)

    return lax.fori_loop(0, total // step, run, init)


def each(total, step, body):
    def run(r, carry):
        body(r)
        return carry

    loop(total, step, run, 0)


def add_into(dst, dst_at, src, src_at, rows):
    step = 128 if rows % 128 == 0 else 64 if rows % 64 == 0 else 16

    def body(r):
        to, at = dst_at(r, step), src_at(r, step)
        dst[to] = dst[to] + src[at]

    each(rows, step, body)


def quarters(row0, rows, orders):
    return [(row0, rows, 256 * q, 256, order) for q, order in enumerate(orders)]


CUBE_FIRST = ((0, 1, 2, 3, 4), (1, 2, 3, 0, 4), (2, 3, 0, 1, 4), (3, 0, 1, 2, 4))
Z_FIRST = ((4, 0, 1, 2, 3), (4, 1, 2, 3, 0), (4, 2, 3, 0, 1), (4, 3, 0, 1, 2))


class Pieces:
    last = 8

    def __init__(self, links, ref, recv, base, free, pieces):
        self.links, self.ref, self.recv, self.base, self.free, self.pieces = links, ref, recv, base, free, pieces
        cube, zp = dp_places()
        self.dims = cube + [(lax.axis_index("dp") % 2, zp)]
        self.cur, self.old = [p[0] for p in pieces], [[] for _ in pieces]
        self.flying, self.sent, self.stage, self.out = [None] * len(pieces), [], 0, [[] for _ in pieces]

    def launch(self, i, s):
        row0, n, col0, width, order = self.pieces[i]
        cols, cur = pl.ds(col0, width), self.cur
        at = self.base + row0 + n - (n >> s)
        if s < 4:
            bit, peer = self.dims[order[s]]
            half = n >> (s + 1)
            give = pl.multiple_of(cur[i] + (1 - bit) * half, 16)
            self.old[i].append(cur[i])
            cur[i] = pl.multiple_of(cur[i] + bit * half, 16)
            cp = self.links.dp(self.ref.at[pl.ds(give, half), cols], self.recv.at[pl.ds(at, half), cols], peer)
        elif s == 4:
            size = n >> 4
            cp = self.links.dp(
                self.ref.at[pl.ds(cur[i], size), cols], self.recv.at[pl.ds(at, size), cols], self.dims[order[4]][1]
            )
        else:
            k = 8 - s
            here = self.ref.at[pl.ds(cur[i], n >> (k + 1)), cols]
            cp = self.links.dp(here, here, self.dims[order[k]][1], self.out[i][k])
            cur[i] = self.old[i][k]
        self.out[i].append(cp)
        self.flying[i] = cp

    def begin(self):
        for i in range(len(self.pieces)):
            self.launch(i, 0)

    def advance(self):
        s = self.stage
        if s == 4:
            pl.semaphore_wait(self.free, 5)
        earlier, self.sent = self.sent, []
        for i, (row0, n, col0, width, _) in enumerate(self.pieces):
            cp, cols = self.flying[i], pl.ds(col0, width)
            if s == 4:
                cp.wait_send()
            else:
                self.sent.append(cp)
            cp.wait_recv()
            if s <= 4:
                at, here = self.base + row0 + n - (n >> s), self.cur[i]
                add_into(
                    self.ref, lambda r, m: (pl.ds(here + r, m), cols),
                    self.recv, lambda r, m: (pl.ds(at + r, m), cols), n >> min(s + 1, 4),
                )
            if s < 8:
                self.launch(i, s + 1)
        for cp in earlier:
            cp.wait_send()
        if s == 3:
            for cp in self.sent:
                cp.wait_send()
            self.sent = []
            for _, peer in self.dims:
                pl.semaphore_signal(self.free, inc=1, device_id=(peer, lax.axis_index("mp")), device_id_type=MESH)
        self.stage += 1

    def finish(self):
        for cp in self.sent:
            cp.wait_send()


DOWN_PIECES = quarters(0, 1024, CUBE_FIRST)
UP_PIECES = quarters(0, 1024, CUBE_FIRST)
SQ_PIECES = quarters(0, 256, CUBE_FIRST) + quarters(256, 512, Z_FIRST)


class Strips:
    last = 9

    def __init__(self, links, ref, recv, pack, got, free):
        self.links, self.ref, self.recv, self.pack, self.got, self.free = links, ref, recv, pack, got, free
        self.cube, self.zp = dp_places()
        self.cur, self.old = [0] * 4, [[] for _ in range(4)]
        self.flying, self.sent, self.stage, self.out = [], [], 0, []

    def launch(self, s):
        ref, cur = self.ref, self.cur
        self.flying = []
        for j in range(STRIPS):
            q, cols = j % 4, pl.ds(128 * j, 128)
            if s < 4:
                bit, peer = self.cube[(q + s) % 4]
                half = 256 >> (s + 1)
                give = pl.multiple_of(cur[q] + (1 - bit) * half, 16)
                cp = self.links.dp(
                    ref.at[:, pl.ds(give, half), cols], self.recv.at[:, pl.ds(256 - (256 >> s), half), cols], peer
                )
            elif s == 4:
                cp = self.links.dp(ref.at[:, pl.ds(cur[q], 16), cols], self.recv.at[:, pl.ds(240, 16), cols], self.zp)
            else:
                k = 9 - s
                bit, peer = self.cube[(q + k) % 4]
                here = ref.at[:, pl.ds(cur[q], 256 >> (k + 1)), cols]
                cp = self.links.dp(here, here, peer, self.out[k][j])
            self.flying.append(cp)
        self.out.append(self.flying)
        for q in range(4):
            if s < 4:
                bit, _ = self.cube[(q + s) % 4]
                self.old[q].append(cur[q])
                cur[q] = pl.multiple_of(cur[q] + bit * (256 >> (s + 1)), 16)
            elif s > 4:
                cur[q] = self.old[q][9 - s]

    def begin(self):
        self.launch(0)

    def advance(self):
        s = self.stage
        if s > 9:
            return
        mp, zl, core, part, far = mp_places()
        earlier, self.sent = self.sent, []
        if s == 5:
            for cp in self.flying:
                cp.wait()
            self.got[mp] = self.pack[mp]
            for j in range(STRIPS):
                self.ref[:, pl.ds(self.cur[j % 4], 16), pl.ds(128 * j, 128)] = self.got[:, j]
            pl.semaphore_wait(self.free, 4)
            self.launch(6)
        else:
            for j, cp in enumerate(self.flying):
                cols = pl.ds(128 * j, 128)
                if s == 4:
                    cp.wait_send()
                else:
                    self.sent.append(cp)
                cp.wait_recv()
                if s <= 4:
                    rows, at, here = 256 >> min(s + 1, 4), 256 - (256 >> s), self.cur[j % 4]
                    add_into(
                        self.ref, lambda r, m: (slice(None), pl.ds(here + r, m), cols),
                        self.recv, lambda r, m: (slice(None), pl.ds(at + r, m), cols), rows,
                    )
            if s == 3:
                for cp in self.sent:
                    cp.wait_send()
                self.sent = []
                for _, peer in self.cube:
                    pl.semaphore_signal(self.free, inc=1, device_id=(peer, mp), device_id_type=MESH)
            if s == 4:
                for j in range(STRIPS):
                    self.pack[:, j] = self.ref[:, pl.ds(self.cur[j % 4], 16), pl.ds(128 * j, 128)]
                self.flying = [self.links.mp(self.pack.at[peer], self.got.at[mp], peer) for peer in (part, far, 3 - mp)]
            elif s < 9:
                self.launch(s + 1)
        for cp in earlier:
            cp.wait_send()
        self.stage += 1

    def finish(self):
        for cp in self.sent:
            cp.wait_send()


class Smalls:
    last = 6

    def __init__(self, links, ref, recv):
        self.links, self.ref, self.recv, self.stage = links, ref, recv, 0
        cube, zp = dp_places()
        self.peers = [peer for _, peer in cube] + [zp]

    def begin(self):
        s = self.stage
        mp, zl, core, part, far = mp_places()
        self.rows = pl.ds(0, 16 if s < 5 else 8)
        src, dst = self.ref.at[self.rows], self.recv.at[s, self.rows]
        if s < 5:
            self.cp = self.links.dp(src, dst, self.peers[s])
        else:
            self.cp = self.links.mp(src, dst, (part, far)[s - 5])

    def advance(self):
        if self.stage > 6:
            return
        self.cp.wait()
        self.ref[self.rows, :] = self.ref[self.rows, :] + self.recv[self.stage, self.rows, :]
        self.stage += 1
        if self.stage <= 6:
            self.begin()

    def finish(self):
        pass


def dg(a, b, left=1, right=0):
    return lax.dot_general(a, b, (((left,), (right,)), ((), ())), preferred_element_type=F32)


def normalize(rows):
    centre = rows - jnp.mean(rows, axis=-1, keepdims=True)
    inv = lax.rsqrt(jnp.mean(centre * centre, axis=-1, keepdims=True) + EPS)
    return centre * inv, inv


def norm_back(grad, gain, unit, inv):
    g = grad * gain
    return inv * (g - jnp.mean(g, axis=-1, keepdims=True) - unit * jnp.mean(g * unit, axis=-1, keepdims=True))


def iota(shape, dim):
    return lax.broadcasted_iota(jnp.int32, shape, dim)


def fold(x, op):
    out = x[:8]
    for i in range(1, x.shape[0] // 8):
        out = op(out, x[8 * i : 8 * i + 8])
    return out


def layer_body(
    seg_in, mem_in, old_in, gout_in, wq_in, wkv_in, wo_in, wup_in, wdn_in, wsq_in,
    mfill, sfill, slopes, again, fgain, ubias,
    lout_out, sqz_out, gin_out, down_out, up_out, sq_out, out_out, t_out, s_out,
    raw, normed, wkvq, wo, wup, wdn, wsq, kv, query, expo, tmp, tmp2, stat, acc, mixt, mixg, mid, nm, hid, gpre,
    out, got, keep, out2, got2, gb, gmix, gkv, gq, win, sqz, skv, esq, gsq, rec, sbuf, sgot, sqsum, trecv, tpack, tgot, srecv,
    x_down, x_up, x_sq, x_out, t_ref, s_ref, lout, gin, lsem, free, ssem, rsem,
):
    links = Links(ssem, rsem)
    mp, zl, core, part, far = mp_places()
    diag = 3 - mp
    cube, zp = dp_places()
    dp = lax.axis_index("dp")
    mine = pl.ds(pl.multiple_of(mp * 256, 256), 256)

    ins = {SEG: seg_in, MEM: mem_in, OLD: old_in, GOUT: gout_in}
    own_loads = {}
    nlocal = [0]

    def load(src, dst):
        cp = pltpu.make_async_copy(src, dst, lsem.at[nlocal[0]])
        nlocal[0] += 1
        cp.start()
        return cp

    for a in (SEG, MEM, OLD, GOUT):
        own_loads[a] = load(ins[a], raw.at[a, mp])
    w_loads = [
        load(wkv_in.at[:, mine], wkvq.at[:, pl.ds(0, 256)]),
        load(wkv_in.at[:, pl.ds(pl.multiple_of(D + mp * 256, 256), 256)], wkvq.at[:, pl.ds(256, 256)]),
        load(wq_in.at[:, mine], wkvq.at[:, pl.ds(512, 256)]),
    ]

    sem = pltpu.get_barrier_semaphore()
    for peer in [peer for _, peer in cube] + [zp]:
        pl.semaphore_signal(sem, inc=1, device_id=(peer, mp), device_id_type=MESH)
    for peer in (part, far, diag):
        pl.semaphore_signal(sem, inc=1, device_id=(dp, peer), device_id_type=MESH)
    pl.semaphore_wait(sem, 8)

    done = []

    far_cp, part_cp, fwd_cp = {}, {}, {}
    sq_load = load(wsq_in, wsq)
    late_loads = [load(wo_in, wo), load(wup_in, wup), load(wdn_in, wdn)]
    mem_limit = M - mfill[0]
    old_limit = C - sfill[0]

    def slope_of(h):
        return slopes[mp * 2 + h]

    def heads(h):
        return pl.ds(h * DH, DH)

    def column(r, rows):
        return iota((rows, 1), 0) + r

    def exponentials(src, dst, dst0, rows, colmask, causal=False):
        step = 64

        def one(r, top):
            s = src[pl.ds(r, step), :] * SCALE + colmask(r, step)
            if causal:
                s = jnp.where(iota((step, 512), 0) + r <= iota((step, 512), 1), s, NEG)
            src[pl.ds(r, step), :] = s
            return jnp.maximum(top, fold(s, jnp.maximum))

        top = loop(rows, step, one, jnp.full((8, 512), NEG, F32))
        top = jnp.max(top, axis=0, keepdims=True)

        def two(r, total):
            e = jnp.exp(src[pl.ds(r, step), :] - top).astype(BF)
            dst[pl.ds(dst0 + r, step), :] = e
            return total + fold(e.astype(F32), jnp.add)

        total = loop(rows, step, two, jnp.zeros((8, 512), F32))
        return top, jnp.sum(total, axis=0, keepdims=True)

    def attend(h, a):
        base = BASE[a]
        rows = pl.ds(base, 512)
        g = base // 512
        tmp[...] = dg(kv[rows, heads(h)], query[:, heads(h)], 1, 1)
        slope = slope_of(h)

        def colmask(r, step):
            j = column(r, step)
            bias = slope * (j + (base - 1536)).astype(F32)
            if a == MEM:
                bias = jnp.where(j >= mem_limit, bias, NEG)
            if a == OLD:
                bias = jnp.where(j >= old_limit, bias, NEG)
            return bias

        top, total = exponentials(tmp, expo.at[h], base, 512, colmask, a == SEG)
        stat[h * 6 + g : h * 6 + g + 1, :] = top
        stat[h * 6 + 3 + g : h * 6 + 4 + g, :] = total
        acc[h * 3 + g] = dg(kv[rows, pl.ds(256 + h * DH, DH)], expo[h, rows, :], 0, 0)

    def first_of(h):
        rows = pl.ds(BASE[MEM], 512)
        tmp[...] = dg(kv[rows, heads(h)], query[:, heads(h)], 1, 1)
        _, total = exponentials(
            tmp, gkv, 0, 512, lambda r, step: jnp.where(column(r, step) >= mem_limit, 0.0, NEG)
        )
        rec[heads(h), :] = dg(kv[rows, pl.ds(256 + h * DH, DH)], gkv[0:512, :], 0, 0) / total

    tasks, ran = {}, set()

    def task(name, *after):
        def keep_it(run):
            tasks[name] = (run, after)
            return run

        return keep_it

    sums = {
        "D": Pieces(links, x_down, wsq, 0, free.at[1], DOWN_PIECES),
        "U": Pieces(links, x_up, wsq, 1024, free.at[2], UP_PIECES),
        "Q": Pieces(links, x_sq, wsq, 2048, free.at[3], SQ_PIECES),
        "O": Pieces(links, x_out, wsq, 2816, free.at[4], quarters(0, 256, [CUBE_FIRST[q] for q in (2, 3, 2, 3)])),
        "T": Strips(links, t_ref, trecv, tpack, tgot, free.at[5]),
        "S": Smalls(links, s_ref, srecv),
    }
    results = {"D": (x_down, down_out), "U": (x_up, up_out), "Q": (x_sq, sq_out), "O": (x_out, out_out), "T": (t_ref, t_out), "S": (s_ref, s_out)}
    flights = {}
    leaving, roomy = [], []
    bias_rows = [jnp.zeros((8, 512), F32)] * 2
    totals = {"gain": jnp.zeros((1, D), F32), "slope": jnp.zeros((1, D), F32), "bias": bias_rows}

    def begin(name):
        if not roomy:
            pl.semaphore_wait(free.at[0], 5)
            roomy.append(True)
        sums[name].begin()

    def half_rows(z):
        return pl.ds(z * 256, 256)

    def block(z, other):
        return pl.ds(pl.multiple_of((2 * z + ((1 - core) if other else core)) * 128, 128), 128)

    waited = set()

    def once(name, copies):
        if name not in waited:
            waited.add(name)
            for cp in copies:
                cp.wait()

    def norm_rows(a, owner):
        unit, _ = normalize(raw[a, owner].astype(F32))
        normed[pl.ds(pl.multiple_of(BASE[a] + owner * 128, 128), 128), :] = (unit * again[...]).astype(BF)

    def send_rows(a, copies, peer):
        copies[a] = links.mp(ins[a], raw.at[a, mp], peer)
        done.append(copies[a])

    def norm_own(a):
        own_loads[a].wait()
        norm_rows(a, mp)

    def norm_part(a):
        part_cp[a].wait_recv()
        norm_rows(a, part)

    def arrive(a):
        far_cp[a].wait_recv()
        fwd_cp[a] = links.mp(raw.at[a, far], raw.at[a, far], part)
        done.append(fwd_cp[a])

    def norm_diag(a):
        fwd_cp[a].wait_recv()
        norm_rows(a, diag)

    def project(a, chip):
        once("wkvq", w_loads)
        own = pl.ds(pl.multiple_of(chip * 256, 256), 256)
        rows = pl.ds(pl.multiple_of(BASE[a] + chip * 256, 256), 256)
        kv[rows, :] = dg(normed[rows, :], wkvq[:, 0:512]).astype(BF)
        if a == SEG:
            query[own, :] = dg(normed[rows, :], wkvq[:, 512:768]).astype(BF)

    for c, a in (("s", SEG), ("m", MEM), ("o", OLD), ("g", GOUT)):
        task(f"send.{c}")(functools.partial(send_rows, a, far_cp, far))
        task(f"psend.{c}")(functools.partial(send_rows, a, part_cp, part))
        task(f"arr.{c}", f"send.{c}")(functools.partial(arrive, a))
        if a != GOUT:
            task(f"own.{c}")(functools.partial(norm_own, a))
            task(f"par.{c}", f"psend.{c}")(functools.partial(norm_part, a))
            task(f"far.{c}", f"arr.{c}")(functools.partial(norm_rows, a, far))
            task(f"dia.{c}", f"arr.{c}")(functools.partial(norm_diag, a))
            task(f"pjo.{c}", f"own.{c}", f"par.{c}")(functools.partial(project, a, zl))
            task(f"pjf.{c}", f"far.{c}", f"dia.{c}")(functools.partial(project, a, 1 - zl))
            for h in range(2):
                task(f"at.{c}.{h}", f"pjo.{c}", f"pjf.{c}", "pjo.s", "pjf.s")(functools.partial(attend, h, a))

    @task("combine", *(f"at.{c}.{h}" for c in "smo" for h in range(2)))
    def _():
        for h in range(2):
            tops = [stat[h * 6 + g : h * 6 + g + 1, :] for g in range(3)]
            sums = [stat[h * 6 + 3 + g : h * 6 + 4 + g, :] for g in range(3)]
            top = jnp.maximum(jnp.maximum(tops[0], tops[1]), tops[2])
            scales = [jnp.exp(t - top) for t in tops]
            total = scales[0] * sums[0] + scales[1] * sums[1] + scales[2] * sums[2]
            mixed = jnp.zeros((DH, 512), F32)
            for g in range(3):
                inv = scales[g] / total
                stat[12 + h * 3 + g : 13 + h * 3 + g, :] = inv
                mixed = mixed + acc[h * 3 + g] * inv
            mixt[heads(h), :] = mixed
            mixg[mp, :, heads(h)] = mixed.T.astype(BF)
        for z in range(2):
            here = mixg.at[mp, half_rows(z)]
            flights["mix_part", z] = links.mp(here, here, part)
            done.append(flights["mix_part", z])
        send_mix(0)

    def send_mix(z):
        here = mixg.at[mp, half_rows(z)]
        flights["mix_far", z] = links.mp(here, here, far)
        done.append(flights["mix_far", z])

    task("mf1", "combine")(functools.partial(send_mix, 1))

    @task("squeeze", "dia.m")
    def _():
        sq_load.wait()
        rows = raw[MEM].reshape(512, D)
        for tap in range(3):
            pick = (iota((CP, 512), 1) == 3 * iota((CP, 512), 0) + tap).astype(BF)
            win[:, tap * D : (tap + 1) * D] = dg(pick, rows).astype(BF)
        for half in range(2):
            cols = pl.ds(half * 512, 512)
            sqz[:, cols] = dg(win[...], wsq[:, cols])
        for peer in [peer for _, peer in cube] + [zp]:
            pl.semaphore_signal(free.at[0], inc=1, device_id=(peer, mp), device_id_type=MESH)

    @task("r1", "squeeze")
    def _():
        pick = (iota((48, CP), 1) == iota((48, CP), 0) + mp * 43).astype(BF)
        sqz_out[...] = dg(pick, sqz[...].astype(BF))[0:43].astype(BF)
        unit, _ = normalize(sqz[...])
        skv[...] = dg((unit * again[...]).astype(BF), wkvq[:, 0:512]).astype(BF)

    for h in range(2):
        task(f"f{h}", "pjo.m", "pjf.m", "pjo.s", "pjf.s")(functools.partial(first_of, h))

    def second_of(h):
        keys, values = skv[:, heads(h)], skv[:, pl.ds(256 + h * DH, DH)]
        tmp[0:CP, :] = dg(keys, query[:, heads(h)], 1, 1)

        def colmask(r, step):
            slot = column(r, step)
            return jnp.where((3 * slot < M) & (3 * slot + 2 >= mem_limit), 0.0, NEG)

        _, total = exponentials(tmp, esq, 0, CP, colmask)
        inv = 1.0 / total
        second = dg(values, esq[...], 0, 0) * inv
        grad = (rec[heads(h), :] - second) * RECON
        inner = inv * jnp.sum(grad * second, axis=0, keepdims=True)
        scaled = (grad * inv).astype(BF)
        gsq[:, pl.ds(256 + h * DH, DH)] = dg(esq[...], scaled, 1, 1).astype(BF)
        gp = dg(values, scaled)
        gs = (esq[...].astype(F32) * (gp - inner)).astype(BF)
        gsq[:, heads(h)] = (dg(gs, query[:, heads(h)]) * SCALE).astype(BF)

    for h in range(2):
        task(f"s{h}", "r1", f"f{h}", "pjo.s", "pjf.s")(functools.partial(second_of, h))

    @task("dsq", "s0", "s1")
    def _():
        unit, inv = normalize(sqz[...])
        sqz[...] = norm_back(dg(gsq[...], wkvq[:, 0:512], 1, 1), again[...], unit, inv)
        sbuf[0] = sqz[pl.ds(pl.multiple_of((1 - core) * 96, 16), 96), :].astype(BF)
        flights["sq_part"] = links.mp(sbuf.at[0], sgot.at[0], part)
        done.append(flights["sq_part"])

    @task("sqS", "dsq")
    def _():
        flights["sq_part"].wait_recv()
        sbuf[1] = (sqz[pl.ds(pl.multiple_of(core * 96, 16), 96), :] + sgot[0].astype(F32)).astype(BF)
        flights["sq_far"] = links.mp(sbuf.at[1], sgot.at[1], far)

    @task("sqT", "sqS")
    def _():
        flights["sq_far"].wait()
        sqsum[core] = (sbuf[1].astype(F32) + sgot[1].astype(F32)).astype(BF)
        flights["sq_back"] = links.mp(sqsum.at[core], sqsum.at[core], part)

    @task("xsq", "sqT")
    def _():
        flights["sq_back"].wait()
        for half in range(2):
            cols = pl.ds(half * 512, 512)
            x_sq[:, cols] = dg(win[:, pl.ds(pl.multiple_of(mp * 768, 256), 768)], sqsum[:, :, cols].reshape(CP, 512), 0, 0).astype(BF)
        begin("Q")

    def mix_into(z, owners, first=False):
        rows = half_rows(z)
        for half in range(2):
            cols = pl.ds(half * 512, 512)
            base = raw[SEG, 2 * z : 2 * z + 2, :, cols].reshape(256, 512).astype(F32) if first else mid[rows, cols]
            for owner in owners:
                base = base + dg(mixg[owner, rows, :], wo[pl.ds(pl.multiple_of(owner * 256, 256), 256), cols])
            mid[rows, cols] = base

    def mix_own(z):
        once("weights", late_loads)
        flights["mix_part", z].wait_recv()
        mix_into(z, (mp, part), True)

    def forward_mix(z):
        flights["mix_far", z].wait_recv()
        here = mixg.at[far, half_rows(z)]
        flights["mix_fwd", z] = links.mp(here, here, part)
        done.append(flights["mix_fwd", z])

    def grad_hidden(z):
        once("weights", late_loads)
        if z == 0:
            own_loads[GOUT].wait()
            part_cp[GOUT].wait_recv()
            fwd_cp[GOUT].wait_recv()
        for half in range(2):
            cols = pl.ds(half * 512, 512)
            keep[z, :, :, cols] = dg(raw[GOUT, 2 * z : 2 * z + 2].reshape(256, D), wdn[cols, :], 1, 1).reshape(2, 128, 512)

    def feed_forward(z):
        flights["mix_fwd", z].wait_recv()
        mix_into(z, (diag,))
        rows = half_rows(z)
        for i in range(2):
            at = pl.ds(z * 256 + i * 128, 128)
            unit, _ = normalize(mid[at, :])
            nm[at, :] = (unit * fgain[...]).astype(BF)
        for half in range(2):
            cols = pl.ds(half * 512, 512)
            tmp[half_rows(half), :] = dg(nm[rows, :], wup[:, cols])
        for half, i in ((0, 0), (0, 1), (1, 0), (1, 1)):
            cols = pl.ds(half * 512, 512)

            def gelu(r, total):
                to = pl.ds(r + z * 256 + i * 128, 64)
                v = tmp[pl.ds(r + half * 256 + i * 128, 64), :] + ubias[:, cols]
                square = v * v
                th = jnp.tanh(0.7978845608028654 * v * (1.0 + 0.044715 * square))
                hid[to, cols] = (0.5 * v * (1.0 + th)).astype(BF)
                slope = 0.5 * (1.0 + th) + (0.5 * 0.7978845608028654) * v * (1.0 - th * th) * (1.0 + 3 * 0.044715 * square)
                g = (slope * keep[z, i, pl.ds(r, 64), cols]).astype(BF)
                gpre[to, cols] = g
                return total + fold(g.astype(F32), jnp.add)

            totals["bias"][half] = loop(128, 64, gelu, totals["bias"][half])
        if z == 1:
            for half in range(2):
                s_ref[8:9, pl.ds(half * 512, 512)] = jnp.sum(totals["bias"][half], axis=0, keepdims=True)

    for z in range(2):
        task(f"mix{z}a", "combine", *(["mix0a"] if z else []))(functools.partial(mix_own, z))
        task(f"fw{z}", "combine", *(["fw0", "mf1"] if z else []))(functools.partial(forward_mix, z))
        task(f"gh{z}", "arr.g", "psend.g", *(["gh0"] if z else []))(functools.partial(grad_hidden, z))
        task(f"mix{z}b", f"mix{z}a", f"fw{z}")(functools.partial(mix_into, z, (far,)))
        task(f"ffn{z}", f"mix{z}b", f"gh{z}", *(["ffn0"] if z else []))(functools.partial(feed_forward, z))

    def tiles(dst, left, right):
        for half in range(2):
            rows = pl.ds(half * 512, 512)
            for quarter in range(2):
                cols = pl.ds(quarter * 512, 512)
                dst[rows, cols] = dg(left(rows), right(cols), 0, 0).astype(BF)

    @task("down", "ffn1", "squeeze")
    def _():
        tiles(x_down, lambda rows: hid[:, rows], lambda cols: raw[GOUT, :, :, cols].reshape(512, 512))
        begin("D")

    @task("up", "ffn1", "squeeze")
    def _():
        tiles(x_up, lambda rows: nm[:, rows], lambda cols: gpre[:, cols])
        begin("U")

    @task("gnmo", "ffn1")
    def _():
        for z in range(2):
            out[0, z] = dg(gpre[block(z, True), :], wup[...], 1, 1).astype(BF)
            flights["gnm_part", z] = links.mp(out.at[0, z], got.at[0, z], part)

    @task("gnmw", "gnmo")
    def _():
        for z in range(2):
            keep[0, z] = dg(gpre[block(z, False), :], wup[...], 1, 1)

    def gnm_sum(z):
        flights["gnm_part", z].wait_recv()
        out2[z] = (keep[0, z] + got[0, z].astype(F32)).astype(BF)
        flights["gnm_far", z] = links.mp(out2.at[z], got2.at[z], far)

    @task("dno", "ffn1")
    def _():
        for z in range(2):
            out[1, z] = dg(hid[block(z, True), :], wdn[...]).astype(BF)
            flights["down_part", z] = links.mp(out.at[1, z], got.at[1, z], part)
            done.append(flights["down_part", z])

    @task("dnw", "ffn1")
    def _():
        for z in range(2):
            keep[1, z] = dg(hid[block(z, False), :], wdn[...])

    @task("dnS", "dno", "dnw")
    def _():
        for z in range(2):
            flights["down_part", z].wait_recv()
        out2[2] = (keep[1, 1 - zl] + got[1, 1 - zl].astype(F32)).astype(BF)
        flights["down_far"] = links.mp(out2.at[2], got2.at[2], far)

    @task("lout", "dnS")
    def _():
        flights["down_far"].wait()
        lout[...] = (
            mid[pl.ds(pl.multiple_of(mp * 128, 128), 128), :]
            + keep[1, zl] + got[1, zl].astype(F32) + got2[2].astype(F32)
        ).astype(BF)
        leaving.append(load(lout, lout_out))

    def norm_mid_back(z):
        flights["gnm_far", z].wait()
        rows = block(z, False)
        unit, inv = normalize(mid[rows, :])
        g = out2[z].astype(F32) + got2[z].astype(F32)
        totals["gain"] = totals["gain"] + jnp.sum(g * unit, axis=0, keepdims=True) * jnp.where(zl == z, 1.0, 0.0)
        gmid = raw[GOUT, 2 * z + core].astype(F32) + norm_back(g, fgain[...], unit, inv)
        keep[0, z] = gmid
        gb[z, core] = gmid.astype(BF)
        flights["gb", z] = links.mp(gb.at[z, core], gb.at[z, core], part)
        if z == 1:
            s_ref[1:2, :] = totals["gain"]

    for z in range(2):
        task(f"gS{z}", "gnmw", *(["gS0"] if z else []))(functools.partial(gnm_sum, z))
        task(f"lnb{z}", f"gS{z}", *(["lnb0"] if z else []))(functools.partial(norm_mid_back, z))

    @task("xout", "lnb1", "squeeze")
    def _():
        for z in range(2):
            flights["gb", z].wait()
        gmix[...] = dg(wo[mine, :], gb[...].reshape(512, D), 1, 1)
        for half in range(2):
            cols = pl.ds(half * 512, 512)
            x_out[:, cols] = dg(mixg[mp], gb[:, :, :, cols].reshape(512, 512), 0, 0).astype(BF)
        begin("O")

    carried = {}

    def attend_back(h, a):
        base = BASE[a]
        rows = pl.ds(base, 512)
        grad = gmix[heads(h), :]
        if a == OLD:
            carried["inner"] = jnp.sum(grad * mixt[heads(h), :], axis=0, keepdims=True)
            carried["slope"] = jnp.zeros((8, 512), F32)
        inv = stat[12 + h * 3 + base // 512 : 13 + h * 3 + base // 512, :]
        scaled = (grad * inv).astype(BF)
        shift = inv * carried["inner"]
        tmp[...] = dg(kv[rows, pl.ds(256 + h * DH, DH)], scaled)
        gkv[rows, pl.ds(256 + h * DH, DH)] = dg(expo[h, rows, :], scaled, 1, 1).astype(BF)

        def score_grads(r, total):
            at = pl.ds(base + r, 64)
            gs = (expo[h, at, :].astype(F32) * (tmp[pl.ds(r, 64), :] - shift)).astype(BF)
            expo[h, at, :] = gs
            dist = (iota((64, 512), 1) - iota((64, 512), 0) + (1024 - base - r)).astype(F32)
            return total + fold(gs.astype(F32) * dist, jnp.add)

        carried["slope"] = loop(512, 64, score_grads, carried["slope"])
        gkv[rows, heads(h)] = (dg(expo[h, rows, :], query[:, heads(h)]) * SCALE).astype(BF)
        if a == SEG:
            gqt = dg(kv[:, heads(h)], expo[h], 0, 0)
            gq[:, heads(h)] = (gqt * SCALE).T.astype(BF)
            value = -jnp.sum(jnp.sum(carried["slope"], axis=0, keepdims=True), axis=1, keepdims=True)
            totals["slope"] = totals["slope"] + jnp.where(iota((1, D), 1) == mp * 2 + h, value, 0.0)

    before = ("xout", "f0", "f1")
    for h in range(2):
        for name, a in ((f"att{h}.0", OLD), (f"att{h}.1", MEM), (f"att{h}", SEG)):
            task(name, *before)(functools.partial(attend_back, h, a))
            before = (name,)

    def projections(b):
        feats = pl.ds(b * 256, 256)
        big = dg(normed[:, feats], gkv[...], 0, 0)
        small = dg(normed[1024:1536, feats], gq[...], 0, 0)
        t_ref[b, :, 0:512] = big.astype(BF)
        t_ref[b, :, 512:768] = small.astype(BF)
        terms = small[:, 0:128] * wkvq[feats, 512:640].astype(F32) + small[:, 128:256] * wkvq[feats, 640:768].astype(F32)
        for j in range(4):
            terms = terms + big[:, j * 128 : (j + 1) * 128] * wkvq[feats, j * 128 : (j + 1) * 128].astype(F32)
        s_ref[0:1, feats] = jnp.sum(terms.T, axis=0, keepdims=True) / again[:, feats]
        if b == 3:
            begin("T")
            s_ref[2:3, :] = totals["slope"]
            s_ref[3:8, :] = jnp.zeros((5, D), F32)
            s_ref[9:16, :] = jnp.zeros((7, D), F32)
            begin("S")

    for b in range(4):
        task(("t.0", "t.1", "t.2", "t")[b], "att1", *([("t.0", "t.1", "t.2")[b - 1]] if b else []))(functools.partial(projections, b))

    def seg_terms(z, other):
        rows = block(z, other)
        at = pl.ds(pl.multiple_of(BASE[SEG] + (2 * z + ((1 - core) if other else core)) * 128, 128), 128)
        return dg(gkv[at, :], wkvq[:, 0:512], 1, 1) + dg(gq[rows, :], wkvq[:, 512:768], 1, 1)

    @task("sego", "att1")
    def _():
        for z in range(2):
            flights["gnm_part", z].wait_send()
            out[0, z] = seg_terms(z, True).astype(BF)
            flights["seg_part", z] = links.mp(out.at[0, z], got.at[0, z], part)
            done.append(flights["seg_part", z])

    @task("segw", "att1")
    def _():
        for z in range(2):
            terms = seg_terms(z, False)
            for half in range(2):
                tmp2[(2 * z + half) * 128 : (2 * z + half + 1) * 128, :] = terms[:, half * 512 : (half + 1) * 512]

    @task("segS", "sego", "segw")
    def _():
        for z in range(2):
            flights["seg_part", z].wait_recv()
        for half in range(2):
            cols = pl.ds(half * 512, 512)
            at = pl.ds(pl.multiple_of((2 * (1 - zl) + half) * 128, 128), 128)
            out2[3, :, cols] = (tmp2[at, :] + got[0, 1 - zl, :, cols].astype(F32)).astype(BF)
        flights["seg_far"] = links.mp(out2.at[3], got2.at[3], far)

    @task("gin", "segS")
    def _():
        flights["seg_far"].wait()
        unit, inv = normalize(raw[SEG, mp].astype(F32))
        own = [tmp2[pl.ds(pl.multiple_of((2 * zl + half) * 128, 128), 128), :] for half in range(2)]
        total = jnp.concatenate(own, axis=1) + got[0, zl].astype(F32) + got2[3].astype(F32)
        gin[...] = keep[0, zl] + norm_back(total, again[...], unit, inv)
        leaving.append(load(gin, gin_out))

    for name in ORDER:
        if name in tasks:
            run, after = tasks[name]
            assert all(other in ran for other in after), name
            run()
        else:
            part_sum = sums[name[0]]
            assert part_sum.stage == int(name[1:]), name
            part_sum.advance()
            if part_sum.stage > part_sum.last:
                leaving.append(load(*results[name[0]]))
        ran.add(name)
    assert len(ran) == len(tasks) + sum(part_sum.last + 1 for part_sum in sums.values())
    for part_sum in sums.values():
        part_sum.finish()
    for cp in leaving:
        cp.wait()
    for cp in done:
        cp.wait_send()
    assert links.sends <= SENDS and links.recvs <= RECVS, (links.sends, links.recvs)


def layer(args):
    def out_shape(shape, dtype):
        return jax.ShapeDtypeStruct(shape, dtype)

    outs = (
        out_shape((128, D), BF), out_shape((43, D), BF), out_shape((128, D), F32), out_shape((1024, D), BF),
        out_shape((1024, D), BF), out_shape((768, D), BF), out_shape((256, D), BF), out_shape((4, 256, 768), BF),
        out_shape((16, D), F32),
    )
    v = pltpu.VMEM
    scratch = [
        v((4, 4, 128, D), BF), v((1536, D), BF), v((D, 768), BF), v((D, D), BF), v((D, D), BF), v((D, D), BF),
        v((3072, D), BF), v((1536, 512), BF), v((512, 256), BF), v((2, 1536, 512), BF), v((512, 512), F32),
        v((512, 512), F32), v((24, 512), F32), v((6, DH, 512), F32), v((256, 512), F32), v((4, 512, 256), BF),
        v((512, D), F32), v((512, D), BF), v((512, D), BF), v((512, D), BF),
        v((2, 2, 128, D), BF), v((2, 2, 128, D), BF), v((2, 2, 128, D), F32), v((4, 128, D), BF), v((4, 128, D), BF),
        v((2, 2, 128, D), BF), v((256, 512), F32), v((1536, 512), BF), v((512, 256), BF),
        v((CP, 3 * D), BF), v((CP, D), F32), v((CP, 512), BF), v((CP, 512), BF), v((CP, 512), BF), v((256, 512), F32),
        v((2, 96, D), BF), v((2, 96, D), BF), v((2, 96, D), BF),
        v((4, 256, 768), BF), v((4, STRIPS, 16, 128), BF), v((4, STRIPS, 16, 128), BF), v((7, 16, D), F32),
        v((D, D), BF), v((D, D), BF), v((768, D), BF), v((256, D), BF), v((4, 256, 768), BF), v((16, D), F32),
        v((128, D), BF), v((128, D), F32),
        pltpu.SemaphoreType.DMA((19,)), pltpu.SemaphoreType.REGULAR((6,)),
        pltpu.SemaphoreType.DMA((SENDS,)), pltpu.SemaphoreType.DMA((RECVS,)),
    ]
    return pl.pallas_call(
        layer_body,
        out_shape=outs,
        in_specs=[ANY] * 10 + [SMEM] * 3 + [VMEM] * 3,
        out_specs=tuple(VMEM if i == 1 else ANY for i in range(9)),
        scratch_shapes=scratch,
        compiler_params=pltpu.CompilerParams(collective_id=0, has_side_effects=True, vmem_limit_bytes=62 << 20),
    )(*args)


def widen_body(lout, sqz, gin, down, up, sq, outp, t, s, *refs):
    (o_lout, o_sqz, o_gin, o_again, o_q, o_kv, o_out, o_slopes, o_fgain, o_up, o_ubias, o_down, o_sq) = refs[:13]
    tin, lin, kv_wide, q_wide, wide, b_lout, b_gin, b_s, r_again, r_fgain, r_ubias, sem_in, sem_out = refs[13:]
    loads = []

    def load(src, dst):
        cp = pltpu.make_async_copy(src, dst, sem_in.at[len(loads)])
        cp.start()
        loads.append(cp)
        return cp

    s_load = load(s, b_s)
    t_load = load(t, tin)
    pieces = []
    for src, dst, n in ((down, o_down, 4), (up, o_up, 4), (sq, o_sq, 3), (outp, o_out, 1)):
        for i in range(n):
            k = len(pieces)
            pieces.append((load(src.at[pl.ds(256 * i, 256)], lin.at[k]), dst.at[pl.ds(256 * i, 256)]))
    plain = [(load(lout, b_lout), b_lout, o_lout), (load(gin, b_gin), b_gin, o_gin)]
    stores = []

    def leave(src, dst):
        stores.append(pltpu.make_async_copy(src, dst, sem_out.at[len(stores)]))
        stores[-1].start()

    s_load.wait()
    for row, to, dst in ((0, r_again, o_again), (1, r_fgain, o_fgain), (8, r_ubias, o_ubias)):
        to[...] = b_s[row : row + 1, :]
        leave(to, dst)
    o_slopes[...] = b_s[2:3, 0:8]
    o_sqz[...] = sqz[...]
    t_load.wait()
    for b in range(4):
        for part in range(2):
            kv_wide[:, pl.ds(part * D + b * 256, 256)] = tin[b, :, part * 256 : part * 256 + 256].astype(F32)
        q_wide[:, pl.ds(b * 256, 256)] = tin[b, :, 512:768].astype(F32)
    leave(kv_wide, o_kv)
    leave(q_wide, o_q)
    for i, (cp, dst) in enumerate(pieces):
        cp.wait()
        wide[i] = lin[i].astype(F32)
        leave(wide.at[i], dst)
    for cp, src, dst in plain:
        cp.wait()
        leave(src, dst)
    for cp in stores:
        cp.wait()


def widen(args):
    def out_shape(shape, dtype):
        return jax.ShapeDtypeStruct(shape, dtype)

    outs = (
        out_shape((128, D), BF), out_shape((43, D), BF), out_shape((128, D), F32), out_shape((1, D), F32),
        out_shape((256, D), F32), out_shape((256, 2 * D), F32), out_shape((256, D), F32), out_shape((1, 8), F32),
        out_shape((1, D), F32), out_shape((D, D), F32), out_shape((1, D), F32), out_shape((D, D), F32),
        out_shape((768, D), F32),
    )
    hbm = (0, 2, 3, 4, 5, 6, 8, 9, 10, 11, 12)
    v = pltpu.VMEM
    return pl.pallas_call(
        widen_body,
        out_shape=outs,
        in_specs=[ANY, VMEM, ANY, ANY, ANY, ANY, ANY, ANY, ANY],
        out_specs=tuple(ANY if i in hbm else VMEM for i in range(13)),
        scratch_shapes=[
            v((4, 256, 768), BF), v((12, 256, D), BF), v((256, 2 * D), F32), v((256, D), F32), v((12, 256, D), F32),
            v((128, D), BF), v((128, D), F32), v((16, D), F32), v((1, D), F32), v((1, D), F32), v((1, D), F32),
            pltpu.SemaphoreType.DMA((16,)), pltpu.SemaphoreType.DMA((19,)),
        ],
        compiler_params=pltpu.CompilerParams(vmem_limit_bytes=62 << 20),
    )(*args)


def per_device(
    layer_in, memory, squeezed_mem, memory_fill, squeezed_fill, grad_out, attn_gain, w_query, w_keyval,
    w_output, slopes, ffn_gain, w_up, up_bias, w_down, w_squeeze,
):
    done = layer((
        layer_in[0], memory[0], squeezed_mem[0], grad_out[0], w_query, w_keyval, w_output, w_up, w_down, w_squeeze,
        memory_fill, squeezed_fill, slopes, attn_gain[None], ffn_gain[None], up_bias[None],
    ))
    lout, sqz, gin, again, q, kv, out, slope, fgain, up, ubias, down, sq = widen(done)
    return (
        lout[None], sqz[None], gin[None], again[0], q, kv, out, slope[0], fgain[0], up, ubias[0], down, sq,
    )


def solution(mesh):
    rows = P("dp", "mp", None)
    in_specs = (
        rows, rows, rows, P("dp"), P("dp"), rows, P(), P(), P(), P(), P(), P(), P(None, "mp"), P("mp"), P("mp", None), P(),
    )
    out_specs = (
        rows, rows, rows, P(), P("mp", None), P("mp", None), P("mp", None), P(), P(), P(None, "mp"), P("mp"), P("mp", None), P("mp", None),
    )
    return jax.shard_map(per_device, mesh=mesh, in_specs=in_specs, out_specs=out_specs, check_vma=False)
```

time: 165 us -> 157 us (0.952); the launches traced: 165 us -> 153 us
  Pallas kernels: 163 us -> 151 us
    pallas_call x1, Pallas kernels: 153 us -> 141 us  [layer(): pl.pallas_call(layer_body, out_shape=outs, in_specs=[ANY] * 10 + [SMEM] *...]
where the time goes in v4:
time: 157 us; the launch traced here: 153 us
  Pallas kernels  151 us (96%)
  between operations  2.41 us (2%)
    pallas_call x1, Pallas kernels, layer(): pl.pallas_call(layer_body, out_shape=outs, in_specs=[ANY] * 10 + [SMEM] *...  141 us
    pallas_call x1, Pallas kernels, widen(): pl.pallas_call(widen_body, out_shape=outs, in_specs=[ANY, VMEM, ANY, ANY,...  9.75 us

profile of v4, /device:TPU:0, one launch (start us, length us, event | category | flops | bytes accessed | tf_op | source)
XLA Modules:
  0.0 153.5 jit_solution(15610090093750365061)
XLA Ops:
  1.9 141.3 %shard_map.255 = (bf16[128,1024]{1,0:T(8,128)(2,1)}, bf16[43,1024]{1,0:T(8,128)(2,1)}, f32[128,1024]{1,0:T(8,128)}, bf16[1024,1024]{1,0:T(8,128)(2,1)}, bf16[102...) custom-call(bf16[128,1024]{1,0:T(8,128)(2,1)} %bitcast.14, ...), custom_call_target="tpu_custom_call" | custom-call | tf_op jit(solution)/shard_map/pallas_call | solution.py:963
  143.3 9.7 %shard_map.256 = (bf16[128,1024]{1,0:T(8,128)(2,1)}, bf16[43,1024]{1,0:T(8,128)(2,1)}, f32[128,1024]{1,0:T(8,128)}, f32[1,1024]{1,0:T(1,128)}, f32[256,1024]{1,0...) custom-call(bf16[128,1024]{1,0:T(8,128)(2,1)} %get-tuple-element.35., ...), custom_call_target="tpu_custom_call" | custom-call | tf_op jit(solution)/shard_map/pallas_call | solution.py:1034

commit v5 on v4

--- a/solution.py
+++ b/solution.py
@@ -367,11 +367,11 @@
 
 def layer_body(
     seg_in, mem_in, old_in, gout_in, wq_in, wkv_in, wo_in, wup_in, wdn_in, wsq_in,
-    mfill, sfill, slopes, again, fgain, ubias,
+    mfill, sfill, slopes, again_in, fgain_in, ubias_in,
     lout_out, sqz_out, gin_out, down_out, up_out, sq_out, out_out, t_out, s_out,
     raw, normed, wkvq, wo, wup, wdn, wsq, kv, query, expo, tmp, tmp2, stat, acc, mixt, mixg, mid, nm, hid, gpre,
     out, got, keep, out2, got2, gb, gmix, gkv, gq, win, sqz, skv, esq, gsq, rec, sbuf, sgot, sqsum, trecv, tpack, tgot, srecv,
-    x_down, x_up, x_sq, x_out, t_ref, s_ref, lout, gin, lsem, free, ssem, rsem,
+    x_down, x_up, x_sq, x_out, t_ref, s_ref, lout, gin, sqz_rows, again, fgain, ubias, lsem, free, ssem, rsem,
 ):
     links = Links(ssem, rsem)
     mp, zl, core, part, far = mp_places()
@@ -380,6 +380,12 @@
     dp = lax.axis_index("dp")
     mine = pl.ds(pl.multiple_of(mp * 256, 256), 256)
 
+    sem = pltpu.get_barrier_semaphore()
+    for peer in [peer for _, peer in cube] + [zp]:
+        pl.semaphore_signal(sem, inc=1, device_id=(peer, mp), device_id_type=MESH)
+    for peer in (part, far, diag):
+        pl.semaphore_signal(sem, inc=1, device_id=(dp, peer), device_id_type=MESH)
+
     ins = {SEG: seg_in, MEM: mem_in, OLD: old_in, GOUT: gout_in}
     own_loads = {}
     nlocal = [0]
@@ -392,17 +398,13 @@
 
     for a in (SEG, MEM, OLD, GOUT):
         own_loads[a] = load(ins[a], raw.at[a, mp])
+    gains = [load(again_in, again), load(fgain_in, fgain), load(ubias_in, ubias)]
     w_loads = [
         load(wkv_in.at[:, mine], wkvq.at[:, pl.ds(0, 256)]),
         load(wkv_in.at[:, pl.ds(pl.multiple_of(D + mp * 256, 256), 256)], wkvq.at[:, pl.ds(256, 256)]),
         load(wq_in.at[:, mine], wkvq.at[:, pl.ds(512, 256)]),
     ]
 
-    sem = pltpu.get_barrier_semaphore()
-    for peer in [peer for _, peer in cube] + [zp]:
-        pl.semaphore_signal(sem, inc=1, device_id=(peer, mp), device_id_type=MESH)
-    for peer in (part, far, diag):
-        pl.semaphore_signal(sem, inc=1, device_id=(dp, peer), device_id_type=MESH)
     pl.semaphore_wait(sem, 8)
 
     done = []
@@ -516,6 +518,7 @@
                 cp.wait()
 
     def norm_rows(a, owner):
+        once("gains", gains)
         unit, _ = normalize(raw[a, owner].astype(F32))
         normed[pl.ds(pl.multiple_of(BASE[a] + owner * 128, 128), 128), :] = (unit * again[...]).astype(BF)
 
@@ -606,7 +609,8 @@
     @task("r1", "squeeze")
     def _():
         pick = (iota((48, CP), 1) == iota((48, CP), 0) + mp * 43).astype(BF)
-        sqz_out[...] = dg(pick, sqz[...].astype(BF))[0:43].astype(BF)
+        sqz_rows[...] = dg(pick, sqz[...].astype(BF))[0:43].astype(BF)
+        leaving.append(load(sqz_rows, sqz_out))
         unit, _ = normalize(sqz[...])
         skv[...] = dg((unit * again[...]).astype(BF), wkvq[:, 0:512]).astype(BF)
 
@@ -956,15 +960,15 @@
         v((2, 96, D), BF), v((2, 96, D), BF), v((2, 96, D), BF),
         v((4, 256, 768), BF), v((4, STRIPS, 16, 128), BF), v((4, STRIPS, 16, 128), BF), v((7, 16, D), F32),
         v((D, D), BF), v((D, D), BF), v((768, D), BF), v((256, D), BF), v((4, 256, 768), BF), v((16, D), F32),
-        v((128, D), BF), v((128, D), F32),
-        pltpu.SemaphoreType.DMA((19,)), pltpu.SemaphoreType.REGULAR((6,)),
+        v((128, D), BF), v((128, D), F32), v((43, D), BF), v((1, D), F32), v((1, D), F32), v((1, D), F32),
+        pltpu.SemaphoreType.DMA((23,)), pltpu.SemaphoreType.REGULAR((6,)),
         pltpu.SemaphoreType.DMA((SENDS,)), pltpu.SemaphoreType.DMA((RECVS,)),
     ]
     return pl.pallas_call(
         layer_body,
         out_shape=outs,
-        in_specs=[ANY] * 10 + [SMEM] * 3 + [VMEM] * 3,
-        out_specs=tuple(VMEM if i == 1 else ANY for i in range(9)),
+        in_specs=[ANY] * 10 + [SMEM] * 3 + [ANY] * 3,
+        out_specs=(ANY,) * 9,
         scratch_shapes=scratch,
         compiler_params=pltpu.CompilerParams(collective_id=0, has_side_effects=True, vmem_limit_bytes=62 << 20),
     )(*args)
@@ -972,7 +976,7 @@
 
 def widen_body(lout, sqz, gin, down, up, sq, outp, t, s, *refs):
     (o_lout, o_sqz, o_gin, o_again, o_q, o_kv, o_out, o_slopes, o_fgain, o_up, o_ubias, o_down, o_sq) = refs[:13]
-    tin, lin, kv_wide, q_wide, wide, b_lout, b_gin, b_s, r_again, r_fgain, r_ubias, sem_in, sem_out = refs[13:]
+    tin, lin, kv_wide, q_wide, wide, b_lout, b_gin, b_s, b_sqz, r_again, r_fgain, r_ubias, r_slopes, sem_in, sem_out = refs[13:]
     loads = []
 
     def load(src, dst):
@@ -988,7 +992,7 @@
         for i in range(n):
             k = len(pieces)
             pieces.append((load(src.at[pl.ds(256 * i, 256)], lin.at[k]), dst.at[pl.ds(256 * i, 256)]))
-    plain = [(load(lout, b_lout), b_lout, o_lout), (load(gin, b_gin), b_gin, o_gin)]
+    plain = [(load(lout, b_lout), b_lout, o_lout), (load(gin, b_gin), b_gin, o_gin), (load(sqz, b_sqz), b_sqz, o_sqz)]
     stores = []
 
     def leave(src, dst):
@@ -999,8 +1003,8 @@
     for row, to, dst in ((0, r_again, o_again), (1, r_fgain, o_fgain), (8, r_ubias, o_ubias)):
         to[...] = b_s[row : row + 1, :]
         leave(to, dst)
-    o_slopes[...] = b_s[2:3, 0:8]
-    o_sqz[...] = sqz[...]
+    r_slopes[...] = b_s[2:3, 0:8]
+    leave(r_slopes, o_slopes)
     t_load.wait()
     for b in range(4):
         for part in range(2):
@@ -1029,17 +1033,17 @@
         out_shape((1, D), F32), out_shape((D, D), F32), out_shape((1, D), F32), out_shape((D, D), F32),
         out_shape((768, D), F32),
     )
-    hbm = (0, 2, 3, 4, 5, 6, 8, 9, 10, 11, 12)
     v = pltpu.VMEM
     return pl.pallas_call(
         widen_body,
         out_shape=outs,
-        in_specs=[ANY, VMEM, ANY, ANY, ANY, ANY, ANY, ANY, ANY],
-        out_specs=tuple(ANY if i in hbm else VMEM for i in range(13)),
+        in_specs=[ANY] * 9,
+        out_specs=(ANY,) * 13,
         scratch_shapes=[
             v((4, 256, 768), BF), v((12, 256, D), BF), v((256, 2 * D), F32), v((256, D), F32), v((12, 256, D), F32),
-            v((128, D), BF), v((128, D), F32), v((16, D), F32), v((1, D), F32), v((1, D), F32), v((1, D), F32),
-            pltpu.SemaphoreType.DMA((16,)), pltpu.SemaphoreType.DMA((19,)),
+            v((128, D), BF), v((128, D), F32), v((16, D), F32), v((43, D), BF),
+            v((1, D), F32), v((1, D), F32), v((1, D), F32), v((1, 8), F32),
+            pltpu.SemaphoreType.DMA((17,)), pltpu.SemaphoreType.DMA((21,)),
         ],
         compiler_params=pltpu.CompilerParams(vmem_limit_bytes=62 << 20),
     )(*args)

time: 157 us -> 154 us (0.981)
  Pallas kernels: 151 us -> 149 us
where the time goes in v5:
time: 154 us; the launch traced here: 151 us
  Pallas kernels  149 us (97%)
  between operations  2.41 us (2%)
    pallas_call x1, Pallas kernels, layer(): pl.pallas_call(layer_body, out_shape=outs, in_specs=[ANY] * 10 + [SMEM] *...  141 us
    pallas_call x1, Pallas kernels, widen(): pl.pallas_call(widen_body, out_shape=outs, in_specs=[ANY] * 9, out_specs=...  8.3 us

profile of v5, /device:TPU:0, one launch (start us, length us, event | category | flops | bytes accessed | tf_op | source)
XLA Modules:
  0.0 151.3 jit_solution(1119602786736668484)
XLA Ops:
  1.9 140.6 %shard_map.255 = (bf16[128,1024]{1,0:T(8,128)(2,1)}, bf16[43,1024]{1,0:T(8,128)(2,1)}, f32[128,1024]{1,0:T(8,128)}, bf16[1024,1024]{1,0:T(8,128)(2,1)}, bf16[102...) custom-call(bf16[128,1024]{1,0:T(8,128)(2,1)} %bitcast.14, ...), custom_call_target="tpu_custom_call" | custom-call | tf_op jit(solution)/shard_map/pallas_call | solution.py:967
  142.6 8.3 %shard_map.256 = (bf16[128,1024]{1,0:T(8,128)(2,1)}, bf16[43,1024]{1,0:T(8,128)(2,1)}, f32[128,1024]{1,0:T(8,128)}, f32[1,1024]{1,0:T(1,128)}, f32[256,1024]{1,0...) custom-call(bf16[128,1024]{1,0:T(8,128)(2,1)} %get-tuple-element.35., ...), custom_call_target="tpu_custom_call" | custom-call | tf_op jit(solution)/shard_map/pallas_call | solution.py:1037

commit v6 on v5

--- a/solution.py
+++ b/solution.py
@@ -29,19 +29,19 @@
 SEG, MEM, OLD, GOUT = 0, 1, 2, 3
 BASE = {OLD: 0, MEM: 512, SEG: 1024}
 ORDER = (
-    "send.s", "psend.m", "psend.s", "own.o", "psend.o", "own.s", "par.o", "send.o", "par.m", "own.m", "par.s",
-    "psend.g", "pjo.s", "arr.s", "pjo.o", "pjo.m", "dia.s", "send.m", "far.s", "pjf.s", "arr.o", "at.s.0", "at.s.1",
-    "far.o", "dia.o", "pjf.o", "at.o.1", "arr.m", "send.g", "far.m", "at.o.0", "dia.m", "pjf.m", "at.m.1", "at.m.0",
-    "combine", "f0", "arr.g", "mf1", "squeeze", "gh0", "mix0a", "fw0", "gh1", "mix0b", "mix1a", "fw1", "ffn0",
-    "mix1b", "ffn1", "gnmo", "up", "gnmw", "gS0", "f1", "down", "gS1", "r1", "s1", "s0", "U0", "dsq", "dno", "lnb0",
-    "sqS", "lnb1", "D0", "U1", "xout", "att0.0", "sqT", "att0.1", "att0", "att1.0", "xsq", "att1.1", "D1", "att1",
-    "t.0", "t.1", "U2", "t.2", "D2", "t", "dnw", "sego", "S0", "D3", "Q0", "dnS", "segw", "T0", "O0", "Q1", "U3",
-    "S1", "D4", "O1", "T1", "Q2", "D5", "S2", "Q3", "U4", "O2", "T2", "D6", "Q4", "T3", "O3", "U5", "Q5", "D7", "U6",
-    "T4", "Q6", "T5", "segS", "O4", "T6", "S3", "lout", "O5", "Q7", "U7", "O6", "T7", "S4", "T8", "gin", "O7", "U8",
-    "S5", "Q8", "D8", "O8", "S6", "T9",
+    "send.s", "psend.m", "psend.o", "psend.s", "own.s", "par.m", "send.m", "arr.s", "far.s", "own.o", "own.m",
+    "par.s", "pjo.s", "send.o", "dia.s", "pjf.s", "at.s.1", "par.o", "arr.m", "pjo.m", "far.m", "pjo.o", "at.s.0",
+    "dia.m", "send.g", "psend.g", "pjf.m", "arr.o", "at.m.0", "far.o", "at.m.1", "dia.o", "pjf.o", "at.o.1", "at.o.0",
+    "combine", "arr.g", "squeeze", "mf1", "gh0", "mix0a", "fw0", "mix1a", "mix0b", "ffn0", "fw1", "gh1",
+    "mix1b", "ffn1", "gnmo", "down", "gnmw", "gS0", "f1", "up", "r1", "gS1", "f0", "s1", "s0", "lnb0", "D0", "dsq",
+    "U0", "lnb1", "sqS", "D1", "xout", "att0.0", "U1", "att0.1", "att0", "sqT", "D2", "att1.0", "att1.1", "xsq",
+    "att1", "t.0", "U2", "t.1", "t.2", "t", "D3", "S0", "Q0", "T0", "O0", "U3", "Q1", "D4", "T1", "O1", "S1", "Q2",
+    "D5", "T2", "U4", "Q3", "S2", "D6", "T3", "Q4", "dno", "U5", "T4", "sego", "O2", "D7", "segw", "O3", "U6", "Q5",
+    "S3", "dnw", "O4", "dnS", "T5", "Q6", "T6", "O5", "D8", "S4", "segS", "U7", "T7", "S5", "O6", "lout", "Q7", "T8",
+    "O7", "gin", "S6", "Q8", "U8", "O8", "T9",
 )
-SENDS = 86
-RECVS = 173
+SENDS = 116
+RECVS = 252
 
 
 def dp_places():
@@ -147,32 +147,32 @@
         self.links, self.ref, self.recv, self.base, self.free, self.pieces = links, ref, recv, base, free, pieces
         cube, zp = dp_places()
         self.dims = cube + [(lax.axis_index("dp") % 2, zp)]
-        self.cur, self.old = [p[0] for p in pieces], [[] for _ in pieces]
+        self.at = [[p[0]] for p in pieces]
         self.flying, self.sent, self.stage, self.out = [None] * len(pieces), [], 0, [[] for _ in pieces]
+        self.back = [[[] for _ in range(4)] for _ in pieces]
 
     def launch(self, i, s):
         row0, n, col0, width, order = self.pieces[i]
-        cols, cur = pl.ds(col0, width), self.cur
-        at = self.base + row0 + n - (n >> s)
+        cols = pl.ds(col0, width)
+        room = self.base + row0 + n - (n >> s)
+        bit, peer = self.dims[order[s]]
         if s < 4:
-            bit, peer = self.dims[order[s]]
             half = n >> (s + 1)
-            give = pl.multiple_of(cur[i] + (1 - bit) * half, 16)
-            self.old[i].append(cur[i])
-            cur[i] = pl.multiple_of(cur[i] + bit * half, 16)
-            cp = self.links.dp(self.ref.at[pl.ds(give, half), cols], self.recv.at[pl.ds(at, half), cols], peer)
-        elif s == 4:
-            size = n >> 4
-            cp = self.links.dp(
-                self.ref.at[pl.ds(cur[i], size), cols], self.recv.at[pl.ds(at, size), cols], self.dims[order[4]][1]
-            )
+            give = pl.multiple_of(self.at[i][s] + (1 - bit) * half, 16)
+            self.at[i].append(pl.multiple_of(self.at[i][s] + bit * half, 16))
         else:
-            k = 8 - s
-            here = self.ref.at[pl.ds(cur[i], n >> (k + 1)), cols]
-            cp = self.links.dp(here, here, self.dims[order[k]][1], self.out[i][k])
-            cur[i] = self.old[i][k]
+            half, give = n >> 4, self.at[i][4]
+        cp = self.links.dp(self.ref.at[pl.ds(give, half), cols], self.recv.at[pl.ds(room, half), cols], peer)
         self.out[i].append(cp)
         self.flying[i] = cp
+
+    def give_back(self, i, k, later):
+        row0, n, col0, width, order = self.pieces[i]
+        start, size, like = self.at[i][min(k + 2, 4)], n >> min(k + 2, 4), self.out[i][k]
+        if later:
+            start, like = pl.multiple_of(2 * self.at[i][k + 1] + size - start, 16), None
+        here = self.ref.at[pl.ds(start, size), pl.ds(col0, width)]
+        self.back[i][k].append(self.links.dp(here, here, self.dims[order[k]][1], like))
 
     def begin(self):
         for i in range(len(self.pieces)):
@@ -184,20 +184,33 @@
             pl.semaphore_wait(self.free, 5)
         earlier, self.sent = self.sent, []
         for i, (row0, n, col0, width, _) in enumerate(self.pieces):
+            if s > 4:
+                k = 8 - s
+                for cp in self.back[i][k]:
+                    cp.wait_recv()
+                self.back[i][k][0].wait_send()
+                self.sent.extend(self.back[i][k][1:])
+                if k >= 1:
+                    self.give_back(i, k - 1, True)
+                if k >= 2:
+                    self.give_back(i, k - 2, False)
+                continue
             cp, cols = self.flying[i], pl.ds(col0, width)
             if s == 4:
                 cp.wait_send()
             else:
                 self.sent.append(cp)
             cp.wait_recv()
-            if s <= 4:
-                at, here = self.base + row0 + n - (n >> s), self.cur[i]
-                add_into(
-                    self.ref, lambda r, m: (pl.ds(here + r, m), cols),
-                    self.recv, lambda r, m: (pl.ds(at + r, m), cols), n >> min(s + 1, 4),
-                )
-            if s < 8:
+            room, here = self.base + row0 + n - (n >> s), self.at[i][min(s + 1, 4)]
+            add_into(
+                self.ref, lambda r, m: (pl.ds(here + r, m), cols),
+                self.recv, lambda r, m: (pl.ds(room + r, m), cols), n >> min(s + 1, 4),
+            )
+            if s < 4:
                 self.launch(i, s + 1)
+            else:
+                self.give_back(i, 3, False)
+                self.give_back(i, 2, False)
         for cp in earlier:
             cp.wait_send()
         if s == 3:
@@ -215,7 +228,7 @@
 
 DOWN_PIECES = quarters(0, 1024, CUBE_FIRST)
 UP_PIECES = quarters(0, 1024, CUBE_FIRST)
-SQ_PIECES = quarters(0, 256, CUBE_FIRST) + quarters(256, 512, Z_FIRST)
+SQ_PIECES = quarters(0, 512, CUBE_FIRST) + quarters(512, 256, Z_FIRST)
 
 
 class Strips:
@@ -224,55 +237,67 @@
     def __init__(self, links, ref, recv, pack, got, free):
         self.links, self.ref, self.recv, self.pack, self.got, self.free = links, ref, recv, pack, got, free
         self.cube, self.zp = dp_places()
-        self.cur, self.old = [0] * 4, [[] for _ in range(4)]
+        self.at = [[0] for _ in range(4)]
         self.flying, self.sent, self.stage, self.out = [], [], 0, []
+        self.back = [[[] for _ in range(4)] for _ in range(STRIPS)]
 
     def launch(self, s):
-        ref, cur = self.ref, self.cur
+        ref = self.ref
         self.flying = []
+        if s < 4:
+            for q in range(4):
+                bit, _ = self.cube[(q + s) % 4]
+                self.at[q].append(pl.multiple_of(self.at[q][s] + bit * (256 >> (s + 1)), 16))
         for j in range(STRIPS):
             q, cols = j % 4, pl.ds(128 * j, 128)
             if s < 4:
                 bit, peer = self.cube[(q + s) % 4]
                 half = 256 >> (s + 1)
-                give = pl.multiple_of(cur[q] + (1 - bit) * half, 16)
+                give = pl.multiple_of(self.at[q][s] + (1 - bit) * half, 16)
                 cp = self.links.dp(
                     ref.at[:, pl.ds(give, half), cols], self.recv.at[:, pl.ds(256 - (256 >> s), half), cols], peer
                 )
-            elif s == 4:
-                cp = self.links.dp(ref.at[:, pl.ds(cur[q], 16), cols], self.recv.at[:, pl.ds(240, 16), cols], self.zp)
             else:
-                k = 9 - s
-                bit, peer = self.cube[(q + k) % 4]
-                here = ref.at[:, pl.ds(cur[q], 256 >> (k + 1)), cols]
-                cp = self.links.dp(here, here, peer, self.out[k][j])
+                cp = self.links.dp(ref.at[:, pl.ds(self.at[q][4], 16), cols], self.recv.at[:, pl.ds(240, 16), cols], self.zp)
             self.flying.append(cp)
         self.out.append(self.flying)
-        for q in range(4):
-            if s < 4:
-                bit, _ = self.cube[(q + s) % 4]
-                self.old[q].append(cur[q])
-                cur[q] = pl.multiple_of(cur[q] + bit * (256 >> (s + 1)), 16)
-            elif s > 4:
-                cur[q] = self.old[q][9 - s]
+
+    def give_back(self, j, k, later):
+        at = self.at[j % 4]
+        start, size, like = at[min(k + 2, 4)], 256 >> min(k + 2, 4), self.out[k][j]
+        if later:
+            start, like = pl.multiple_of(2 * at[k + 1] + size - start, 16), None
+        here = self.ref.at[:, pl.ds(start, size), pl.ds(128 * j, 128)]
+        self.back[j][k].append(self.links.dp(here, here, self.cube[(j % 4 + k) % 4][1], like))
 
     def begin(self):
         self.launch(0)
 
     def advance(self):
         s = self.stage
-        if s > 9:
-            return
         mp, zl, core, part, far = mp_places()
         earlier, self.sent = self.sent, []
-        if s == 5:
+        if s > 5:
+            k = 9 - s
+            for j in range(STRIPS):
+                for cp in self.back[j][k]:
+                    cp.wait_recv()
+                self.back[j][k][0].wait_send()
+                self.sent.extend(self.back[j][k][1:])
+                if k >= 1:
+                    self.give_back(j, k - 1, True)
+                if k >= 2:
+                    self.give_back(j, k - 2, False)
+        elif s == 5:
             for cp in self.flying:
                 cp.wait()
             self.got[mp] = self.pack[mp]
             for j in range(STRIPS):
-                self.ref[:, pl.ds(self.cur[j % 4], 16), pl.ds(128 * j, 128)] = self.got[:, j]
+                self.ref[:, pl.ds(self.at[j % 4][4], 16), pl.ds(128 * j, 128)] = self.got[:, j]
             pl.semaphore_wait(self.free, 4)
-            self.launch(6)
+            for j in range(STRIPS):
+                self.give_back(j, 3, False)
+                self.give_back(j, 2, False)
         else:
             for j, cp in enumerate(self.flying):
                 cols = pl.ds(128 * j, 128)
@@ -281,12 +306,11 @@
                 else:
                     self.sent.append(cp)
                 cp.wait_recv()
-                if s <= 4:
-                    rows, at, here = 256 >> min(s + 1, 4), 256 - (256 >> s), self.cur[j % 4]
-                    add_into(
-                        self.ref, lambda r, m: (slice(None), pl.ds(here + r, m), cols),
-                        self.recv, lambda r, m: (slice(None), pl.ds(at + r, m), cols), rows,
-                    )
+                rows, room, here = 256 >> min(s + 1, 4), 256 - (256 >> s), self.at[j % 4][min(s + 1, 4)]
+                add_into(
+                    self.ref, lambda r, m: (slice(None), pl.ds(here + r, m), cols),
+                    self.recv, lambda r, m: (slice(None), pl.ds(room + r, m), cols), rows,
+                )
             if s == 3:
                 for cp in self.sent:
                     cp.wait_send()
@@ -295,9 +319,9 @@
                     pl.semaphore_signal(self.free, inc=1, device_id=(peer, mp), device_id_type=MESH)
             if s == 4:
                 for j in range(STRIPS):
-                    self.pack[:, j] = self.ref[:, pl.ds(self.cur[j % 4], 16), pl.ds(128 * j, 128)]
+                    self.pack[:, j] = self.ref[:, pl.ds(self.at[j % 4][4], 16), pl.ds(128 * j, 128)]
                 self.flying = [self.links.mp(self.pack.at[peer], self.got.at[mp], peer) for peer in (part, far, 3 - mp)]
-            elif s < 9:
+            else:
                 self.launch(s + 1)
         for cp in earlier:
             cp.wait_send()

time: 154 us -> 153 us (level)
  no operation moved by 1% of the time
where the time goes in v6:
time: 153 us; the launch traced here: 150 us
  Pallas kernels  148 us (97%)
  between operations  2.24 us (1%)
    pallas_call x1, Pallas kernels, layer(): pl.pallas_call(layer_body, out_shape=outs, in_specs=[ANY] * 10 + [SMEM] *...  139 us
    pallas_call x1, Pallas kernels, widen(): pl.pallas_call(widen_body, out_shape=outs, in_specs=[ANY] * 9, out_specs=...  8.3 us

profile of v6, /device:TPU:0, one launch (start us, length us, event | category | flops | bytes accessed | tf_op | source)
XLA Modules:
  0.0 150.0 jit_solution(16344233635206812138)
XLA Ops:
  1.9 139.4 %shard_map.255 = (bf16[128,1024]{1,0:T(8,128)(2,1)}, bf16[43,1024]{1,0:T(8,128)(2,1)}, f32[128,1024]{1,0:T(8,128)}, bf16[1024,1024]{1,0:T(8,128)(2,1)}, bf16[102...) custom-call(bf16[128,1024]{1,0:T(8,128)(2,1)} %bitcast.14, ...), custom_call_target="tpu_custom_call" | custom-call | tf_op jit(solution)/shard_map/pallas_call | solution.py:991
  141.4 8.3 %shard_map.256 = (bf16[128,1024]{1,0:T(8,128)(2,1)}, bf16[43,1024]{1,0:T(8,128)(2,1)}, f32[128,1024]{1,0:T(8,128)}, f32[1,1024]{1,0:T(1,128)}, f32[256,1024]{1,0...) custom-call(bf16[128,1024]{1,0:T(8,128)(2,1)} %get-tuple-element.35., ...), custom_call_target="tpu_custom_call" | custom-call | tf_op jit(solution)/shard_map/pallas_call | solution.py:1061

commit v7 on v6

--- a/solution.py
+++ b/solution.py
@@ -633,7 +633,7 @@
     @task("r1", "squeeze")
     def _():
         pick = (iota((48, CP), 1) == iota((48, CP), 0) + mp * 43).astype(BF)
-        sqz_rows[...] = dg(pick, sqz[...].astype(BF))[0:43].astype(BF)
+        sqz_rows[...] = dg(pick, sqz[...].astype(BF)).astype(BF)
         leaving.append(load(sqz_rows, sqz_out))
         unit, _ = normalize(sqz[...])
         skv[...] = dg((unit * again[...]).astype(BF), wkvq[:, 0:512]).astype(BF)
@@ -968,7 +968,7 @@
         return jax.ShapeDtypeStruct(shape, dtype)
 
     outs = (
-        out_shape((128, D), BF), out_shape((43, D), BF), out_shape((128, D), F32), out_shape((1024, D), BF),
+        out_shape((128, D), BF), out_shape((48, D), BF), out_shape((128, D), F32), out_shape((1024, D), BF),
         out_shape((1024, D), BF), out_shape((768, D), BF), out_shape((256, D), BF), out_shape((4, 256, 768), BF),
         out_shape((16, D), F32),
     )
@@ -984,7 +984,7 @@
         v((2, 96, D), BF), v((2, 96, D), BF), v((2, 96, D), BF),
         v((4, 256, 768), BF), v((4, STRIPS, 16, 128), BF), v((4, STRIPS, 16, 128), BF), v((7, 16, D), F32),
         v((D, D), BF), v((D, D), BF), v((768, D), BF), v((256, D), BF), v((4, 256, 768), BF), v((16, D), F32),
-        v((128, D), BF), v((128, D), F32), v((43, D), BF), v((1, D), F32), v((1, D), F32), v((1, D), F32),
+        v((128, D), BF), v((128, D), F32), v((48, D), BF), v((1, D), F32), v((1, D), F32), v((1, D), F32),
         pltpu.SemaphoreType.DMA((23,)), pltpu.SemaphoreType.REGULAR((6,)),
         pltpu.SemaphoreType.DMA((SENDS,)), pltpu.SemaphoreType.DMA((RECVS,)),
     ]
@@ -1016,7 +1016,8 @@
         for i in range(n):
             k = len(pieces)
             pieces.append((load(src.at[pl.ds(256 * i, 256)], lin.at[k]), dst.at[pl.ds(256 * i, 256)]))
-    plain = [(load(lout, b_lout), b_lout, o_lout), (load(gin, b_gin), b_gin, o_gin), (load(sqz, b_sqz), b_sqz, o_sqz)]
+    plain = [(load(lout, b_lout), b_lout, o_lout), (load(gin, b_gin), b_gin, o_gin)]
+    sqz_load = load(sqz, b_sqz)
     stores = []
 
     def leave(src, dst):
@@ -1040,6 +1041,8 @@
         cp.wait()
         wide[i] = lin[i].astype(F32)
         leave(wide.at[i], dst)
+    sqz_load.wait()
+    o_sqz[...] = b_sqz[0:43, :]
     for cp, src, dst in plain:
         cp.wait()
         leave(src, dst)
@@ -1062,12 +1065,12 @@
         widen_body,
         out_shape=outs,
         in_specs=[ANY] * 9,
-        out_specs=(ANY,) * 13,
+        out_specs=tuple(VMEM if i == 1 else ANY for i in range(13)),
         scratch_shapes=[
             v((4, 256, 768), BF), v((12, 256, D), BF), v((256, 2 * D), F32), v((256, D), F32), v((12, 256, D), F32),
-            v((128, D), BF), v((128, D), F32), v((16, D), F32), v((43, D), BF),
+            v((128, D), BF), v((128, D), F32), v((16, D), F32), v((48, D), BF),
             v((1, D), F32), v((1, D), F32), v((1, D), F32), v((1, 8), F32),
-            pltpu.SemaphoreType.DMA((17,)), pltpu.SemaphoreType.DMA((21,)),
+            pltpu.SemaphoreType.DMA((17,)), pltpu.SemaphoreType.DMA((20,)),
         ],
         compiler_params=pltpu.CompilerParams(vmem_limit_bytes=62 << 20),
     )(*args)

time: 153 us -> 153 us (level)
  no operation moved by 1% of the time
where the time goes in v7:
time: 153 us; the launch traced here: 151 us
  Pallas kernels  148 us (97%)
  between operations  2.24 us (1%)
    pallas_call x1, Pallas kernels, layer(): pl.pallas_call(layer_body, out_shape=outs, in_specs=[ANY] * 10 + [SMEM] *...  139 us
    pallas_call x1, Pallas kernels, widen(): pl.pallas_call(widen_body, out_shape=outs, in_specs=[ANY] * 9, out_specs=...  8.9 us

profile of v7, /device:TPU:0, one launch (start us, length us, event | category | flops | bytes accessed | tf_op | source)
XLA Modules:
  0.0 150.5 jit_solution(4581320893256388783)
XLA Ops:
  1.9 139.4 %shard_map.255 = (bf16[128,1024]{1,0:T(8,128)(2,1)}, bf16[48,1024]{1,0:T(8,128)(2,1)}, f32[128,1024]{1,0:T(8,128)}, bf16[1024,1024]{1,0:T(8,128)(2,1)}, bf16[102...) custom-call(bf16[128,1024]{1,0:T(8,128)(2,1)} %bitcast.14, ...), custom_call_target="tpu_custom_call" | custom-call | tf_op jit(solution)/shard_map/pallas_call | solution.py:991
  141.4 8.9 %shard_map.256 = (bf16[128,1024]{1,0:T(8,128)(2,1)}, bf16[43,1024]{1,0:T(8,128)(2,1)}, f32[128,1024]{1,0:T(8,128)}, f32[1,1024]{1,0:T(1,128)}, f32[256,1024]{1,0...) custom-call(bf16[128,1024]{1,0:T(8,128)(2,1)} %get-tuple-element.35., ...), custom_call_target="tpu_custom_call" | custom-call | tf_op jit(solution)/shard_map/pallas_call | solution.py:1064
